TPU v7x, 32 devices: a whole 2x2x4 slice. The times are simulated.
32 devices in a mesh: sky: 4 (over z), tm: 8 (over y, x, core).
Axes of the slice: x: 2, y: 2, z: 4, core: 2. Of those that a mesh axis runs over, the one named last changes fastest.
Arguments:
- tiles: float32 [512, 128, 256], P(('sky', 'tm')), may hold values from -0.375 to 0.375
- tile_seg: int32 [512], P(('sky', 'tm')), may hold values from 0 to 127, as said below
- tile_count: int32 [512], P(('sky', 'tm')), may hold values from 32 to 128
- src_index: int32 [512, 128], P(('sky', 'tm')), may hold values from 0 to 32767, as said below
- src_coef: float32 [5, 512, 128], P(None, ('sky', 'tm')), may hold values from -6 to 6
- obs_weight: float32 [512, 128], P(('sky', 'tm')), may hold values from 0.2 to 5
- att_dir: float32 [128, 256], P('tm'), may hold values from -6 to 6
- src_dir: float32 [5, 131072], P(None, ('sky', 'tm')), may hold values from -6 to 6
Outputs:
- projected: float32 [512, 128], P(('sky', 'tm'))
- att_normal: float32 [128, 256], P('tm')
- src_normal: float32 [5, 131072], P(None, ('sky', 'tm'))
- curvature: float32 [], replicated
Inputs may be any that keep to these rules, and one draw needn't show every extreme that they name: `tile_seg`: within each aligned block of 16 tiles, at most 4 tiles name segments s with s // 16 equal to any one value; every block reaches 4 for some value. `src_index`: within each aligned block of 16 tiles, at most 512 observations name sources i with i // 4096 equal to any one value; every block reaches 512 for some value.
All inputs are finite; a program needn't handle non-finite values.
Results may differ from a plain program's by a relative error of at most 0.00011.
Values sent between devices are 32-bit elements; how exact they have to be, the bound alone decides.
No kernel may reach another device: no remote copies, remote signals or barrier semaphores. Data moves between devices by JAX's collectives and lax.ppermute only.
A program may use at most 192 MiB of HBM per device.

v0:
```python
import jax
import jax.numpy as jnp
from jax import lax
from jax.sharding import PartitionSpec as P


def per_device(tiles, tile_seg, tile_count, src_index, src_coef, obs_weight, att_dir, src_dir):
    row_count = tiles.shape[1]
    params = src_coef.shape[0]
    row_ids = jnp.arange(row_count, dtype=jnp.int32)
    live_rows = row_ids[None, :] < tile_count[:, None]
    att_whole = lax.all_gather(att_dir, "tm", axis=0, tiled=True)
    src_region = lax.all_gather(src_dir, "tm", axis=1, tiled=True)
    seg_total = att_whole.shape[0]
    region_size = src_region.shape[1]
    seg_rows = att_whole[tile_seg]
    att_part = jnp.einsum("tjc,tc->tj", tiles, seg_rows, precision=lax.Precision.HIGHEST)
    picked = src_region[:, src_index]
    projected = jnp.where(
        live_rows, att_part + jnp.sum(src_coef * picked, axis=0), jnp.zeros_like(att_part)
    )
    weighted = obs_weight * projected
    curvature = lax.psum(jnp.sum(projected * weighted), ("sky", "tm"))
    tile_grad = jnp.einsum("tjc,tj->tc", tiles, weighted, precision=lax.Precision.HIGHEST)
    terms = (src_coef * weighted[None]).reshape(params, -1)
    src_terms = jax.ops.segment_sum(terms.T, src_index.reshape(-1), num_segments=region_size).T
    src_normal = lax.psum_scatter(src_terms, "tm", scatter_dimension=1, tiled=True)
    onehot = (tile_seg[:, None] == jnp.arange(seg_total, dtype=jnp.int32)[None, :]).astype(
        jnp.float32
    )
    seg_part = jnp.dot(
        onehot.T, tile_grad, precision=lax.Precision.HIGHEST, preferred_element_type=jnp.float32
    )
    owned = lax.psum_scatter(seg_part, "tm", scatter_dimension=0, tiled=True)
    att_normal = lax.psum(owned, "sky")
    return (projected, att_normal, src_normal, curvature)


def solution(mesh):
    placed = (
        P(("sky", "tm"), None, None),
        P(("sky", "tm")),
        P(("sky", "tm")),
        P(("sky", "tm"), None),
        P(None, ("sky", "tm"), None),
        P(("sky", "tm"), None),
        P("tm", None),
        P(None, ("sky", "tm")),
    )
    return jax.shard_map(
        per_device,
        mesh=mesh,
        in_specs=placed,
        out_specs=(P(("sky", "tm"), None), P("tm", None), P(None, ("sky", "tm")), P()),
        check_vma=False,
    )
```

profile of v0, /device:TPU:0, one launch (start us, length us, event | category | flops | bytes accessed | tf_op | source)
XLA Modules:
  0.0 282.6 jit_solution(17800097066806534412)
XLA Ops:
  7.2 0.0 copy-start
  7.2 0.0 reduce-scatter.3.cloned.1.call-start
  7.2 3.0 %copy.12 = f32[5,4096]{0,1:T(8,128)} copy(f32[5,4096]{1,0:T(8,128)} %param.15) | data formatting | bytes 163840 | tf_op args[7]
  10.3 0.0 copy-start.3
  10.3 0.0 copy-start.2
  10.3 0.0 copy-start.6
  10.3 0.0 copy-start.1
  10.3 83.0 %all_gather.7 = f32[5,32768]{0,1:T(8,128)} all-gather(f32[5,4096]{0,1:T(8,128)} %copy.12), channel_id=1, replica_groups=mesh['sky'=4,'tm'=8] {'tm'}, dimensions={1}, use_global_device_ids=true | all-gather | bytes 737280 | tf_op jit(solution)/shard_map/all_gather | solution.py:13
  93.3 0.0 copy-done.3
  93.3 0.0 copy-start.4
  93.3 0.0 copy-start.5
  93.3 11.2 %gather_fusion.1 = f32[2048,5]{1,0:T(8,128)S(1)} fusion(f32[5,32768]{0,1:T(8,128)} %all_gather.7, s32[2048]{0:T(1024)S(1)} %fusion.9), kind=kCustom, calls=%fused_computation.1 | custom fusion | bytes 90112 | tf_op jit(solution)/shard_map/gather | solution.py:18
  104.6 0.3 copy.13
  104.9 0.0 copy-done.2
  104.9 8.3 %all_gather.6 = f32[128,256]{1,0:T(8,128)S(1)} all-gather(f32[16,256]{1,0:T(8,128)S(1)} %copy-done.2), channel_id=1, replica_groups=mesh['sky'=4,'tm'=8] {'tm'}, dimensions={0}, use_global_device_ids=true | all-gather | bytes 147456 | tf_op jit(solution)/shard_map/all_gather | solution.py:12
  113.2 0.0 copy-done.6
  113.2 0.0 copy-done.1
  113.2 0.6 gather_fusion
  113.8 0.0 copy-done
  113.8 1.8 fusion.6
  115.6 0.0 copy-done.4
  115.6 0.0 copy-done.5
  115.6 1.3 multiply_reduce_fusion
  116.9 1.1 fusion.11
  118.0 1.0 fusion.3
  119.0 0.0 reduce-scatter.3.cloned.1.call-update
  119.0 0.0 reduce-scatter.5.cloned.1.call-start
  119.1 0.4 copy.20
  119.5 18.2 %scatter_custom_fusion = f32[32768,5]{1,0:T(8,128)} fusion(s32[2048]{0:T(1024)S(1)} %bitcast.32, f32[2048,5]{1,0:T(8,128)S(1)} %bitcast.28, f32[]{:T(128)} %constant.0.clone.1), kind=kCustom, calls=%fused_computation.3 | custom fusion | flops 10240 | bytes 655364 | tf_op jit(solution)/shard_map/scatter-add | solution.py:26
  137.7 0.0 reduce-scatter.5.cloned.1.call-update
  137.7 39.8 %psum.15 = f32[]{:T(128)} all-reduce(f32[]{:T(128)} %get-tuple-element.8), channel_id=1, replica_groups=mesh['sky'=4,'tm'=8] {'sky','tm'}, use_global_device_ids=true, to_apply=%region_6.7 | all-reduce | flops 1 | bytes 8 | tf_op jit(solution)/shard_map/psum | solution.py:23
  177.5 0.0 reduce-scatter.3.cloned.1.call-done
  177.5 18.8 %psum.14 = f32[16,256]{1,0:T(8,128)} all-reduce(f32[16,256]{1,0:T(8,128)} %reduce-scatter.3.cloned.1.call-done), channel_id=1, replica_groups=mesh['sky'=4,'tm'=8] {'sky'}, use_global_device_ids=true, to_apply=%region_2.3 | all-reduce | flops 4096 | bytes 32768 | tf_op jit(solution)/shard_map/psum | solution.py:35
  196.3 76.5 %reduce-scatter.5.cloned.1.call-done = f32[5,4096]{0,1:T(8,128)} async-done(((f32[5,32768]{0,1:T(8,128)}), f32[5,4096]{0,1:T(8,128)}) %reduce-scatter.5.cloned.1.call-update) | async-done | bytes 81936 | tf_op jit(solution)/shard_map/reduce_scatter | solution.py:27
  272.9 2.9 %copy.15 = f32[5,4096]{1,0:T(8,128)} copy(f32[5,4096]{0,1:T(8,128)} %reduce-scatter.5.cloned.1.call-done) | data formatting | bytes 163840
  (5 shorter events, 0.0 us)
Async XLA Ops:
  7.2 106.6 %copy-start = (f32[16,128,256]{2,1,0:T(8,128)S(1)}, f32[16,128,256]{2,1,0:T(8,128)}, u32[]{:S(2)}) copy-start(f32[16,128,256]{2,1,0:T(8,128)} %param.8) | copy-start | bytes 6291460
  7.2 170.3 %reduce-scatter.3.cloned.1.call-start = ((), (), s32[]{:S(2)}) async-start(), calls=%async_computation.2 | async-start | bytes 147456 | tf_op jit(solution)/shard_map/reduce_scatter | solution.py:34
  10.3 83.0 %copy-start.3 = (s32[16,128]{1,0:T(8,128)S(1)}, s32[16,128]{1,0:T(8,128)}, u32[]{:S(2)}) copy-start(s32[16,128]{1,0:T(8,128)} %param.11) | copy-start | bytes 24580
  10.3 94.6 %copy-start.2 = (f32[16,256]{1,0:T(8,128)S(1)}, f32[16,256]{1,0:T(8,128)}, u32[]{:S(2)}) copy-start(f32[16,256]{1,0:T(8,128)} %param.14) | copy-start | bytes 49156
  10.3 102.9 %copy-start.6 = (s32[16]{0:T(128)S(1)}, s32[16]{0:T(128)}, u32[]{:S(2)}) copy-start(s32[16]{0:T(128)} %param.9) | copy-start | bytes 196
  10.3 102.9 %copy-start.1 = (f32[5,16,128]{2,1,0:T(8,128)S(1)}, f32[5,16,128]{2,1,0:T(8,128)}, u32[]{:S(2)}) copy-start(f32[5,16,128]{2,1,0:T(8,128)} %param.12) | copy-start | bytes 122884
  93.3 22.3 %copy-start.4 = (f32[16,128]{1,0:T(8,128)S(1)}, f32[16,128]{1,0:T(8,128)}, u32[]{:S(2)}) copy-start(f32[16,128]{1,0:T(8,128)} %param.13) | copy-start | bytes 24580
  93.3 22.3 %copy-start.5 = (s32[16]{0:T(128)S(1)}, s32[16]{0:T(128)}, u32[]{:S(2)}) copy-start(s32[16]{0:T(128)} %param.10) | copy-start | bytes 196
  119.0 153.8 %reduce-scatter.5.cloned.1.call-start = ((), (), s32[]{:S(2)}) async-start(), calls=%async_computation.3 | async-start | bytes 18874368 | tf_op jit(solution)/shard_map/reduce_scatter | solution.py:27
Sparse Core Ops, SparseCore 0:
  119.2 33.6 reduce-scatter.2
  156.8 115.9 reduce-scatter.4
where the time goes:
time: 283 us
  blocking collectives  150 us (53%)
  waiting for transfers between devices  76.5 us (27%)
  other arithmetic  19.5 us (7%)
  local copies, waits for them, and re-layouts  18.4 us (7%)
  between operations  14.1 us (5%)
  matrix products  3.93 us (1%)
    all_gather x1, blocking collectives, per_device(): src_region = lax.all_gather(src_dir, 'tm', axis=1, tiled=True)  83 us
    reduce_scatter x1, waiting for transfers between devices, per_device(): lax.psum_scatter(src_terms, 'tm', scatter_dimension=1, tiled=True)  76.5 us
    psum x1, blocking collectives, per_device(): curvature = lax.psum(jnp.sum(projected * weighted), ('sky', 'tm'))  39.8 us
    psum x1, blocking collectives, per_device(): att_normal = lax.psum(owned, 'sky')  18.8 us
    scatter-add x1, other arithmetic, per_device(): jax.ops.segment_sum(terms.T, src_index.reshape(-1), num_segments=region_s...  18.2 us
    gather x2, local copies, waits for them, and re-layouts, per_device(): picked = src_region[:, src_index]  11.6 us
    all_gather x1, blocking collectives, per_device(): att_whole = lax.all_gather(att_dir, 'tm', axis=0, tiled=True)  8.27 us
    unnamed x16, local copies, waits for them, and re-layouts  5.93 us
  transfers between devices with their start and end apart: 2, of which 1 were waited for; matrix products, arithmetic and copies ran while one was open for 7% of the time, Pallas kernels for 0%

commit v1 on v0

v1 whole, which is shorter than its diff:
```python
import functools

import jax
import jax.numpy as jnp
from jax import lax
from jax.experimental import pallas as pl
from jax.experimental.pallas import tpu as pltpu
from jax.sharding import PartitionSpec as P

LANES = 128
SLOTS = 8
WIDE = 256
NT = (((1,), (1,)), ((), ()))
F32 = jnp.float32
BF16 = jnp.bfloat16
VMEM = pl.BlockSpec(memory_space=pltpu.VMEM)
SMEM = pl.BlockSpec(memory_space=pltpu.SMEM)
PARAMS = pltpu.CompilerParams(vmem_limit_bytes=16 * 1024 * 1024)


def halves(x):
    high = x.astype(BF16)
    return high, (x - high.astype(F32)).astype(BF16)


def rows_of(values, shape):
    ids = lax.broadcasted_iota(jnp.int32, shape, 0)
    out = jnp.zeros(shape, jnp.int32)
    for t, value in enumerate(values):
        out = jnp.where(ids == t, value, out)
    return out


def project_kernel(seg, count, table, tiles, index, coef, weight, projected, sent):
    params, tile_total, width = coef.shape
    cols = tiles.shape[2]
    owners, _, span = table.shape
    seg_rows = span // cols
    blocks = span // LANES
    ids = index[...]
    lane = lax.rem(ids, LANES)
    block = lax.div(ids, LANES)

    def take(owner, picked):
        picked = list(picked)
        for b in range(blocks):
            hit = block == owner * blocks + b
            for k in range(params):
                row = table[owner, k : k + 1, b * LANES : (b + 1) * LANES]
                found = jnp.take_along_axis(jnp.broadcast_to(row, ids.shape), lane, axis=1)
                picked[k] = jnp.where(hit, found, picked[k])
        return tuple(picked)

    picked = lax.fori_loop(0, owners, take, tuple(jnp.zeros(ids.shape, F32) for _ in range(params)))
    row_ids = lax.broadcasted_iota(jnp.int32, ids.shape, 0)
    total = jnp.zeros(ids.shape, F32)
    for t in range(tile_total):
        s = seg[t]
        start = pl.multiple_of(lax.rem(s, seg_rows) * cols, cols)
        direction = table[lax.div(s, seg_rows), params : params + 1, pl.ds(start, cols)]
        product = tiles[t] * direction
        folded = product[:, :LANES]
        for c in range(1, cols // LANES):
            folded = folded + product[:, c * LANES : (c + 1) * LANES]
        ones = jnp.where(row_ids == t, 1.0, 0.0).astype(BF16)
        for part in halves(folded):
            total = total + lax.dot_general(ones, part, NT, preferred_element_type=F32)
    for k in range(params):
        total = total + coef[k] * picked[k]
    live = lax.broadcasted_iota(jnp.int32, ids.shape, 1) < rows_of(
        [count[t] for t in range(tile_total)], ids.shape
    )
    value = jnp.where(live, total, 0.0)
    weighted = weight[...] * value
    projected[...] = value
    for k in range(params):
        sent[pl.ds(k, tile_total, stride=SLOTS), :] = coef[k] * weighted
    sent[pl.ds(params, tile_total, stride=SLOTS), :] = ids.astype(F32)
    names = rows_of([seg[t] for t in range(tile_total)], ids.shape)
    sent[pl.ds(params + 1, tile_total, stride=SLOTS), :] = names.astype(F32)
    sent[pl.ds(params + 2, tile_total, stride=SLOTS), :] = value * weighted
    columns = weighted.T
    base = tile_total * SLOTS
    for t in range(tile_total):
        grad = jnp.sum(tiles[t] * columns[:, t : t + 1], axis=0, keepdims=True)
        for c in range(cols // LANES):
            sent[pl.ds(base + c * tile_total + t, 1), :] = grad[:, c * LANES : (c + 1) * LANES]


def attitude_kernel(me, got, part, *, params, tile_total, seg_rows, folds):
    owners = got.shape[0]
    lane = lax.broadcasted_iota(jnp.int32, (tile_total, LANES), 1)
    first = me[0] * seg_rows
    base = tile_total * SLOTS
    group = LANES // tile_total
    sums = [jnp.zeros((seg_rows, LANES), F32) for _ in range(folds)]
    curve = jnp.zeros((tile_total, LANES), F32)
    for g in range(0, owners, group):
        members = range(g, min(g + group, owners))
        hits = []
        for d in members:
            name = got[d, pl.ds(params + 1, tile_total, stride=SLOTS), :].astype(jnp.int32)
            hits.append(jnp.where(name - first == lane, 1.0, 0.0))
            curve = curve + got[d, pl.ds(params + 2, tile_total, stride=SLOTS), :]
        pick = jnp.concatenate(hits, axis=0).T[:seg_rows].astype(BF16)
        for c in range(folds):
            grads = jnp.concatenate(
                [got[d, pl.ds(base + c * tile_total, tile_total), :] for d in members], axis=0
            )
            for piece in halves(grads):
                sums[c] = sums[c] + jnp.dot(pick, piece, preferred_element_type=F32)
    for c in range(folds):
        part[pl.ds(c * seg_rows, seg_rows), :] = sums[c]
    whole = jnp.sum(jnp.sum(curve, axis=0, keepdims=True), axis=1, keepdims=True)
    part[pl.ds(folds * seg_rows, 8), :] = jnp.broadcast_to(whole, (8, LANES))


def source_kernel(me, got, out, left, right, acc, *, params, tile_total):
    owners = got.shape[0]
    span = out.shape[1]
    high_total = span // WIDE
    depth = params * high_total
    high_ids = lax.broadcasted_iota(jnp.int32, (high_total, LANES), 0)
    low_ids = lax.broadcasted_iota(jnp.int32, (WIDE, LANES), 0)
    acc[...] = jnp.zeros_like(acc)

    def add(d, carry):
        for t in range(tile_total):
            at = slice(t * LANES, (t + 1) * LANES)
            tile = got[d, t * SLOTS : (t + 1) * SLOTS, :]
            local = tile[params : params + 1].astype(jnp.int32) - me[0] * span
            high = lax.shift_right_arithmetic(local, 8)
            low = lax.bitwise_and(local, WIDE - 1)
            right[:, at] = jnp.where(low_ids == low, 1.0, 0.0).astype(BF16)
            hit = high_ids == high
            for k in range(params):
                for p, piece in enumerate(halves(tile[k : k + 1])):
                    row = p * depth + k * high_total
                    left[row : row + high_total, at] = jnp.where(hit, piece.astype(F32), 0.0).astype(BF16)
        acc[...] += lax.dot_general(left[...], right[...], NT, preferred_element_type=F32)
        return carry

    lax.fori_loop(0, owners, add, 0)
    for k in range(params):
        for h in range(high_total):
            row = k * high_total + h
            out[k : k + 1, h * WIDE : (h + 1) * WIDE] = acc[row : row + 1, :] + acc[depth + row : depth + row + 1, :]


def finish_kernel(*refs, seg_rows, folds):
    *parts, normal, curvature = refs
    total = parts[0][...]
    for part in parts[1:]:
        total = total + part[...]
    for c in range(folds):
        normal[:, c * LANES : (c + 1) * LANES] = total[c * seg_rows : (c + 1) * seg_rows]
    curvature[0, 0] = total[folds * seg_rows, 0]


def per_device(tiles, tile_seg, tile_count, src_index, src_coef, obs_weight, att_dir, src_dir, *, sky):
    tile_total, row_count, cols = tiles.shape
    params, span = src_dir.shape
    seg_rows = att_dir.shape[0]
    folds = cols // LANES
    me = lax.axis_index("tm").astype(jnp.int32).reshape(1)
    directions = jnp.concatenate([src_dir, att_dir.reshape(-1, span)], axis=0)
    table = lax.all_gather(directions, "tm", axis=0, tiled=False)
    projected, sent = pl.pallas_call(
        project_kernel,
        out_shape=(
            jax.ShapeDtypeStruct((tile_total, row_count), F32),
            jax.ShapeDtypeStruct((tile_total * (SLOTS + folds), LANES), F32),
        ),
        in_specs=[SMEM, SMEM] + [VMEM] * 5,
        out_specs=(VMEM, VMEM),
        compiler_params=PARAMS,
        name="project",
    )(tile_seg, tile_count, table, tiles, src_index, src_coef, obs_weight)
    got = lax.all_gather(sent, "tm", axis=0, tiled=False)
    part = pl.pallas_call(
        functools.partial(
            attitude_kernel, params=params, tile_total=tile_total, seg_rows=seg_rows, folds=folds
        ),
        out_shape=jax.ShapeDtypeStruct((folds * seg_rows + 8, LANES), F32),
        in_specs=[SMEM, VMEM],
        out_specs=VMEM,
        compiler_params=PARAMS,
        name="attitude",
    )(me, got)
    others = [
        lax.ppermute(part, "sky", [(i, (i + k) % sky) for i in range(sky)]) for k in range(1, sky)
    ]
    depth = params * (span // WIDE)
    src_normal = pl.pallas_call(
        functools.partial(source_kernel, params=params, tile_total=tile_total),
        out_shape=jax.ShapeDtypeStruct((params, span), F32),
        in_specs=[SMEM, VMEM],
        out_specs=VMEM,
        scratch_shapes=[
            pltpu.VMEM((2 * depth, tile_total * LANES), BF16),
            pltpu.VMEM((WIDE, tile_total * LANES), BF16),
            pltpu.VMEM((2 * depth, WIDE), F32),
        ],
        compiler_params=PARAMS,
        cost_estimate=pl.CostEstimate(flops=2_000_000_000, bytes_accessed=1_000_000, transcendentals=0),
        name="source",
    )(me, got)
    att_normal, curvature = pl.pallas_call(
        functools.partial(finish_kernel, seg_rows=seg_rows, folds=folds),
        out_shape=(
            jax.ShapeDtypeStruct((seg_rows, cols), F32),
            jax.ShapeDtypeStruct((1, 1), F32),
        ),
        in_specs=[VMEM] * sky,
        out_specs=(VMEM, SMEM),
        compiler_params=PARAMS,
        name="finish",
    )(part, *others)
    return projected, att_normal, src_normal, curvature.reshape(())


def solution(mesh):
    placed = (
        P(("sky", "tm"), None, None),
        P(("sky", "tm")),
        P(("sky", "tm")),
        P(("sky", "tm"), None),
        P(None, ("sky", "tm"), None),
        P(("sky", "tm"), None),
        P("tm", None),
        P(None, ("sky", "tm")),
    )
    return jax.shard_map(
        functools.partial(per_device, sky=mesh.shape["sky"]),
        mesh=mesh,
        in_specs=placed,
        out_specs=(P(("sky", "tm"), None), P("tm", None), P(None, ("sky", "tm")), P()),
        check_vma=False,
    )
```

time: 283 us -> 48.5 us (0.17)
  blocking collectives: 150 us -> 22.5 us
  waiting for transfers between devices: 76.5 us -> 0.01 us
  other arithmetic: 19.5 us -> 0.94 us
  between operations: 14.1 us -> 0.66 us
  Pallas kernels: 0 us -> 12.6 us
  local copies, waits for them, and re-layouts: 18.4 us -> 5.81 us
  starting transfers between devices: 0.08 us -> 5.52 us
  matrix products: 3.93 us -> 0 us
    reduce_scatter x2 -> x0, waiting for transfers between devices: 76.5 us -> none  [the longest x1 76.5 us: per_device(): lax.psum_scatter(src_terms, 'tm', scatter_dimension=1, tiled=True)]
    all_gather x2, blocking collectives: 91.3 us -> 22.5 us  [the longest x1 12.4 us: per_device(): table = lax.all_gather(directions, 'tm', axis=0, tiled=False)]
    psum x2 -> x0, blocking collectives: 58.6 us -> none  [the longest x1 39.8 us: per_device(): curvature = lax.psum(jnp.sum(projected * weighted), ('sky', 'tm'))]
    scatter-add x1 -> x0, other arithmetic: 18.2 us -> none  [per_device(): jax.ops.segment_sum(terms.T, src_index.reshape(-1), num_segments=region_s...]
    pallas_call x0 -> x4, Pallas kernels: none -> 12.6 us  [the longest x1 6.58 us: per_device(): pl.pallas_call(functools.partial(source_kernel, params=params, tile_total...]
    gather x3 -> x0, local copies, waits for them, and re-layouts: 12.2 us -> none  [the longest x2 11.6 us: per_device(): picked = src_region[:, src_index]]
    ppermute x0 -> x3, starting transfers between devices: none -> 5.52 us  [per_device(): lax.ppermute(part, 'sky', [(i, (i + k) % sky) for i in range(sky)])]
    dot_general x3 -> x0, matrix products: 3.93 us -> none  [the longest x1 1.83 us: per_device(): jnp.einsum('tjc,tc->tj', tiles, seg_rows, precision=lax.Precision.HIGHEST)]
  transfers between devices with their start and end apart: 2 -> 3, of which waited for: 1 -> 0; matrix products, arithmetic and copies ran while one was open for 7% -> 0% of each run, Pallas kernels for 0% -> 14%
where the time goes in v1:
time: 48.5 us; the launch traced here: 48.1 us
  blocking collectives  22.5 us (46%)
  Pallas kernels  12.6 us (26%)
  local copies, waits for them, and re-layouts  5.81 us (12%)
  starting transfers between devices  5.52 us (11%)
  other arithmetic  0.94 us (2%)
  between operations  0.66 us (1%)
    all_gather x1, blocking collectives, per_device(): table = lax.all_gather(directions, 'tm', axis=0, tiled=False)  12.4 us
    all_gather x1, blocking collectives, per_device(): got = lax.all_gather(sent, 'tm', axis=0, tiled=False)  10.1 us
    pallas_call x1, Pallas kernels, per_device(): pl.pallas_call(functools.partial(source_kernel, params=params, tile_total...  6.58 us
    unnamed x13, local copies, waits for them, and re-layouts  5.81 us
    ppermute x3, starting transfers between devices, per_device(): lax.ppermute(part, 'sky', [(i, (i + k) % sky) for i in range(sky)])  5.52 us
    pallas_call x1, Pallas kernels, per_device(): pl.pallas_call(project_kernel, out_shape=(jax.ShapeDtypeStruct((tile_tota...  5.19 us
  transfers between devices with their start and end apart: 3, of which 0 were waited for; matrix products, arithmetic and copies ran while one was open for 0% of the time, Pallas kernels for 14%

profile of v1, /device:TPU:0, one launch (start us, length us, event | category | flops | bytes accessed | tf_op | source)
XLA Modules:
  0.0 48.1 jit_solution(6932972065531733528)
XLA Ops:
  0.6 0.7 %copy.12 = f32[1,1,16,256]{3,1,2,0:T(1,128)S(1)} copy(f32[1,1,16,256]{3,2,1,0:T(8,128)} %bitcast.11) | data formatting | bytes 32768
  1.4 0.9 %maximum_bitcast_fusion = f32[1,6,4096]{2,1,0:T(8,128)S(1)} fusion(f32[1,4096]{1,0:T(1,128)S(1)} %bitcast.10, f32[5,4096]{1,0:T(8,128)} %param.15), kind=kLoop, calls=%fused_computation | loop fusion | flops 24576 | bytes 196608
  2.3 12.4 %all-gather.2.table = f32[8,6,4096]{2,1,0:T(8,128)S(1)} all-gather(f32[1,6,4096]{2,1,0:T(8,128)S(1)} %maximum_bitcast_fusion), channel_id=2, replica_groups=mesh['sky'=4,'tm'=8] {'tm'}, dimensions={0}, use_global_device_ids=true | all-gather | bytes 884736 | tf_op jit(solution)/shard_map/all_gather | solution.py:167
  14.7 0.0 copy-start
  14.7 1.6 %copy-done = f32[16,128,256]{2,1,0:T(8,128)S(1)} copy-done((f32[16,128,256]{2,1,0:T(8,128)S(1)}, f32[16,128,256]{2,1,0:T(8,128)}, u32[]{:S(2)}) %copy-start) | copy-done | bytes 2097176
  16.3 0.0 copy-start.1
  16.3 0.8 %copy-done.1 = f32[5,16,128]{2,1,0:T(8,128)S(1)} copy-done((f32[5,16,128]{2,1,0:T(8,128)S(1)}, f32[5,16,128]{2,1,0:T(8,128)}, u32[]{:S(2)}) %copy-start.1) | copy-done | bytes 40984
  17.1 0.0 copy-start.2
  17.1 0.7 %copy-done.2 = s32[16,128]{1,0:T(8,128)S(1)} copy-done((s32[16,128]{1,0:T(8,128)S(1)}, s32[16,128]{1,0:T(8,128)}, u32[]{:S(2)}) %copy-start.2) | copy-done | bytes 8216
  17.8 0.0 copy-start.3
  17.8 0.7 %copy-done.3 = f32[16,128]{1,0:T(8,128)S(1)} copy-done((f32[16,128]{1,0:T(8,128)S(1)}, f32[16,128]{1,0:T(8,128)}, u32[]{:S(2)}) %copy-start.3) | copy-done | bytes 8216
  18.5 0.0 copy-start.4
  18.5 0.7 %copy-done.4 = s32[16]{0:T(128)S(1)} copy-done((s32[16]{0:T(128)S(1)}, s32[16]{0:T(128)}, u32[]{:S(2)}) %copy-start.4) | copy-done | bytes 88
  19.1 0.0 copy-start.5
  19.1 0.7 %copy-done.5 = s32[16]{0:T(128)S(1)} copy-done((s32[16]{0:T(128)S(1)}, s32[16]{0:T(128)}, u32[]{:S(2)}) %copy-start.5) | copy-done | bytes 88
  19.8 5.2 %project.1 = (f32[16,128]{1,0:T(8,128)}, f32[160,128]{1,0:T(8,128)S(1)}) custom-call(s32[16]{0:T(128)S(1)} %copy-done.4, s32[16]{0:T(128)S(1)} %copy-done.5, f32[8,6,4096]{2,1,0:T(8,128)S(1)} %all-gather.2.table, f32[16,128,256]{2,1,0:T(8,128)S(1)} %copy-done, s32[16,128]{1,0:T(8,128)S(1)} %copy-done.2, f32[5,16,128]{2,1,0:T(8,128)S(1)} %copy-done.1, ...), custom_call_target="tpu_custom_call" | custom-call | tf_op jit(solution)/shard_map/project/pallas_call | solution.py:168
  25.0 10.1 %all-gather.1 = f32[1280,128]{1,0:T(8,128)S(1)} all-gather(f32[160,128]{1,0:T(8,128)S(1)} %get-tuple-element.9), channel_id=3, replica_groups=mesh['sky'=4,'tm'=8] {'tm'}, dimensions={0}, use_global_device_ids=true | all-gather | bytes 737280 | tf_op jit(solution)/shard_map/all_gather | solution.py:179
  35.1 0.2 attitude.1.refs_0_
  35.3 1.6 %collective-permute-start = (f32[40,128]{1,0:T(8,128)S(1)}, f32[40,128]{1,0:T(8,128)S(1)}, u32[]{:S(2)}, u32[]{:S(2)}) collective-permute-start(f32[40,128]{1,0:T(8,128)S(1)} %attitude.1.refs_0_), channel_id=1, source_target_pairs={{0,8},{8,16},{16,24},{24,0},{1,9},{9,17},{17,25},{25,1},{2,10},{10... | collective-permute-start | bytes 61448 | tf_op jit(solution)/shard_map/ppermute | solution.py:191
  36.9 2.6 %collective-permute-start.1 = (f32[40,128]{1,0:T(8,128)S(1)}, f32[40,128]{1,0:T(8,128)S(1)}, u32[]{:S(2)}, u32[]{:S(2)}) collective-permute-start(f32[40,128]{1,0:T(8,128)S(1)} %attitude.1.refs_0_), channel_id=1, source_target_pairs={{0,16},{8,24},{16,0},{24,8},{1,17},{9,25},{17,1},{25,9},{2,18},{10... | collective-permute-start | bytes 61448 | tf_op jit(solution)/shard_map/ppermute | solution.py:191
  39.5 1.3 %collective-permute-start.2 = (f32[40,128]{1,0:T(8,128)S(1)}, f32[40,128]{1,0:T(8,128)S(1)}, u32[]{:S(2)}, u32[]{:S(2)}) collective-permute-start(f32[40,128]{1,0:T(8,128)S(1)} %attitude.1.refs_0_), channel_id=1, source_target_pairs={{0,24},{8,0},{16,8},{24,16},{1,25},{9,1},{17,9},{25,17},{2,26},{10... | collective-permute-start | bytes 61448 | tf_op jit(solution)/shard_map/ppermute | solution.py:191
  40.8 6.6 %source.1 = f32[5,4096]{1,0:T(8,128)} custom-call(s32[1]{0:T(128)} %bitcast.1.me, f32[8,160,128]{2,1,0:T(8,128)S(1)} %bitcast.9), custom_call_target="tpu_custom_call" | custom-call | flops 2000000000 | bytes 1000000 | tf_op jit(solution)/shard_map/source/pallas_call | solution.py:194
  47.4 0.0 collective-permute-done.refs_1_
  47.4 0.0 collective-permute-done.1.refs_2_
  47.4 0.0 collective-permute-done.2.refs_3_
  47.4 0.6 %finish.1 = (f32[16,256]{1,0:T(8,128)}, f32[1,1]{1,0:T(1,128)}) custom-call(f32[40,128]{1,0:T(8,128)S(1)} %attitude.1.refs_0_, f32[40,128]{1,0:T(8,128)S(1)} %collective-permute-done.refs_1_, f32[40,128]{1,0:T(8,128)S(1)} %collective-permute-done.1.refs_2_, f32[40,128]{1,0:T(8,128)S(1)} %collective-permute-done.2.refs_3_), custom_call_target="tpu_custom_call" | custom-call | tf_op jit(solution)/shard_map/finish/pallas_call | solution.py:208
Async XLA Ops:
  14.7 1.6 %copy-start = (f32[16,128,256]{2,1,0:T(8,128)S(1)}, f32[16,128,256]{2,1,0:T(8,128)}, u32[]{:S(2)}) copy-start(f32[16,128,256]{2,1,0:T(8,128)} %tiles.1) | copy-start | bytes 6291460
  16.3 0.8 %copy-start.1 = (f32[5,16,128]{2,1,0:T(8,128)S(1)}, f32[5,16,128]{2,1,0:T(8,128)}, u32[]{:S(2)}) copy-start(f32[5,16,128]{2,1,0:T(8,128)} %coef.1) | copy-start | bytes 122884
  17.1 0.7 %copy-start.2 = (s32[16,128]{1,0:T(8,128)S(1)}, s32[16,128]{1,0:T(8,128)}, u32[]{:S(2)}) copy-start(s32[16,128]{1,0:T(8,128)} %index.1) | copy-start | bytes 24580
  17.8 0.7 %copy-start.3 = (f32[16,128]{1,0:T(8,128)S(1)}, f32[16,128]{1,0:T(8,128)}, u32[]{:S(2)}) copy-start(f32[16,128]{1,0:T(8,128)} %weight.1) | copy-start | bytes 24580
  18.5 0.7 %copy-start.4 = (s32[16]{0:T(128)S(1)}, s32[16]{0:T(128)}, u32[]{:S(2)}) copy-start(s32[16]{0:T(128)} %seg.1) | copy-start | bytes 196
  19.1 0.7 %copy-start.5 = (s32[16]{0:T(128)S(1)}, s32[16]{0:T(128)}, u32[]{:S(2)}) copy-start(s32[16]{0:T(128)} %count.1) | copy-start | bytes 196
  35.3 12.1 %collective-permute-start = (f32[40,128]{1,0:T(8,128)S(1)}, f32[40,128]{1,0:T(8,128)S(1)}, u32[]{:S(2)}, u32[]{:S(2)}) collective-permute-start(f32[40,128]{1,0:T(8,128)S(1)} %attitude.1.refs_0_), channel_id=1, source_target_pairs={{0,8},{8,16},{16,24},{24,0},{1,9},{9,17},{17,25},{25,1},{2,10},{10... | collective-permute-start | bytes 61448 | tf_op jit(solution)/shard_map/ppermute | solution.py:191
  36.9 10.5 %collective-permute-start.1 = (f32[40,128]{1,0:T(8,128)S(1)}, f32[40,128]{1,0:T(8,128)S(1)}, u32[]{:S(2)}, u32[]{:S(2)}) collective-permute-start(f32[40,128]{1,0:T(8,128)S(1)} %attitude.1.refs_0_), channel_id=1, source_target_pairs={{0,16},{8,24},{16,0},{24,8},{1,17},{9,25},{17,1},{25,9},{2,18},{10... | collective-permute-start | bytes 61448 | tf_op jit(solution)/shard_map/ppermute | solution.py:191
  39.5 7.9 %collective-permute-start.2 = (f32[40,128]{1,0:T(8,128)S(1)}, f32[40,128]{1,0:T(8,128)S(1)}, u32[]{:S(2)}, u32[]{:S(2)}) collective-permute-start(f32[40,128]{1,0:T(8,128)S(1)} %attitude.1.refs_0_), channel_id=1, source_target_pairs={{0,24},{8,0},{16,8},{24,16},{1,25},{9,1},{17,9},{25,17},{2,26},{10... | collective-permute-start | bytes 61448 | tf_op jit(solution)/shard_map/ppermute | solution.py:191

commit v2 on v1

--- a/solution.py
+++ b/solution.py
@@ -14,8 +14,13 @@
 F32 = jnp.float32
 BF16 = jnp.bfloat16
 VMEM = pl.BlockSpec(memory_space=pltpu.VMEM)
+HBM = pl.BlockSpec(memory_space=pltpu.HBM)
 SMEM = pl.BlockSpec(memory_space=pltpu.SMEM)
 PARAMS = pltpu.CompilerParams(vmem_limit_bytes=16 * 1024 * 1024)
+
+
+def in_hbm(x):
+    return pltpu.with_memory_space_constraint(x, pltpu.HBM)
 
 
 def halves(x):
@@ -31,12 +36,47 @@
     return out
 
 
-def project_kernel(seg, count, table, tiles, index, coef, weight, projected, sent):
+def pack_kernel(source, attitude, index, coef, weight, directions, index_out, coef_out, weight_out, held, sems):
+    params, span = source.shape
+    seg_rows, cols = attitude.shape
+    copies = [
+        pltpu.make_async_copy(source, held, sems.at[0]),
+        pltpu.make_async_copy(index, index_out, sems.at[2]),
+        pltpu.make_async_copy(coef, coef_out, sems.at[3]),
+        pltpu.make_async_copy(weight, weight_out, sems.at[4]),
+    ]
+    base = params * (span // LANES)
+    for c in range(cols // LANES):
+        copies.append(
+            pltpu.make_async_copy(
+                attitude.at[:, pl.ds(c * LANES, LANES)],
+                directions.at[pl.ds(base + c * seg_rows, seg_rows), :],
+                sems.at[5 + c],
+            )
+        )
+    for copy in copies:
+        copy.start()
+    copies[0].wait()
+    for b in range(span // LANES):
+        directions[b * params : (b + 1) * params, :] = held[:, b * LANES : (b + 1) * LANES]
+    for copy in copies[1:]:
+        copy.wait()
+
+
+def project_kernel(seg_in, count_in, tiles_in, table, index, coef, weight, projected, sent, seg, count, tiles, sems, *, seg_rows):
     params, tile_total, width = coef.shape
     cols = tiles.shape[2]
-    owners, _, span = table.shape
-    seg_rows = span // cols
-    blocks = span // LANES
+    folds = cols // LANES
+    owners = table.shape[0]
+    base = table.shape[1] - folds * seg_rows
+    blocks = base // params
+    copies = [
+        pltpu.make_async_copy(seg_in, seg, sems.at[0]),
+        pltpu.make_async_copy(count_in, count, sems.at[1]),
+        pltpu.make_async_copy(tiles_in, tiles, sems.at[2]),
+    ]
+    for copy in copies:
+        copy.start()
     ids = index[...]
     lane = lax.rem(ids, LANES)
     block = lax.div(ids, LANES)
@@ -46,22 +86,24 @@
         for b in range(blocks):
             hit = block == owner * blocks + b
             for k in range(params):
-                row = table[owner, k : k + 1, b * LANES : (b + 1) * LANES]
+                row = table[owner, pl.ds(b * params + k, 1), :]
                 found = jnp.take_along_axis(jnp.broadcast_to(row, ids.shape), lane, axis=1)
                 picked[k] = jnp.where(hit, found, picked[k])
         return tuple(picked)
 
     picked = lax.fori_loop(0, owners, take, tuple(jnp.zeros(ids.shape, F32) for _ in range(params)))
+    for copy in copies:
+        copy.wait()
     row_ids = lax.broadcasted_iota(jnp.int32, ids.shape, 0)
     total = jnp.zeros(ids.shape, F32)
     for t in range(tile_total):
         s = seg[t]
-        start = pl.multiple_of(lax.rem(s, seg_rows) * cols, cols)
-        direction = table[lax.div(s, seg_rows), params : params + 1, pl.ds(start, cols)]
-        product = tiles[t] * direction
-        folded = product[:, :LANES]
-        for c in range(1, cols // LANES):
-            folded = folded + product[:, c * LANES : (c + 1) * LANES]
+        owner, local = lax.div(s, seg_rows), lax.rem(s, seg_rows)
+        folded = None
+        for c in range(folds):
+            direction = table[owner, pl.ds(base + c * seg_rows + local, 1), :]
+            product = tiles[t, :, c * LANES : (c + 1) * LANES] * direction
+            folded = product if folded is None else folded + product
         ones = jnp.where(row_ids == t, 1.0, 0.0).astype(BF16)
         for part in halves(folded):
             total = total + lax.dot_general(ones, part, NT, preferred_element_type=F32)
@@ -83,7 +125,7 @@
     base = tile_total * SLOTS
     for t in range(tile_total):
         grad = jnp.sum(tiles[t] * columns[:, t : t + 1], axis=0, keepdims=True)
-        for c in range(cols // LANES):
+        for c in range(folds):
             sent[pl.ds(base + c * tile_total + t, 1), :] = grad[:, c * LANES : (c + 1) * LANES]
 
 
@@ -163,19 +205,38 @@
     seg_rows = att_dir.shape[0]
     folds = cols // LANES
     me = lax.axis_index("tm").astype(jnp.int32).reshape(1)
-    directions = jnp.concatenate([src_dir, att_dir.reshape(-1, span)], axis=0)
+    directions, index, coef, weight = pl.pallas_call(
+        pack_kernel,
+        out_shape=(
+            jax.ShapeDtypeStruct((params * (span // LANES) + folds * seg_rows, LANES), F32),
+            jax.ShapeDtypeStruct(src_index.shape, src_index.dtype),
+            jax.ShapeDtypeStruct(src_coef.shape, F32),
+            jax.ShapeDtypeStruct(obs_weight.shape, F32),
+        ),
+        in_specs=[HBM] * 5,
+        out_specs=(VMEM,) * 4,
+        scratch_shapes=[pltpu.VMEM((params, span), F32), pltpu.SemaphoreType.DMA((5 + folds,))],
+        compiler_params=PARAMS,
+        name="pack",
+    )(*map(in_hbm, (src_dir, att_dir, src_index, src_coef, obs_weight)))
     table = lax.all_gather(directions, "tm", axis=0, tiled=False)
     projected, sent = pl.pallas_call(
-        project_kernel,
+        functools.partial(project_kernel, seg_rows=seg_rows),
         out_shape=(
             jax.ShapeDtypeStruct((tile_total, row_count), F32),
             jax.ShapeDtypeStruct((tile_total * (SLOTS + folds), LANES), F32),
         ),
-        in_specs=[SMEM, SMEM] + [VMEM] * 5,
+        in_specs=[HBM] * 3 + [VMEM] * 4,
         out_specs=(VMEM, VMEM),
+        scratch_shapes=[
+            pltpu.SMEM(tile_seg.shape, jnp.int32),
+            pltpu.SMEM(tile_count.shape, jnp.int32),
+            pltpu.VMEM(tiles.shape, F32),
+            pltpu.SemaphoreType.DMA((3,)),
+        ],
         compiler_params=PARAMS,
         name="project",
-    )(tile_seg, tile_count, table, tiles, src_index, src_coef, obs_weight)
+    )(*map(in_hbm, (tile_seg, tile_count, tiles)), table, index, coef, weight)
     got = lax.all_gather(sent, "tm", axis=0, tiled=False)
     part = pl.pallas_call(
         functools.partial(

time: 48.5 us -> 41.4 us (0.85)
  local copies, waits for them, and re-layouts: 5.81 us -> 0 us
  other arithmetic: 0.94 us -> 0 us
  Pallas kernels: 12.6 us -> 13.1 us
  blocking collectives: 22.5 us -> 22 us
    unnamed x13 -> x0, local copies, waits for them, and re-layouts: 5.81 us -> none
    unnamed x1 -> x0, other arithmetic: 0.94 us -> none
    all_gather x1, blocking collectives: 12.4 us -> 11.9 us  [per_device(): table = lax.all_gather(directions, 'tm', axis=0, tiled=False)]
    pallas_call x1 -> x2, Pallas kernels: 5.19 us -> 5.68 us  [the longest x1 4.7 us: per_device(): pl.pallas_call(functools.partial(project_kernel, seg_rows=seg_rows), out_...]
  transfers between devices with their start and end apart: 3 -> 3, of which waited for: 0 -> 0; matrix products, arithmetic and copies ran while one was open for 0% -> 0% of each run, Pallas kernels for 14% -> 16%
where the time goes in v2:
time: 41.4 us; the launch traced here: 41.3 us
  blocking collectives  22 us (53%)
  Pallas kernels  13.1 us (32%)
  starting transfers between devices  5.52 us (13%)
  between operations  0.66 us (2%)
    all_gather x1, blocking collectives, per_device(): table = lax.all_gather(directions, 'tm', axis=0, tiled=False)  11.9 us
    all_gather x1, blocking collectives, per_device(): got = lax.all_gather(sent, 'tm', axis=0, tiled=False)  10.1 us
    pallas_call x1, Pallas kernels, per_device(): pl.pallas_call(functools.partial(source_kernel, params=params, tile_total...  6.58 us
    ppermute x3, starting transfers between devices, per_device(): lax.ppermute(part, 'sky', [(i, (i + k) % sky) for i in range(sky)])  5.52 us
    pallas_call x1, Pallas kernels, per_device(): pl.pallas_call(functools.partial(project_kernel, seg_rows=seg_rows), out_...  4.7 us
    pallas_call x1, Pallas kernels, per_device(): pl.pallas_call(pack_kernel, out_shape=(jax.ShapeDtypeStruct((params * (sp...  0.99 us
  transfers between devices with their start and end apart: 3, of which 0 were waited for; matrix products, arithmetic and copies ran while one was open for 0% of the time, Pallas kernels for 16%

profile of v2, /device:TPU:0, one launch (start us, length us, event | category | flops | bytes accessed | tf_op | source)
XLA Modules:
  0.0 41.3 jit_solution(15992913553201717223)
XLA Ops:
  0.6 1.0 %pack.1 = (f32[192,128]{1,0:T(8,128)S(1)}, s32[16,128]{1,0:T(8,128)S(1)}, f32[5,16,128]{2,1,0:T(8,128)S(1)}, f32[16,128]{1,0:T(8,128)S(1)}) custom-call(f32[5,4096]{1,0:T(8,128)} %source.2, f32[16,256]{1,0:T(8,128)} %attitude.2, s32[16,128]{1,0:T(8,128)} %index.1, f32[5,16,128]{2,1,0:T(8,128)} %coef.1, f32[16,128]{1,0:T(8,128)} %weight.1), custom_call_target="tpu_custom_call" | custom-call | tf_op jit(solution)/shard_map/pack/pallas_call | solution.py:208
  1.6 11.9 %all-gather = f32[1536,128]{1,0:T(8,128)S(1)} all-gather(f32[192,128]{1,0:T(8,128)S(1)} %get-tuple-element.12), channel_id=2, replica_groups=mesh['sky'=4,'tm'=8] {'tm'}, dimensions={0}, use_global_device_ids=true | all-gather | bytes 884736 | tf_op jit(solution)/shard_map/all_gather | solution.py:222
  13.5 4.7 %project.1 = (f32[16,128]{1,0:T(8,128)}, f32[160,128]{1,0:T(8,128)S(1)}) custom-call(s32[16]{0:T(128)} %seg_in.1, s32[16]{0:T(128)} %count_in.1, f32[16,128,256]{2,1,0:T(8,128)} %tiles_in.1, f32[8,192,128]{2,1,0:T(8,128)S(1)} %bitcast.4, s32[16,128]{1,0:T(8,128)S(1)} %get-tuple-element.13.index, f32[5,16,128]{2,1,0:T(8,128)S(1)} %get-tuple-element.14.coef, ...), custom_call_target="tpu_custom_call" | custom-call | tf_op jit(solution)/shard_map/project/pallas_call | solution.py:223
  18.2 10.1 %all-gather.1 = f32[1280,128]{1,0:T(8,128)S(1)} all-gather(f32[160,128]{1,0:T(8,128)S(1)} %get-tuple-element.17), channel_id=3, replica_groups=mesh['sky'=4,'tm'=8] {'tm'}, dimensions={0}, use_global_device_ids=true | all-gather | bytes 737280 | tf_op jit(solution)/shard_map/all_gather | solution.py:240
  28.3 0.2 attitude.3.refs_0_
  28.5 1.6 %collective-permute-start = (f32[40,128]{1,0:T(8,128)S(1)}, f32[40,128]{1,0:T(8,128)S(1)}, u32[]{:S(2)}, u32[]{:S(2)}) collective-permute-start(f32[40,128]{1,0:T(8,128)S(1)} %attitude.3.refs_0_), channel_id=1, source_target_pairs={{0,8},{8,16},{16,24},{24,0},{1,9},{9,17},{17,25},{25,1},{2,10},{10... | collective-permute-start | bytes 61448 | tf_op jit(solution)/shard_map/ppermute | solution.py:252
  30.1 2.6 %collective-permute-start.1 = (f32[40,128]{1,0:T(8,128)S(1)}, f32[40,128]{1,0:T(8,128)S(1)}, u32[]{:S(2)}, u32[]{:S(2)}) collective-permute-start(f32[40,128]{1,0:T(8,128)S(1)} %attitude.3.refs_0_), channel_id=1, source_target_pairs={{0,16},{8,24},{16,0},{24,8},{1,17},{9,25},{17,1},{25,9},{2,18},{10... | collective-permute-start | bytes 61448 | tf_op jit(solution)/shard_map/ppermute | solution.py:252
  32.7 1.3 %collective-permute-start.2 = (f32[40,128]{1,0:T(8,128)S(1)}, f32[40,128]{1,0:T(8,128)S(1)}, u32[]{:S(2)}, u32[]{:S(2)}) collective-permute-start(f32[40,128]{1,0:T(8,128)S(1)} %attitude.3.refs_0_), channel_id=1, source_target_pairs={{0,24},{8,0},{16,8},{24,16},{1,25},{9,1},{17,9},{25,17},{2,26},{10... | collective-permute-start | bytes 61448 | tf_op jit(solution)/shard_map/ppermute | solution.py:252
  34.0 6.6 %source.3 = f32[5,4096]{1,0:T(8,128)} custom-call(s32[1]{0:T(128)} %bitcast.1.me, f32[8,160,128]{2,1,0:T(8,128)S(1)} %bitcast.6), custom_call_target="tpu_custom_call" | custom-call | flops 2000000000 | bytes 1000000 | tf_op jit(solution)/shard_map/source/pallas_call | solution.py:255
  40.6 0.0 collective-permute-done.refs_1_
  40.6 0.0 collective-permute-done.1.refs_2_
  40.6 0.0 collective-permute-done.2.refs_3_
  40.6 0.6 %finish.1 = (f32[16,256]{1,0:T(8,128)}, f32[1,1]{1,0:T(1,128)}) custom-call(f32[40,128]{1,0:T(8,128)S(1)} %attitude.3.refs_0_, f32[40,128]{1,0:T(8,128)S(1)} %collective-permute-done.refs_1_, f32[40,128]{1,0:T(8,128)S(1)} %collective-permute-done.1.refs_2_, f32[40,128]{1,0:T(8,128)S(1)} %collective-permute-done.2.refs_3_), custom_call_target="tpu_custom_call" | custom-call | tf_op jit(solution)/shard_map/finish/pallas_call | solution.py:269
Async XLA Ops:
  28.5 12.1 %collective-permute-start = (f32[40,128]{1,0:T(8,128)S(1)}, f32[40,128]{1,0:T(8,128)S(1)}, u32[]{:S(2)}, u32[]{:S(2)}) collective-permute-start(f32[40,128]{1,0:T(8,128)S(1)} %attitude.3.refs_0_), channel_id=1, source_target_pairs={{0,8},{8,16},{16,24},{24,0},{1,9},{9,17},{17,25},{25,1},{2,10},{10... | collective-permute-start | bytes 61448 | tf_op jit(solution)/shard_map/ppermute | solution.py:252
  30.1 10.5 %collective-permute-start.1 = (f32[40,128]{1,0:T(8,128)S(1)}, f32[40,128]{1,0:T(8,128)S(1)}, u32[]{:S(2)}, u32[]{:S(2)}) collective-permute-start(f32[40,128]{1,0:T(8,128)S(1)} %attitude.3.refs_0_), channel_id=1, source_target_pairs={{0,16},{8,24},{16,0},{24,8},{1,17},{9,25},{17,1},{25,9},{2,18},{10... | collective-permute-start | bytes 61448 | tf_op jit(solution)/shard_map/ppermute | solution.py:252
  32.7 7.9 %collective-permute-start.2 = (f32[40,128]{1,0:T(8,128)S(1)}, f32[40,128]{1,0:T(8,128)S(1)}, u32[]{:S(2)}, u32[]{:S(2)}) collective-permute-start(f32[40,128]{1,0:T(8,128)S(1)} %attitude.3.refs_0_), channel_id=1, source_target_pairs={{0,24},{8,0},{16,8},{24,16},{1,25},{9,1},{17,9},{25,17},{2,26},{10... | collective-permute-start | bytes 61448 | tf_op jit(solution)/shard_map/ppermute | solution.py:252

commit v3 on v2

v3 whole, which is shorter than its diff:
```python
import functools

import jax
import jax.numpy as jnp
from jax import lax
from jax.experimental import pallas as pl
from jax.experimental.pallas import tpu as pltpu
from jax.sharding import PartitionSpec as P

LANES = 128
SLOTS = 8
WIDE = 256
NT = (((1,), (1,)), ((), ()))
F32 = jnp.float32
BF16 = jnp.bfloat16
VMEM = pl.BlockSpec(memory_space=pltpu.VMEM)
HBM = pl.BlockSpec(memory_space=pltpu.HBM)
SMEM = pl.BlockSpec(memory_space=pltpu.SMEM)
PARAMS = pltpu.CompilerParams(vmem_limit_bytes=16 * 1024 * 1024)


def in_hbm(x):
    return pltpu.with_memory_space_constraint(x, pltpu.HBM)


def halves(x):
    high = x.astype(BF16)
    return high, (x - high.astype(F32)).astype(BF16)


def rows_of(values, shape):
    ids = lax.broadcasted_iota(jnp.int32, shape, 0)
    out = jnp.zeros(shape, jnp.int32)
    for t, value in enumerate(values):
        out = jnp.where(ids == t, value, out)
    return out


def pack_kernel(source, attitude, index, coef, weight, directions, index_out, coef_out, weight_out, held, sems):
    params, span = source.shape
    seg_rows, cols = attitude.shape
    copies = [
        pltpu.make_async_copy(source, held, sems.at[0]),
        pltpu.make_async_copy(index, index_out, sems.at[2]),
        pltpu.make_async_copy(coef, coef_out, sems.at[3]),
        pltpu.make_async_copy(weight, weight_out, sems.at[4]),
    ]
    base = params * (span // LANES)
    for c in range(cols // LANES):
        copies.append(
            pltpu.make_async_copy(
                attitude.at[:, pl.ds(c * LANES, LANES)],
                directions.at[pl.ds(base + c * seg_rows, seg_rows), :],
                sems.at[5 + c],
            )
        )
    for copy in copies:
        copy.start()
    copies[0].wait()
    for b in range(span // LANES):
        directions[b * params : (b + 1) * params, :] = held[:, b * LANES : (b + 1) * LANES]
    for copy in copies[1:]:
        copy.wait()


def gather(owner, table, ids, picked, params):
    blocks = (table.shape[0] // (params * 8)) * 8
    lane = lax.rem(ids, LANES)
    block = lax.div(ids, LANES) - owner * blocks

    def step(i, picked):
        picked = list(picked)
        for j in range(8):
            hit = block == i * 8 + j
            for k in range(params):
                row = table[pl.ds((i * 8 + j) * params + k, 1), :]
                found = jnp.take_along_axis(jnp.broadcast_to(row, ids.shape), lane, axis=1)
                picked[k] = jnp.where(hit, found, picked[k])
        return tuple(picked)

    return lax.fori_loop(0, blocks // 8, step, tuple(picked))


def pass_kernel(*refs, count):
    for q in range(count):
        refs[-1][q] = refs[q][...]


def pick_kernel(*refs, params, offsets, first):
    me, index, *refs = refs
    ids = index[...]
    rows = ids.shape[0]
    tables, refs = refs[: len(offsets)], refs[len(offsets) :]
    if first:
        tiles_in, out, tiles, sem = refs
        copy = pltpu.make_async_copy(tiles_in, tiles, sem)
        copy.start()
        picked = [jnp.zeros(ids.shape, F32) for _ in range(params)]
    else:
        before, out = refs
        picked = [before[k * rows : (k + 1) * rows, :] for k in range(params)]
    for offset, table in zip(offsets, tables):
        picked = gather(lax.bitwise_xor(me[0], offset), table, ids, picked, params)
    for k in range(params):
        out[k * rows : (k + 1) * rows, :] = picked[k]
    if first:
        copy.wait()


def project_kernel(*refs, seg_rows, offsets, late):
    me, seg_in, count_in, tiles, before, index, coef, weight, *refs = refs
    tables, refs = refs[: len(offsets)], refs[len(offsets) :]
    projected, sent, seg, count, lines, sems = refs
    params, tile_total, width = coef.shape
    folds = tiles.shape[2] // LANES
    base = tables[0].shape[0] - folds * seg_rows
    copies = [
        pltpu.make_async_copy(seg_in, seg, sems.at[0]),
        pltpu.make_async_copy(count_in, count, sems.at[1]),
    ]
    for copy in copies:
        copy.start()
    ids = index[...]
    picked = [before[k * tile_total : (k + 1) * tile_total, :] for k in range(params)]
    for offset, table in zip(offsets, tables):
        lines[offset] = table[base:, :]
        if offset in late:
            picked = gather(lax.bitwise_xor(me[0], offset), table, ids, picked, params)
    for copy in copies:
        copy.wait()
    row_ids = lax.broadcasted_iota(jnp.int32, ids.shape, 0)
    total = jnp.zeros(ids.shape, F32)
    for t in range(tile_total):
        s = seg[t]
        place, local = lax.bitwise_xor(lax.div(s, seg_rows), me[0]), lax.rem(s, seg_rows)
        folded = None
        for c in range(folds):
            direction = lines[place, pl.ds(c * seg_rows + local, 1), :]
            product = tiles[t, :, c * LANES : (c + 1) * LANES] * direction
            folded = product if folded is None else folded + product
        ones = jnp.where(row_ids == t, 1.0, 0.0).astype(BF16)
        for part in halves(folded):
            total = total + lax.dot_general(ones, part, NT, preferred_element_type=F32)
    for k in range(params):
        total = total + coef[k] * picked[k]
    live = lax.broadcasted_iota(jnp.int32, ids.shape, 1) < rows_of(
        [count[t] for t in range(tile_total)], ids.shape
    )
    value = jnp.where(live, total, 0.0)
    weighted = weight[...] * value
    projected[...] = value
    for k in range(params):
        sent[pl.ds(k, tile_total, stride=SLOTS), :] = coef[k] * weighted
    sent[pl.ds(params, tile_total, stride=SLOTS), :] = ids.astype(F32)
    names = rows_of([seg[t] for t in range(tile_total)], ids.shape)
    sent[pl.ds(params + 1, tile_total, stride=SLOTS), :] = names.astype(F32)
    sent[pl.ds(params + 2, tile_total, stride=SLOTS), :] = value * weighted
    columns = weighted.T
    base = tile_total * SLOTS
    for t in range(tile_total):
        grad = jnp.sum(tiles[t] * columns[:, t : t + 1], axis=0, keepdims=True)
        for c in range(folds):
            sent[pl.ds(base + c * tile_total + t, 1), :] = grad[:, c * LANES : (c + 1) * LANES]


def attitude_kernel(*refs, params, tile_total, seg_rows, folds):
    me, *blocks, _, mine, other, packed = refs
    core = lax.rem(me[0], 2)
    lane = lax.broadcasted_iota(jnp.int32, (tile_total, LANES), 1)
    first = (me[0] - core) * seg_rows
    base = tile_total * SLOTS
    group = LANES // tile_total
    sums = [jnp.zeros((2 * seg_rows, LANES), F32) for _ in range(folds)]
    curve = jnp.zeros((tile_total, LANES), F32)
    for g in range(0, len(blocks), group):
        members = blocks[g : g + group]
        hits = []
        for got in members:
            name = got[pl.ds(params + 1, tile_total, stride=SLOTS), :].astype(jnp.int32)
            hits.append(jnp.where(name - first == lane, 1.0, 0.0))
            curve = curve + got[pl.ds(params + 2, tile_total, stride=SLOTS), :]
        pick = jnp.concatenate(hits, axis=0).T[: 2 * seg_rows].astype(BF16)
        for c in range(folds):
            grads = jnp.concatenate(
                [got[pl.ds(base + c * tile_total, tile_total), :] for got in members], axis=0
            )
            for piece in halves(grads):
                sums[c] = sums[c] + jnp.dot(pick, piece, preferred_element_type=F32)
    even = core == 0
    for c in range(folds):
        low, high = sums[c][:seg_rows], sums[c][seg_rows:]
        mine[pl.ds(c * seg_rows, seg_rows), :] = jnp.where(even, low, high)
        other[pl.ds(c * seg_rows, seg_rows), :] = jnp.where(even, high, low)
    whole = jnp.sum(jnp.sum(curve, axis=0, keepdims=True), axis=1, keepdims=True)
    whole = jnp.broadcast_to(whole, (8, LANES))
    mine[pl.ds(folds * seg_rows, 8), :] = whole
    other[pl.ds(folds * seg_rows, 8), :] = whole
    for q, got in enumerate(blocks):
        packed[q] = got[:base, :]


def join_kernel(mine, other, _, part):
    part[...] = mine[...] + other[...]


def source_kernel(*refs, params, tile_total, span, singles, starts, ends, carries, many_range):
    me, *refs = refs
    if ends:
        *refs, token, left, right = refs
        token[...] = jnp.zeros_like(token)
        refs += [left, right]
    left, right = refs[-2:]
    refs = refs[:-2]
    if carries:
        refs[-1][...] = refs[-3][...]
        refs = refs[:-3] + refs[-2:-1]
    target = refs.pop()
    if not starts:
        acc = refs.pop(0)
    high_total = span // WIDE
    depth = params * high_total
    high_ids = lax.broadcasted_iota(jnp.int32, (high_total, LANES), 0).astype(BF16)
    low_ids = lax.broadcasted_iota(jnp.int32, (WIDE, LANES), 0).astype(BF16)
    one, zero = jnp.ones((), BF16), jnp.zeros((), BF16)

    def product(tiles_of):
        for t in range(tile_total):
            at = slice(t * LANES, (t + 1) * LANES)
            tile = tiles_of(t)
            local = tile[params : params + 1].astype(jnp.int32) - me[0] * span
            high = lax.shift_right_arithmetic(local, 8)
            high = jnp.where((high >= 0) & (high < high_total), high, high_total).astype(F32)
            low = lax.bitwise_and(local, WIDE - 1).astype(F32)
            low = jnp.broadcast_to(low, (WIDE, LANES)).astype(BF16)
            right[:, at] = jnp.where(low_ids == low, one, zero)
            hit = high_ids == jnp.broadcast_to(high, (high_total, LANES)).astype(BF16)
            for k in range(params):
                for p, piece in enumerate(halves(jnp.broadcast_to(tile[k : k + 1], (high_total, LANES)))):
                    row = p * depth + k * high_total
                    left[row : row + high_total, at] = jnp.where(hit, piece, zero)
        return lax.dot_general(left[...], right[...], NT, preferred_element_type=F32)

    total = jnp.zeros((2 * depth, WIDE), F32) if starts else acc[...]
    for got in refs[:singles]:
        total = total + product(lambda t: got[t * SLOTS : (t + 1) * SLOTS, :])
    if many_range:
        many = refs[singles]

        def step(d, total):
            return total + product(lambda t: many[d, t * SLOTS : (t + 1) * SLOTS, :])

        total = lax.fori_loop(*many_range, step, total)
    if ends:
        for k in range(params):
            for h in range(high_total):
                row = k * high_total + h
                target[k : k + 1, h * WIDE : (h + 1) * WIDE] = (
                    total[row : row + 1, :] + total[depth + row : depth + row + 1, :]
                )
    else:
        target[...] = total


def finish_kernel(*refs, seg_rows, folds):
    *parts, _, normal, curvature = refs
    total = parts[0][...]
    for part in parts[1:]:
        total = total + part[...]
    for c in range(folds):
        normal[:, c * LANES : (c + 1) * LANES] = total[c * seg_rows : (c + 1) * seg_rows]
    curvature[0, 0] = total[folds * seg_rows, 0]


def cost(microseconds):
    return pl.CostEstimate(flops=int(microseconds * 1e9), bytes_accessed=1, transcendentals=0)


def swapped(x, axis, size, offset):
    return lax.ppermute(x, axis, [(i, i ^ offset) for i in range(size)])


def per_device(tiles, tile_seg, tile_count, src_index, src_coef, obs_weight, att_dir, src_dir, *, sky, tm):
    tile_total, row_count, cols = tiles.shape
    params, span = src_dir.shape
    seg_rows = att_dir.shape[0]
    folds = cols // LANES
    across = range(2, tm, 2)
    me = lax.axis_index("tm").astype(jnp.int32).reshape(1)

    directions, index, coef, weight = pl.pallas_call(
        pack_kernel,
        out_shape=(
            jax.ShapeDtypeStruct((params * (span // LANES) + folds * seg_rows, LANES), F32),
            jax.ShapeDtypeStruct(src_index.shape, src_index.dtype),
            jax.ShapeDtypeStruct(src_coef.shape, F32),
            jax.ShapeDtypeStruct(obs_weight.shape, F32),
        ),
        in_specs=[HBM] * 5,
        out_specs=(VMEM,) * 4,
        scratch_shapes=[pltpu.VMEM((params, span), F32), pltpu.SemaphoreType.DMA((5 + folds,))],
        compiler_params=PARAMS,
        name="pack",
    )(*map(in_hbm, (src_dir, att_dir, src_index, src_coef, obs_weight)))

    far = list(across[1:])
    tables = {0: directions}
    for offset in across:
        tables[offset] = swapped(directions, "tm", tm, offset)
    tables[1] = swapped(directions, "tm", tm, 1)

    picked_shape = jax.ShapeDtypeStruct((params * tile_total, row_count), F32)

    def pick(offsets, before):
        return pl.pallas_call(
            functools.partial(pick_kernel, params=params, offsets=offsets, first=False),
            out_shape=picked_shape,
            in_specs=[SMEM] + [VMEM] * (len(offsets) + 2),
            out_specs=VMEM,
            compiler_params=PARAMS,
            cost_estimate=cost(0.4 * len(offsets)),
            name="pick",
        )(me, index, *[tables[o] for o in offsets], before)

    early = [0]
    picked, tiles_held = pl.pallas_call(
        functools.partial(pick_kernel, params=params, offsets=early, first=True),
        out_shape=(picked_shape, jax.ShapeDtypeStruct(tiles.shape, F32)),
        in_specs=[SMEM] + [VMEM] * (len(early) + 1) + [HBM],
        out_specs=(VMEM, VMEM),
        scratch_shapes=[pltpu.SemaphoreType.DMA],
        compiler_params=PARAMS,
        cost_estimate=cost(1.6),
        name="pick",
    )(me, index, *[tables[o] for o in early], in_hbm(tiles))

    def passed(offsets, after):
        return pl.pallas_call(
            functools.partial(pass_kernel, count=len(offsets)),
            out_shape=jax.ShapeDtypeStruct((len(offsets), *directions.shape), F32),
            in_specs=[VMEM] * (len(offsets) + 1),
            out_specs=VMEM,
            compiler_params=PARAMS,
            name="pass",
        )(*[tables[o] for o in offsets], after)

    first_pair = swapped(passed([2], picked), "tm", tm, 1)
    tables[3] = first_pair[0]
    picked = pick([1, 2], picked)
    others = swapped(passed(far, picked), "tm", tm, 1)
    for q, offset in enumerate(far):
        tables[offset + 1] = others[q]
    picked = pick([3, *far], picked)
    late = [o + 1 for o in across[1:]]
    offsets = sorted(tables)
    projected, sent = pl.pallas_call(
        functools.partial(project_kernel, seg_rows=seg_rows, offsets=offsets, late=late),
        out_shape=(
            jax.ShapeDtypeStruct((tile_total, row_count), F32),
            jax.ShapeDtypeStruct((tile_total * (SLOTS + folds), LANES), F32),
        ),
        in_specs=[SMEM] + [HBM] * 2 + [VMEM] * (5 + tm),
        out_specs=(VMEM, VMEM),
        scratch_shapes=[
            pltpu.SMEM(tile_seg.shape, jnp.int32),
            pltpu.SMEM(tile_count.shape, jnp.int32),
            pltpu.VMEM((tm, folds * seg_rows, LANES), F32),
            pltpu.SemaphoreType.DMA((2,)),
        ],
        compiler_params=PARAMS,
        name="project",
    )(
        me,
        *map(in_hbm, (tile_seg, tile_count)),
        tiles_held,
        picked,
        index,
        coef,
        weight,
        *[tables[o] for o in offsets],
    )

    blocks = [swapped(sent, "tm", tm, offset) for offset in across]
    part_shape = jax.ShapeDtypeStruct((folds * seg_rows + 8, LANES), F32)
    depth = params * (span // WIDE)
    sum_shape = jax.ShapeDtypeStruct((2 * depth, WIDE), F32)

    def source(before, singles, many=None, many_range=(), carried=None, after=None, out=sum_shape):
        operands = [x for x in (before, *singles, many, after, carried) if x is not None]
        ends = out is not sum_shape
        copied = () if carried is None else (jax.ShapeDtypeStruct(carried.shape, F32),)
        if ends:
            copied = (jax.ShapeDtypeStruct((8, LANES), F32),)
        return pl.pallas_call(
            functools.partial(
                source_kernel,
                params=params,
                tile_total=tile_total,
                span=span,
                singles=len(singles),
                starts=before is None,
                ends=ends,
                many_range=many_range,
                carries=carried is not None,
            ),
            out_shape=(out, *copied),
            in_specs=[SMEM] + [VMEM] * len(operands),
            out_specs=(VMEM,) * (1 + len(copied)),
            scratch_shapes=[
                pltpu.VMEM((2 * depth, tile_total * LANES), BF16),
                pltpu.VMEM((WIDE, tile_total * LANES), BF16),
            ],
            compiler_params=PARAMS,
            cost_estimate=cost(0.8 * (len(singles) + (len(range(*many_range)) if many_range else 0))),
            name="source",
        )(me, *operands)

    def join(one, two, after):
        return pl.pallas_call(
            join_kernel,
            out_shape=part_shape,
            in_specs=[VMEM] * 3,
            out_specs=VMEM,
            compiler_params=PARAMS,
            name="join",
        )(one, two, after)

    sums, projected = source(None, [sent], carried=projected)
    (sums,) = source(sums, blocks[:1])
    mine, other, packed = pl.pallas_call(
        functools.partial(
            attitude_kernel, params=params, tile_total=tile_total, seg_rows=seg_rows, folds=folds
        ),
        out_shape=(
            part_shape,
            part_shape,
            jax.ShapeDtypeStruct((tm // 2, tile_total * SLOTS, LANES), F32),
        ),
        in_specs=[SMEM] + [VMEM] * (tm // 2 + 1),
        out_specs=(VMEM,) * 3,
        compiler_params=PARAMS,
        name="attitude",
    )(me, sent, *blocks, sums)
    other = swapped(other, "tm", tm, 1)
    packed = swapped(packed, "tm", tm, 1)
    (sums,) = source(sums, blocks[1:2])
    part = join(mine, other, sums)
    half = tm // 4
    ranges = [(0, half), (half, tm // 2)]
    singles = blocks[2:]
    step = 1
    while step < sky:
        moved = swapped(part, "sky", sky, step)
        step *= 2
        if step < sky:
            if ranges[1:]:
                (sums,) = source(sums, singles, packed, ranges.pop(0), after=None)
                singles = []
            part = join(part, moved, sums)
    src_normal, token = source(
        sums, singles, packed, (ranges[0][0], tm // 2), after=part, out=jax.ShapeDtypeStruct((params, span), F32)
    )
    att_normal, curvature = pl.pallas_call(
        functools.partial(finish_kernel, seg_rows=seg_rows, folds=folds),
        out_shape=(
            jax.ShapeDtypeStruct((seg_rows, cols), F32),
            jax.ShapeDtypeStruct((1, 1), F32),
        ),
        in_specs=[VMEM] * 3,
        out_specs=(VMEM, SMEM),
        compiler_params=PARAMS,
        name="finish",
    )(part, moved, token)
    return projected, att_normal, src_normal, curvature.reshape(())


def solution(mesh):
    placed = (
        P(("sky", "tm"), None, None),
        P(("sky", "tm")),
        P(("sky", "tm")),
        P(("sky", "tm"), None),
        P(None, ("sky", "tm"), None),
        P(("sky", "tm"), None),
        P("tm", None),
        P(None, ("sky", "tm")),
    )
    return jax.shard_map(
        functools.partial(per_device, sky=mesh.shape["sky"], tm=mesh.shape["tm"]),
        mesh=mesh,
        in_specs=placed,
        out_specs=(P(("sky", "tm"), None), P("tm", None), P(None, ("sky", "tm")), P()),
        check_vma=False,
    )
```

time: 41.4 us -> 35.2 us (0.85)
  blocking collectives: 22 us -> 0 us
  starting transfers between devices: 5.52 us -> 13.1 us
  waiting for transfers between devices: 0.01 us -> 5.67 us
  Pallas kernels: 13.1 us -> 15.5 us
    all_gather x2 -> x0, blocking collectives: 22 us -> none  [the longest x1 11.9 us: per_device(): table = lax.all_gather(directions, 'tm', axis=0, tiled=False)]
    ppermute x3 -> x13, starting transfers between devices: 5.52 us -> 13.1 us  [swapped(): return lax.ppermute(x, axis, [(i, i ^ offset) for i in range(size)])]
    ppermute x3 -> x13, waiting for transfers between devices: 0.01 us -> 5.67 us  [swapped(): return lax.ppermute(x, axis, [(i, i ^ offset) for i in range(size)])]
    pallas_call x2 -> x13, Pallas kernels: 11.3 us -> 13.7 us  [the longest x5 6.32 us: source(): pl.pallas_call(functools.partial(source_kernel, params=params, tile_total...]
  transfers between devices with their start and end apart: 3 -> 13, of which waited for: 0 -> 8; matrix products, arithmetic and copies ran while one was open for 0% -> 0% of each run, Pallas kernels for 16% -> 32%
where the time goes in v3:
time: 35.2 us; the launch traced here: 35.1 us
  Pallas kernels  15.5 us (44%)
  starting transfers between devices  13.1 us (37%)
  waiting for transfers between devices  5.67 us (16%)
  between operations  0.76 us (2%)
    ppermute x13, starting transfers between devices, swapped(): return lax.ppermute(x, axis, [(i, i ^ offset) for i in range(size)])  13.1 us
    pallas_call x5, Pallas kernels, source(): pl.pallas_call(functools.partial(source_kernel, params=params, tile_total...  6.32 us
    ppermute x13, waiting for transfers between devices, swapped(): return lax.ppermute(x, axis, [(i, i ^ offset) for i in range(size)])  5.67 us
    pallas_call x2, Pallas kernels, pick(): pl.pallas_call(functools.partial(pick_kernel, params=params, offsets=offs...  3.15 us
    pallas_call x1, Pallas kernels, per_device(): pl.pallas_call(functools.partial(project_kernel, seg_rows=seg_rows, offse...  2.59 us
    pallas_call x1, Pallas kernels, per_device(): pl.pallas_call(functools.partial(pick_kernel, params=params, offsets=earl...  1.6 us
    pallas_call x1, Pallas kernels, per_device(): pl.pallas_call(pack_kernel, out_shape=(jax.ShapeDtypeStruct((params * (sp...  0.99 us
  transfers between devices with their start and end apart: 13, of which 8 were waited for; matrix products, arithmetic and copies ran while one was open for 0% of the time, Pallas kernels for 32%

profile of v3, /device:TPU:0, one launch (start us, length us, event | category | flops | bytes accessed | tf_op | source)
XLA Modules:
  0.0 35.1 jit_solution(5691103283027307498)
XLA Ops:
  0.6 1.0 %pack.1 = (f32[192,128]{1,0:T(8,128)S(1)}, s32[16,128]{1,0:T(8,128)S(1)}, f32[5,16,128]{2,1,0:T(8,128)S(1)}, f32[16,128]{1,0:T(8,128)S(1)}) custom-call(f32[5,4096]{1,0:T(8,128)} %source.6, f32[16,256]{1,0:T(8,128)} %attitude.2, s32[16,128]{1,0:T(8,128)} %index.1, f32[5,16,128]{2,1,0:T(8,128)} %coef.1, f32[16,128]{1,0:T(8,128)} %weight.1), custom_call_target="tpu_custom_call" | custom-call | tf_op jit(solution)/shard_map/pack/pallas_call | solution.py:290
  1.6 3.0 %collective-permute-start = (f32[192,128]{1,0:T(8,128)S(1)}, f32[192,128]{1,0:T(8,128)S(1)}, u32[]{:S(2)}, u32[]{:S(2)}) collective-permute-start(f32[192,128]{1,0:T(8,128)S(1)} %get-tuple-element.22.refs_2_.refs_8_), channel_id=1, source_target_pairs={{0,2},{1,3},{2,0},{3,1},{4,6},{5,7},{6,4},{7,5},{8,10},{9,11},{10,... | collective-permute-start | bytes 294920 | tf_op jit(solution)/shard_map/ppermute | solution.py:279
  4.6 0.0 collective-permute-start.4
  4.6 1.5 %collective-permute-start.2 = (f32[192,128]{1,0:T(8,128)S(1)}, f32[192,128]{1,0:T(8,128)S(1)}, u32[]{:S(2)}, u32[]{:S(2)}) collective-permute-start(f32[192,128]{1,0:T(8,128)S(1)} %get-tuple-element.22.refs_2_.refs_8_), channel_id=1, source_target_pairs={{0,4},{1,5},{2,6},{3,7},{4,0},{5,1},{6,2},{7,3},{8,12},{9,13},{10,... | collective-permute-start | bytes 294920 | tf_op jit(solution)/shard_map/ppermute | solution.py:279
  6.2 0.1 collective-permute-start.3
  6.3 1.6 %pick.3 = (f32[80,128]{1,0:T(8,128)S(1)}, f32[16,128,256]{2,1,0:T(8,128)S(1)}) custom-call(s32[1]{0:T(128)} %bitcast.refs_0_, s32[16,128]{1,0:T(8,128)S(1)} %get-tuple-element.21.refs_1_.refs_5_, f32[192,128]{1,0:T(8,128)S(1)} %get-tuple-element.22.refs_2_.refs_8_, f32[16,128,256]{2,1,0:T(8,128)} %refs_3_.1), custom_call_target="tpu_custom_call" | custom-call | flops 1600000000 | bytes 1 | tf_op jit(solution)/shard_map/pick/pallas_call | solution.py:325
  7.9 0.0 collective-permute-done.refs_0_.refs_3_.refs_10_
  7.9 0.2 collective-permute-start.1
  8.1 0.0 collective-permute-done.4.refs_2_.refs_9_
  8.1 1.3 %pick.4.refs_5_.refs_2_ = f32[80,128]{1,0:T(8,128)S(1)} custom-call(s32[1]{0:T(128)} %bitcast.refs_0_, s32[16,128]{1,0:T(8,128)S(1)} %get-tuple-element.21.refs_1_.refs_5_, f32[192,128]{1,0:T(8,128)S(1)} %collective-permute-done.4.refs_2_.refs_9_, f32[192,128]{1,0:T(8,128)S(1)} %collective-permute-done.refs_0_.refs_3_.refs_10_, ...), custom_call_target="tpu_custom_call" | custom-call | flops 800000000 | bytes 1 | tf_op jit(solution)/shard_map/pick/pallas_call | solution.py:314
  9.4 1.6 %collective-permute-done.2.refs_3_.refs_0_.refs_12_ = f32[192,128]{1,0:T(8,128)S(1)} collective-permute-done((f32[192,128]{1,0:T(8,128)S(1)}, f32[192,128]{1,0:T(8,128)S(1)}, u32[]{:S(2)}, u32[]{:S(2)}) %collective-permute-start.2) | collective-permute-done | bytes 98336 | tf_op jit(solution)/shard_map/ppermute | solution.py:279
  11.0 1.0 %collective-permute-done.3.refs_4_.refs_1_.refs_14_ = f32[192,128]{1,0:T(8,128)S(1)} collective-permute-done((f32[192,128]{1,0:T(8,128)S(1)}, f32[192,128]{1,0:T(8,128)S(1)}, u32[]{:S(2)}, u32[]{:S(2)}) %collective-permute-start.3) | collective-permute-done | bytes 98336 | tf_op jit(solution)/shard_map/ppermute | solution.py:279
  12.0 0.1 collective-permute-start.5
  12.1 0.0 collective-permute-done.1
  12.1 1.9 %pick.5.refs_4_ = f32[80,128]{1,0:T(8,128)S(1)} custom-call(s32[1]{0:T(128)} %bitcast.refs_0_, s32[16,128]{1,0:T(8,128)S(1)} %get-tuple-element.21.refs_1_.refs_5_, f32[192,128]{1,0:T(8,128)S(1)} %bitcast.7, f32[192,128]{1,0:T(8,128)S(1)} %collective-permute-done.2.refs_3_.refs_0_.refs_12_, f32[192,128]{1,0:T(8,128)S(1)} %collective-permute-done.3.refs_4_.refs_1_.refs_14_, ...), custom_call_target="tpu_custom_call" | custom-call | flops 1200000000 | bytes 1 | tf_op jit(solution)/shard_map/pick/pallas_call | solution.py:314
  14.0 0.0 collective-permute-done.5
  14.0 2.6 %project.1 = (f32[16,128]{1,0:T(8,128)S(1)}, f32[160,128]{1,0:T(8,128)S(1)}) custom-call(s32[1]{0:T(128)} %bitcast.refs_0_, s32[16]{0:T(128)} %refs_1_.1, s32[16]{0:T(128)} %refs_2_.1, f32[16,128,256]{2,1,0:T(8,128)S(1)} %get-tuple-element.23.refs_3_, f32[80,128]{1,0:T(8,128)S(1)} %pick.5.refs_4_, s32[16,128]{1,0:T(8,128)S(1)} %get-tuple-element.21.refs_1_.refs_5_, ...), custom_call_target="tpu_custom_call" | custom-call | tf_op jit(solution)/shard_map/project/pallas_call | solution.py:355
  16.6 0.6 %collective-permute-start.6 = (f32[160,128]{1,0:T(8,128)S(1)}, f32[160,128]{1,0:T(8,128)S(1)}, u32[]{:S(2)}, u32[]{:S(2)}) collective-permute-start(f32[160,128]{1,0:T(8,128)S(1)} %get-tuple-element.27.refs_1_), channel_id=1, source_target_pairs={{0,2},{1,3},{2,0},{3,1},{4,6},{5,7},{6,4},{7,5},{8,10},{9,11},{10,... | collective-permute-start | bytes 245768 | tf_op jit(solution)/shard_map/ppermute | solution.py:279
  17.2 1.5 %collective-permute-start.7 = (f32[160,128]{1,0:T(8,128)S(1)}, f32[160,128]{1,0:T(8,128)S(1)}, u32[]{:S(2)}, u32[]{:S(2)}) collective-permute-start(f32[160,128]{1,0:T(8,128)S(1)} %get-tuple-element.27.refs_1_), channel_id=1, source_target_pairs={{0,4},{1,5},{2,6},{3,7},{4,0},{5,1},{6,2},{7,3},{8,12},{9,13},{10,... | collective-permute-start | bytes 245768 | tf_op jit(solution)/shard_map/ppermute | solution.py:279
  18.7 1.5 %collective-permute-start.8 = (f32[160,128]{1,0:T(8,128)S(1)}, f32[160,128]{1,0:T(8,128)S(1)}, u32[]{:S(2)}, u32[]{:S(2)}) collective-permute-start(f32[160,128]{1,0:T(8,128)S(1)} %get-tuple-element.27.refs_1_), channel_id=1, source_target_pairs={{0,6},{1,7},{2,4},{3,5},{4,2},{5,3},{6,0},{7,1},{8,14},{9,15},{10,... | collective-permute-start | bytes 245768 | tf_op jit(solution)/shard_map/ppermute | solution.py:279
  20.2 1.1 %source.7 = (f32[160,256]{1,0:T(8,128)S(1)}, f32[16,128]{1,0:T(8,128)}) custom-call(s32[1]{0:T(128)} %bitcast.refs_0_, f32[160,128]{1,0:T(8,128)S(1)} %get-tuple-element.27.refs_1_, f32[16,128]{1,0:T(8,128)S(1)} %get-tuple-element.28.refs_2_), custom_call_target="tpu_custom_call" | custom-call | flops 800000000 | bytes 1 | tf_op jit(solution)/shard_map/source/pallas_call | solution.py:393
  21.3 0.6 %collective-permute-done.6.refs_2_ = f32[160,128]{1,0:T(8,128)S(1)} collective-permute-done((f32[160,128]{1,0:T(8,128)S(1)}, f32[160,128]{1,0:T(8,128)S(1)}, u32[]{:S(2)}, u32[]{:S(2)}) %collective-permute-start.6) | collective-permute-done | bytes 81952 | tf_op jit(solution)/shard_map/ppermute | solution.py:279
  21.8 0.6 %source.8.refs_5_.refs_1_ = f32[160,256]{1,0:T(8,128)S(1)} custom-call(s32[1]{0:T(128)} %bitcast.refs_0_, f32[160,256]{1,0:T(8,128)S(1)} %get-tuple-element.30.refs_1_, f32[160,128]{1,0:T(8,128)S(1)} %collective-permute-done.6.refs_2_), custom_call_target="tpu_custom_call" | custom-call | flops 800000000 | bytes 1 | tf_op jit(solution)/shard_map/source/pallas_call | solution.py:393
  22.5 0.1 collective-permute-done.7.refs_3_.refs_2_
  22.6 1.6 %collective-permute-done.8.refs_4_.refs_2_ = f32[160,128]{1,0:T(8,128)S(1)} collective-permute-done((f32[160,128]{1,0:T(8,128)S(1)}, f32[160,128]{1,0:T(8,128)S(1)}, u32[]{:S(2)}, u32[]{:S(2)}) %collective-permute-start.8) | collective-permute-done | bytes 81952 | tf_op jit(solution)/shard_map/ppermute | solution.py:279
  24.2 0.2 attitude.3
  24.4 0.0 collective-permute-start.11
  24.4 0.5 %collective-permute-start.9 = (f32[40,128]{1,0:T(8,128)S(1)}, f32[40,128]{1,0:T(8,128)S(1)}, u32[]{:S(2)}, u32[]{:S(2)}) collective-permute-start(f32[40,128]{1,0:T(8,128)S(1)} %get-tuple-element.32), channel_id=1, source_target_pairs={{0,1},{1,0},{2,3},{3,2},{4,5},{5,4},{6,7},{7,6},{8,9},{9,8},{10,11... | collective-permute-start | bytes 61448 | tf_op jit(solution)/shard_map/ppermute | solution.py:279
  24.9 0.6 %source.9._.refs_1_ = f32[160,256]{1,0:T(8,128)S(1)} custom-call(s32[1]{0:T(128)} %bitcast.refs_0_, f32[160,256]{1,0:T(8,128)S(1)} %source.8.refs_5_.refs_1_, f32[160,128]{1,0:T(8,128)S(1)} %collective-permute-done.7.refs_3_.refs_2_), custom_call_target="tpu_custom_call" | custom-call | flops 800000000 | bytes 1 | tf_op jit(solution)/shard_map/source/pallas_call | solution.py:393
  25.6 0.4 %collective-permute-done.9.other = f32[40,128]{1,0:T(8,128)S(1)} collective-permute-done((f32[40,128]{1,0:T(8,128)S(1)}, f32[40,128]{1,0:T(8,128)S(1)}, u32[]{:S(2)}, u32[]{:S(2)}) %collective-permute-start.9) | collective-permute-done | bytes 20512 | tf_op jit(solution)/shard_map/ppermute | solution.py:279
  26.0 1.6 %collective-permute-start.10 = (f32[40,128]{1,0:T(8,128)S(1)}, f32[40,128]{1,0:T(8,128)S(1)}, u32[]{:S(2)}, u32[]{:S(2)}) collective-permute-start(f32[40,128]{1,0:T(8,128)S(1)} %join.2.mine), channel_id=1, source_target_pairs={{0,8},{8,0},{16,24},{24,16},{1,9},{9,1},{17,25},{25,17},{2,10},{10... | collective-permute-start | bytes 61448 | tf_op jit(solution)/shard_map/ppermute | solution.py:279
  27.6 0.0 collective-permute-done.11.refs_3_.refs_2_
  27.6 1.9 %source.10._.refs_1_ = f32[160,256]{1,0:T(8,128)S(1)} custom-call(s32[1]{0:T(128)} %bitcast.refs_0_, f32[160,256]{1,0:T(8,128)S(1)} %source.9._.refs_1_, f32[160,128]{1,0:T(8,128)S(1)} %collective-permute-done.8.refs_4_.refs_2_, f32[4,128,128]{2,1,0:T(8,128)S(1)} %collective-permute-done.11.refs_3_.refs_2_), custom_call_target="tpu_custom_call" | custom-call | flops 2400000000 | bytes 1 | tf_op jit(solution)/shard_map/source/pallas_call | solution.py:393
  29.5 0.3 collective-permute-done.10.other
  29.8 2.6 %collective-permute-start.12 = (f32[40,128]{1,0:T(8,128)S(1)}, f32[40,128]{1,0:T(8,128)S(1)}, u32[]{:S(2)}, u32[]{:S(2)}) collective-permute-start(f32[40,128]{1,0:T(8,128)S(1)} %join.3.refs_3_.refs_0_), channel_id=1, source_target_pairs={{0,16},{8,24},{16,0},{24,8},{1,17},{9,25},{17,1},{25,9},{2,18},{10... | collective-permute-start | bytes 61448 | tf_op jit(solution)/shard_map/ppermute | solution.py:279
  32.4 2.0 %source.11 = (f32[5,4096]{1,0:T(8,128)}, f32[8,128]{1,0:T(8,128)S(1)}) custom-call(s32[1]{0:T(128)} %bitcast.refs_0_, f32[160,256]{1,0:T(8,128)S(1)} %source.10._.refs_1_, f32[4,128,128]{2,1,0:T(8,128)S(1)} %collective-permute-done.11.refs_3_.refs_2_, f32[40,128]{1,0:T(8,128)S(1)} %join.3.refs_3_.refs_0_), custom_call_target="tpu_custom_call" | custom-call | flops 1600000000 | bytes 1 | tf_op jit(solution)/shard_map/source/pallas_call | solution.py:393
  34.4 0.1 collective-permute-done.12.refs_1_
  34.5 0.6 %finish.1 = (f32[16,256]{1,0:T(8,128)}, f32[1,1]{1,0:T(1,128)}) custom-call(f32[40,128]{1,0:T(8,128)S(1)} %join.3.refs_3_.refs_0_, f32[40,128]{1,0:T(8,128)S(1)} %collective-permute-done.12.refs_1_, f32[8,128]{1,0:T(8,128)S(1)} %get-tuple-element.34.refs_2_), custom_call_target="tpu_custom_call" | custom-call | tf_op jit(solution)/shard_map/finish/pallas_call | solution.py:462
  (5 shorter events, 0.0 us)
Async XLA Ops:
  1.6 6.3 %collective-permute-start = (f32[192,128]{1,0:T(8,128)S(1)}, f32[192,128]{1,0:T(8,128)S(1)}, u32[]{:S(2)}, u32[]{:S(2)}) collective-permute-start(f32[192,128]{1,0:T(8,128)S(1)} %get-tuple-element.22.refs_2_.refs_8_), channel_id=1, source_target_pairs={{0,2},{1,3},{2,0},{3,1},{4,6},{5,7},{6,4},{7,5},{8,10},{9,11},{10,... | collective-permute-start | bytes 294920 | tf_op jit(solution)/shard_map/ppermute | solution.py:279
  4.6 3.5 %collective-permute-start.4 = (f32[192,128]{1,0:T(8,128)S(1)}, f32[192,128]{1,0:T(8,128)S(1)}, u32[]{:S(2)}, u32[]{:S(2)}) collective-permute-start(f32[192,128]{1,0:T(8,128)S(1)} %get-tuple-element.22.refs_2_.refs_8_), channel_id=1, source_target_pairs={{0,1},{1,0},{2,3},{3,2},{4,5},{5,4},{6,7},{7,6},{8,9},{9,8},{10,11... | collective-permute-start | bytes 294920 | tf_op jit(solution)/shard_map/ppermute | solution.py:279
  4.6 6.4 %collective-permute-start.2 = (f32[192,128]{1,0:T(8,128)S(1)}, f32[192,128]{1,0:T(8,128)S(1)}, u32[]{:S(2)}, u32[]{:S(2)}) collective-permute-start(f32[192,128]{1,0:T(8,128)S(1)} %get-tuple-element.22.refs_2_.refs_8_), channel_id=1, source_target_pairs={{0,4},{1,5},{2,6},{3,7},{4,0},{5,1},{6,2},{7,3},{8,12},{9,13},{10,... | collective-permute-start | bytes 294920 | tf_op jit(solution)/shard_map/ppermute | solution.py:279
  6.2 5.8 %collective-permute-start.3 = (f32[192,128]{1,0:T(8,128)S(1)}, f32[192,128]{1,0:T(8,128)S(1)}, u32[]{:S(2)}, u32[]{:S(2)}) collective-permute-start(f32[192,128]{1,0:T(8,128)S(1)} %get-tuple-element.22.refs_2_.refs_8_), channel_id=1, source_target_pairs={{0,6},{1,7},{2,4},{3,5},{4,2},{5,3},{6,0},{7,1},{8,14},{9,15},{10,... | collective-permute-start | bytes 294920 | tf_op jit(solution)/shard_map/ppermute | solution.py:279
  7.9 4.2 %collective-permute-start.1 = (f32[1,192,128]{2,1,0:T(8,128)S(1)}, f32[1,192,128]{2,1,0:T(8,128)S(1)}, u32[]{:S(2)}, u32[]{:S(2)}) collective-permute-start(f32[1,192,128]{2,1,0:T(8,128)S(1)} %pass.2), channel_id=1, source_target_pairs={{0,1},{1,0},{2,3},{3,2},{4,5},{5,4},{6,7},{7,6},{8,9},{9,8},{10,11... | collective-permute-start | bytes 294920 | tf_op jit(solution)/shard_map/ppermute | solution.py:279
  12.0 2.0 %collective-permute-start.5 = (f32[2,192,128]{2,1,0:T(8,128)S(1)}, f32[2,192,128]{2,1,0:T(8,128)S(1)}, u32[]{:S(2)}, u32[]{:S(2)}) collective-permute-start(f32[2,192,128]{2,1,0:T(8,128)S(1)} %pass.3), channel_id=1, source_target_pairs={{0,1},{1,0},{2,3},{3,2},{4,5},{5,4},{6,7},{7,6},{8,9},{9,8},{10,11... | collective-permute-start | bytes 589832 | tf_op jit(solution)/shard_map/ppermute | solution.py:279
  16.6 5.2 %collective-permute-start.6 = (f32[160,128]{1,0:T(8,128)S(1)}, f32[160,128]{1,0:T(8,128)S(1)}, u32[]{:S(2)}, u32[]{:S(2)}) collective-permute-start(f32[160,128]{1,0:T(8,128)S(1)} %get-tuple-element.27.refs_1_), channel_id=1, source_target_pairs={{0,2},{1,3},{2,0},{3,1},{4,6},{5,7},{6,4},{7,5},{8,10},{9,11},{10,... | collective-permute-start | bytes 245768 | tf_op jit(solution)/shard_map/ppermute | solution.py:279
  17.2 5.4 %collective-permute-start.7 = (f32[160,128]{1,0:T(8,128)S(1)}, f32[160,128]{1,0:T(8,128)S(1)}, u32[]{:S(2)}, u32[]{:S(2)}) collective-permute-start(f32[160,128]{1,0:T(8,128)S(1)} %get-tuple-element.27.refs_1_), channel_id=1, source_target_pairs={{0,4},{1,5},{2,6},{3,7},{4,0},{5,1},{6,2},{7,3},{8,12},{9,13},{10,... | collective-permute-start | bytes 245768 | tf_op jit(solution)/shard_map/ppermute | solution.py:279
  18.7 5.5 %collective-permute-start.8 = (f32[160,128]{1,0:T(8,128)S(1)}, f32[160,128]{1,0:T(8,128)S(1)}, u32[]{:S(2)}, u32[]{:S(2)}) collective-permute-start(f32[160,128]{1,0:T(8,128)S(1)} %get-tuple-element.27.refs_1_), channel_id=1, source_target_pairs={{0,6},{1,7},{2,4},{3,5},{4,2},{5,3},{6,0},{7,1},{8,14},{9,15},{10,... | collective-permute-start | bytes 245768 | tf_op jit(solution)/shard_map/ppermute | solution.py:279
  24.4 3.2 %collective-permute-start.11 = (f32[4,128,128]{2,1,0:T(8,128)S(1)}, f32[4,128,128]{2,1,0:T(8,128)S(1)}, u32[]{:S(2)}, u32[]{:S(2)}) collective-permute-start(f32[4,128,128]{2,1,0:T(8,128)S(1)} %get-tuple-element.33), channel_id=1, source_target_pairs={{0,1},{1,0},{2,3},{3,2},{4,5},{5,4},{6,7},{7,6},{8,9},{9,8},{10,11... | collective-permute-start | bytes 786440 | tf_op jit(solution)/shard_map/ppermute | solution.py:279
  24.4 1.6 %collective-permute-start.9 = (f32[40,128]{1,0:T(8,128)S(1)}, f32[40,128]{1,0:T(8,128)S(1)}, u32[]{:S(2)}, u32[]{:S(2)}) collective-permute-start(f32[40,128]{1,0:T(8,128)S(1)} %get-tuple-element.32), channel_id=1, source_target_pairs={{0,1},{1,0},{2,3},{3,2},{4,5},{5,4},{6,7},{7,6},{8,9},{9,8},{10,11... | collective-permute-start | bytes 61448 | tf_op jit(solution)/shard_map/ppermute | solution.py:279
  26.0 3.8 %collective-permute-start.10 = (f32[40,128]{1,0:T(8,128)S(1)}, f32[40,128]{1,0:T(8,128)S(1)}, u32[]{:S(2)}, u32[]{:S(2)}) collective-permute-start(f32[40,128]{1,0:T(8,128)S(1)} %join.2.mine), channel_id=1, source_target_pairs={{0,8},{8,0},{16,24},{24,16},{1,9},{9,1},{17,25},{25,17},{2,10},{10... | collective-permute-start | bytes 61448 | tf_op jit(solution)/shard_map/ppermute | solution.py:279
  29.8 4.7 %collective-permute-start.12 = (f32[40,128]{1,0:T(8,128)S(1)}, f32[40,128]{1,0:T(8,128)S(1)}, u32[]{:S(2)}, u32[]{:S(2)}) collective-permute-start(f32[40,128]{1,0:T(8,128)S(1)} %join.3.refs_3_.refs_0_), channel_id=1, source_target_pairs={{0,16},{8,24},{16,0},{24,8},{1,17},{9,25},{17,1},{25,9},{2,18},{10... | collective-permute-start | bytes 61448 | tf_op jit(solution)/shard_map/ppermute | solution.py:279

commit v4 on v3

--- a/solution.py
+++ b/solution.py
@@ -68,17 +68,14 @@
     lane = lax.rem(ids, LANES)
     block = lax.div(ids, LANES) - owner * blocks
 
-    def step(i, picked):
-        picked = list(picked)
-        for j in range(8):
-            hit = block == i * 8 + j
-            for k in range(params):
-                row = table[pl.ds((i * 8 + j) * params + k, 1), :]
-                found = jnp.take_along_axis(jnp.broadcast_to(row, ids.shape), lane, axis=1)
-                picked[k] = jnp.where(hit, found, picked[k])
-        return tuple(picked)
-
-    return lax.fori_loop(0, blocks // 8, step, tuple(picked))
+    picked = list(picked)
+    for b in range(blocks):
+        hit = block == b
+        for k in range(params):
+            row = table[b * params + k : b * params + k + 1, :]
+            found = jnp.take_along_axis(jnp.broadcast_to(row, ids.shape), lane, axis=1)
+            picked[k] = jnp.where(hit, found, picked[k])
+    return picked
 
 
 def pass_kernel(*refs, count):
@@ -138,9 +135,7 @@
             direction = lines[place, pl.ds(c * seg_rows + local, 1), :]
             product = tiles[t, :, c * LANES : (c + 1) * LANES] * direction
             folded = product if folded is None else folded + product
-        ones = jnp.where(row_ids == t, 1.0, 0.0).astype(BF16)
-        for part in halves(folded):
-            total = total + lax.dot_general(ones, part, NT, preferred_element_type=F32)
+        total = jnp.where(row_ids == t, jnp.sum(folded.T, axis=0, keepdims=True), total)
     for k in range(params):
         total = total + coef[k] * picked[k]
     live = lax.broadcasted_iota(jnp.int32, ids.shape, 1) < rows_of(

time: 35.2 us -> 33.7 us (0.957)
  Pallas kernels: 15.5 us -> 13.3 us
  waiting for transfers between devices: 5.67 us -> 6.3 us
    pallas_call x2, Pallas kernels: 3.15 us -> 1.88 us  [pick(): pl.pallas_call(functools.partial(pick_kernel, params=params, offsets=offs...]
    pallas_call x1, Pallas kernels: 2.59 us -> 1.66 us  [per_device(): pl.pallas_call(functools.partial(project_kernel, seg_rows=seg_rows, offse...]
    ppermute x13, waiting for transfers between devices: 5.67 us -> 6.3 us  [swapped(): return lax.ppermute(x, axis, [(i, i ^ offset) for i in range(size)])]
  transfers between devices with their start and end apart: 13 -> 13, of which waited for: 8 -> 9; matrix products, arithmetic and copies ran while one was open for 0% -> 0% of each run, Pallas kernels for 32% -> 29%
where the time goes in v4:
time: 33.7 us; the launch traced here: 33.5 us
  Pallas kernels  13.3 us (39%)
  starting transfers between devices  13.1 us (39%)
  waiting for transfers between devices  6.3 us (19%)
  between operations  0.75 us (2%)
    ppermute x13, starting transfers between devices, swapped(): return lax.ppermute(x, axis, [(i, i ^ offset) for i in range(size)])  13.1 us
    pallas_call x5, Pallas kernels, source(): pl.pallas_call(functools.partial(source_kernel, params=params, tile_total...  6.32 us
    ppermute x13, waiting for transfers between devices, swapped(): return lax.ppermute(x, axis, [(i, i ^ offset) for i in range(size)])  6.3 us
    pallas_call x2, Pallas kernels, pick(): pl.pallas_call(functools.partial(pick_kernel, params=params, offsets=offs...  1.88 us
    pallas_call x1, Pallas kernels, per_device(): pl.pallas_call(functools.partial(project_kernel, seg_rows=seg_rows, offse...  1.66 us
    pallas_call x1, Pallas kernels, per_device(): pl.pallas_call(functools.partial(pick_kernel, params=params, offsets=earl...  1.61 us
    pallas_call x1, Pallas kernels, per_device(): pl.pallas_call(pack_kernel, out_shape=(jax.ShapeDtypeStruct((params * (sp...  0.99 us
  transfers between devices with their start and end apart: 13, of which 9 were waited for; matrix products, arithmetic and copies ran while one was open for 0% of the time, Pallas kernels for 29%

profile of v4, /device:TPU:0, one launch (start us, length us, event | category | flops | bytes accessed | tf_op | source)
XLA Modules:
  0.0 33.5 jit_solution(7000467470663709992)
XLA Ops:
  0.6 1.0 %pack.1 = (f32[192,128]{1,0:T(8,128)S(1)}, s32[16,128]{1,0:T(8,128)S(1)}, f32[5,16,128]{2,1,0:T(8,128)S(1)}, f32[16,128]{1,0:T(8,128)S(1)}) custom-call(f32[5,4096]{1,0:T(8,128)} %source.6, f32[16,256]{1,0:T(8,128)} %attitude.2, s32[16,128]{1,0:T(8,128)} %index.1, f32[5,16,128]{2,1,0:T(8,128)} %coef.1, f32[16,128]{1,0:T(8,128)} %weight.1), custom_call_target="tpu_custom_call" | custom-call | tf_op jit(solution)/shard_map/pack/pallas_call | solution.py:285
  1.6 3.0 %collective-permute-start = (f32[192,128]{1,0:T(8,128)S(1)}, f32[192,128]{1,0:T(8,128)S(1)}, u32[]{:S(2)}, u32[]{:S(2)}) collective-permute-start(f32[192,128]{1,0:T(8,128)S(1)} %get-tuple-element.22.refs_2_.refs_8_), channel_id=1, source_target_pairs={{0,2},{1,3},{2,0},{3,1},{4,6},{5,7},{6,4},{7,5},{8,10},{9,11},{10,... | collective-permute-start | bytes 294920 | tf_op jit(solution)/shard_map/ppermute | solution.py:274
  4.6 0.0 collective-permute-start.4
  4.6 1.5 %collective-permute-start.2 = (f32[192,128]{1,0:T(8,128)S(1)}, f32[192,128]{1,0:T(8,128)S(1)}, u32[]{:S(2)}, u32[]{:S(2)}) collective-permute-start(f32[192,128]{1,0:T(8,128)S(1)} %get-tuple-element.22.refs_2_.refs_8_), channel_id=1, source_target_pairs={{0,4},{1,5},{2,6},{3,7},{4,0},{5,1},{6,2},{7,3},{8,12},{9,13},{10,... | collective-permute-start | bytes 294920 | tf_op jit(solution)/shard_map/ppermute | solution.py:274
  6.2 0.1 collective-permute-start.3
  6.3 1.6 %pick.3 = (f32[80,128]{1,0:T(8,128)S(1)}, f32[16,128,256]{2,1,0:T(8,128)S(1)}) custom-call(s32[1]{0:T(128)} %bitcast.refs_0_, s32[16,128]{1,0:T(8,128)S(1)} %get-tuple-element.21.refs_1_.refs_5_, f32[192,128]{1,0:T(8,128)S(1)} %get-tuple-element.22.refs_2_.refs_8_, f32[16,128,256]{2,1,0:T(8,128)} %refs_3_.1), custom_call_target="tpu_custom_call" | custom-call | flops 1600000000 | bytes 1 | tf_op jit(solution)/shard_map/pick/pallas_call | solution.py:320
  7.9 0.0 collective-permute-done.refs_0_.refs_3_.refs_10_
  7.9 0.2 collective-permute-start.1
  8.1 0.0 collective-permute-done.4.refs_2_.refs_9_
  8.1 0.8 %pick.4.refs_5_.refs_2_ = f32[80,128]{1,0:T(8,128)S(1)} custom-call(s32[1]{0:T(128)} %bitcast.refs_0_, s32[16,128]{1,0:T(8,128)S(1)} %get-tuple-element.21.refs_1_.refs_5_, f32[192,128]{1,0:T(8,128)S(1)} %collective-permute-done.4.refs_2_.refs_9_, f32[192,128]{1,0:T(8,128)S(1)} %collective-permute-done.refs_0_.refs_3_.refs_10_, ...), custom_call_target="tpu_custom_call" | custom-call | flops 800000000 | bytes 1 | tf_op jit(solution)/shard_map/pick/pallas_call | solution.py:309
  8.9 2.1 %collective-permute-done.2.refs_3_.refs_0_.refs_12_ = f32[192,128]{1,0:T(8,128)S(1)} collective-permute-done((f32[192,128]{1,0:T(8,128)S(1)}, f32[192,128]{1,0:T(8,128)S(1)}, u32[]{:S(2)}, u32[]{:S(2)}) %collective-permute-start.2) | collective-permute-done | bytes 98336 | tf_op jit(solution)/shard_map/ppermute | solution.py:274
  11.0 1.0 %collective-permute-done.3.refs_4_.refs_1_.refs_14_ = f32[192,128]{1,0:T(8,128)S(1)} collective-permute-done((f32[192,128]{1,0:T(8,128)S(1)}, f32[192,128]{1,0:T(8,128)S(1)}, u32[]{:S(2)}, u32[]{:S(2)}) %collective-permute-start.3) | collective-permute-done | bytes 98336 | tf_op jit(solution)/shard_map/ppermute | solution.py:274
  12.0 0.1 collective-permute-start.5
  12.1 0.0 collective-permute-done.1
  12.1 1.1 %pick.5.refs_4_ = f32[80,128]{1,0:T(8,128)S(1)} custom-call(s32[1]{0:T(128)} %bitcast.refs_0_, s32[16,128]{1,0:T(8,128)S(1)} %get-tuple-element.21.refs_1_.refs_5_, f32[192,128]{1,0:T(8,128)S(1)} %bitcast.7, f32[192,128]{1,0:T(8,128)S(1)} %collective-permute-done.2.refs_3_.refs_0_.refs_12_, f32[192,128]{1,0:T(8,128)S(1)} %collective-permute-done.3.refs_4_.refs_1_.refs_14_, ...), custom_call_target="tpu_custom_call" | custom-call | flops 1200000000 | bytes 1 | tf_op jit(solution)/shard_map/pick/pallas_call | solution.py:309
  13.2 0.3 collective-permute-done.5
  13.5 1.7 %project.1 = (f32[16,128]{1,0:T(8,128)S(1)}, f32[160,128]{1,0:T(8,128)S(1)}) custom-call(s32[1]{0:T(128)} %bitcast.refs_0_, s32[16]{0:T(128)} %refs_1_.1, s32[16]{0:T(128)} %refs_2_.1, f32[16,128,256]{2,1,0:T(8,128)S(1)} %get-tuple-element.23.refs_3_, f32[80,128]{1,0:T(8,128)S(1)} %pick.5.refs_4_, s32[16,128]{1,0:T(8,128)S(1)} %get-tuple-element.21.refs_1_.refs_5_, ...), custom_call_target="tpu_custom_call" | custom-call | tf_op jit(solution)/shard_map/project/pallas_call | solution.py:350
  15.2 0.6 %collective-permute-start.6 = (f32[160,128]{1,0:T(8,128)S(1)}, f32[160,128]{1,0:T(8,128)S(1)}, u32[]{:S(2)}, u32[]{:S(2)}) collective-permute-start(f32[160,128]{1,0:T(8,128)S(1)} %get-tuple-element.27.refs_1_), channel_id=1, source_target_pairs={{0,2},{1,3},{2,0},{3,1},{4,6},{5,7},{6,4},{7,5},{8,10},{9,11},{10,... | collective-permute-start | bytes 245768 | tf_op jit(solution)/shard_map/ppermute | solution.py:274
  15.8 1.5 %collective-permute-start.7 = (f32[160,128]{1,0:T(8,128)S(1)}, f32[160,128]{1,0:T(8,128)S(1)}, u32[]{:S(2)}, u32[]{:S(2)}) collective-permute-start(f32[160,128]{1,0:T(8,128)S(1)} %get-tuple-element.27.refs_1_), channel_id=1, source_target_pairs={{0,4},{1,5},{2,6},{3,7},{4,0},{5,1},{6,2},{7,3},{8,12},{9,13},{10,... | collective-permute-start | bytes 245768 | tf_op jit(solution)/shard_map/ppermute | solution.py:274
  17.3 1.5 %collective-permute-start.8 = (f32[160,128]{1,0:T(8,128)S(1)}, f32[160,128]{1,0:T(8,128)S(1)}, u32[]{:S(2)}, u32[]{:S(2)}) collective-permute-start(f32[160,128]{1,0:T(8,128)S(1)} %get-tuple-element.27.refs_1_), channel_id=1, source_target_pairs={{0,6},{1,7},{2,4},{3,5},{4,2},{5,3},{6,0},{7,1},{8,14},{9,15},{10,... | collective-permute-start | bytes 245768 | tf_op jit(solution)/shard_map/ppermute | solution.py:274
  18.7 1.1 %source.7 = (f32[160,256]{1,0:T(8,128)S(1)}, f32[16,128]{1,0:T(8,128)}) custom-call(s32[1]{0:T(128)} %bitcast.refs_0_, f32[160,128]{1,0:T(8,128)S(1)} %get-tuple-element.27.refs_1_, f32[16,128]{1,0:T(8,128)S(1)} %get-tuple-element.28.refs_2_), custom_call_target="tpu_custom_call" | custom-call | flops 800000000 | bytes 1 | tf_op jit(solution)/shard_map/source/pallas_call | solution.py:388
  19.9 0.3 collective-permute-done.6.refs_2_
  20.2 0.6 %source.8.refs_5_.refs_1_ = f32[160,256]{1,0:T(8,128)S(1)} custom-call(s32[1]{0:T(128)} %bitcast.refs_0_, f32[160,256]{1,0:T(8,128)S(1)} %get-tuple-element.30.refs_1_, f32[160,128]{1,0:T(8,128)S(1)} %collective-permute-done.6.refs_2_), custom_call_target="tpu_custom_call" | custom-call | flops 800000000 | bytes 1 | tf_op jit(solution)/shard_map/source/pallas_call | solution.py:388
  20.8 0.2 collective-permute-done.7.refs_3_.refs_2_
  21.0 1.6 %collective-permute-done.8.refs_4_.refs_2_ = f32[160,128]{1,0:T(8,128)S(1)} collective-permute-done((f32[160,128]{1,0:T(8,128)S(1)}, f32[160,128]{1,0:T(8,128)S(1)}, u32[]{:S(2)}, u32[]{:S(2)}) %collective-permute-start.8) | collective-permute-done | bytes 81952 | tf_op jit(solution)/shard_map/ppermute | solution.py:274
  22.6 0.2 attitude.3
  22.8 0.0 collective-permute-start.11
  22.8 0.5 %collective-permute-start.9 = (f32[40,128]{1,0:T(8,128)S(1)}, f32[40,128]{1,0:T(8,128)S(1)}, u32[]{:S(2)}, u32[]{:S(2)}) collective-permute-start(f32[40,128]{1,0:T(8,128)S(1)} %get-tuple-element.32), channel_id=1, source_target_pairs={{0,1},{1,0},{2,3},{3,2},{4,5},{5,4},{6,7},{7,6},{8,9},{9,8},{10,11... | collective-permute-start | bytes 61448 | tf_op jit(solution)/shard_map/ppermute | solution.py:274
  23.4 0.6 %source.9._.refs_1_ = f32[160,256]{1,0:T(8,128)S(1)} custom-call(s32[1]{0:T(128)} %bitcast.refs_0_, f32[160,256]{1,0:T(8,128)S(1)} %source.8.refs_5_.refs_1_, f32[160,128]{1,0:T(8,128)S(1)} %collective-permute-done.7.refs_3_.refs_2_), custom_call_target="tpu_custom_call" | custom-call | flops 800000000 | bytes 1 | tf_op jit(solution)/shard_map/source/pallas_call | solution.py:388
  24.0 0.4 %collective-permute-done.9.other = f32[40,128]{1,0:T(8,128)S(1)} collective-permute-done((f32[40,128]{1,0:T(8,128)S(1)}, f32[40,128]{1,0:T(8,128)S(1)}, u32[]{:S(2)}, u32[]{:S(2)}) %collective-permute-start.9) | collective-permute-done | bytes 20512 | tf_op jit(solution)/shard_map/ppermute | solution.py:274
  24.4 1.6 %collective-permute-start.10 = (f32[40,128]{1,0:T(8,128)S(1)}, f32[40,128]{1,0:T(8,128)S(1)}, u32[]{:S(2)}, u32[]{:S(2)}) collective-permute-start(f32[40,128]{1,0:T(8,128)S(1)} %join.2.mine), channel_id=1, source_target_pairs={{0,8},{8,0},{16,24},{24,16},{1,9},{9,1},{17,25},{25,17},{2,10},{10... | collective-permute-start | bytes 61448 | tf_op jit(solution)/shard_map/ppermute | solution.py:274
  26.0 0.0 collective-permute-done.11.refs_3_.refs_2_
  26.0 1.9 %source.10._.refs_1_ = f32[160,256]{1,0:T(8,128)S(1)} custom-call(s32[1]{0:T(128)} %bitcast.refs_0_, f32[160,256]{1,0:T(8,128)S(1)} %source.9._.refs_1_, f32[160,128]{1,0:T(8,128)S(1)} %collective-permute-done.8.refs_4_.refs_2_, f32[4,128,128]{2,1,0:T(8,128)S(1)} %collective-permute-done.11.refs_3_.refs_2_), custom_call_target="tpu_custom_call" | custom-call | flops 2400000000 | bytes 1 | tf_op jit(solution)/shard_map/source/pallas_call | solution.py:388
  27.9 0.3 collective-permute-done.10.other
  28.2 2.6 %collective-permute-start.12 = (f32[40,128]{1,0:T(8,128)S(1)}, f32[40,128]{1,0:T(8,128)S(1)}, u32[]{:S(2)}, u32[]{:S(2)}) collective-permute-start(f32[40,128]{1,0:T(8,128)S(1)} %join.3.refs_3_.refs_0_), channel_id=1, source_target_pairs={{0,16},{8,24},{16,0},{24,8},{1,17},{9,25},{17,1},{25,9},{2,18},{10... | collective-permute-start | bytes 61448 | tf_op jit(solution)/shard_map/ppermute | solution.py:274
  30.8 2.0 %source.11 = (f32[5,4096]{1,0:T(8,128)}, f32[8,128]{1,0:T(8,128)S(1)}) custom-call(s32[1]{0:T(128)} %bitcast.refs_0_, f32[160,256]{1,0:T(8,128)S(1)} %source.10._.refs_1_, f32[4,128,128]{2,1,0:T(8,128)S(1)} %collective-permute-done.11.refs_3_.refs_2_, f32[40,128]{1,0:T(8,128)S(1)} %join.3.refs_3_.refs_0_), custom_call_target="tpu_custom_call" | custom-call | flops 1600000000 | bytes 1 | tf_op jit(solution)/shard_map/source/pallas_call | solution.py:388
  32.8 0.1 collective-permute-done.12.refs_1_
  32.9 0.6 %finish.1 = (f32[16,256]{1,0:T(8,128)}, f32[1,1]{1,0:T(1,128)}) custom-call(f32[40,128]{1,0:T(8,128)S(1)} %join.3.refs_3_.refs_0_, f32[40,128]{1,0:T(8,128)S(1)} %collective-permute-done.12.refs_1_, f32[8,128]{1,0:T(8,128)S(1)} %get-tuple-element.34.refs_2_), custom_call_target="tpu_custom_call" | custom-call | tf_op jit(solution)/shard_map/finish/pallas_call | solution.py:457
  (5 shorter events, 0.0 us)
Async XLA Ops:
  1.6 6.3 %collective-permute-start = (f32[192,128]{1,0:T(8,128)S(1)}, f32[192,128]{1,0:T(8,128)S(1)}, u32[]{:S(2)}, u32[]{:S(2)}) collective-permute-start(f32[192,128]{1,0:T(8,128)S(1)} %get-tuple-element.22.refs_2_.refs_8_), channel_id=1, source_target_pairs={{0,2},{1,3},{2,0},{3,1},{4,6},{5,7},{6,4},{7,5},{8,10},{9,11},{10,... | collective-permute-start | bytes 294920 | tf_op jit(solution)/shard_map/ppermute | solution.py:274
  4.6 3.5 %collective-permute-start.4 = (f32[192,128]{1,0:T(8,128)S(1)}, f32[192,128]{1,0:T(8,128)S(1)}, u32[]{:S(2)}, u32[]{:S(2)}) collective-permute-start(f32[192,128]{1,0:T(8,128)S(1)} %get-tuple-element.22.refs_2_.refs_8_), channel_id=1, source_target_pairs={{0,1},{1,0},{2,3},{3,2},{4,5},{5,4},{6,7},{7,6},{8,9},{9,8},{10,11... | collective-permute-start | bytes 294920 | tf_op jit(solution)/shard_map/ppermute | solution.py:274
  4.6 6.4 %collective-permute-start.2 = (f32[192,128]{1,0:T(8,128)S(1)}, f32[192,128]{1,0:T(8,128)S(1)}, u32[]{:S(2)}, u32[]{:S(2)}) collective-permute-start(f32[192,128]{1,0:T(8,128)S(1)} %get-tuple-element.22.refs_2_.refs_8_), channel_id=1, source_target_pairs={{0,4},{1,5},{2,6},{3,7},{4,0},{5,1},{6,2},{7,3},{8,12},{9,13},{10,... | collective-permute-start | bytes 294920 | tf_op jit(solution)/shard_map/ppermute | solution.py:274
  6.2 5.8 %collective-permute-start.3 = (f32[192,128]{1,0:T(8,128)S(1)}, f32[192,128]{1,0:T(8,128)S(1)}, u32[]{:S(2)}, u32[]{:S(2)}) collective-permute-start(f32[192,128]{1,0:T(8,128)S(1)} %get-tuple-element.22.refs_2_.refs_8_), channel_id=1, source_target_pairs={{0,6},{1,7},{2,4},{3,5},{4,2},{5,3},{6,0},{7,1},{8,14},{9,15},{10,... | collective-permute-start | bytes 294920 | tf_op jit(solution)/shard_map/ppermute | solution.py:274
  7.9 4.2 %collective-permute-start.1 = (f32[1,192,128]{2,1,0:T(8,128)S(1)}, f32[1,192,128]{2,1,0:T(8,128)S(1)}, u32[]{:S(2)}, u32[]{:S(2)}) collective-permute-start(f32[1,192,128]{2,1,0:T(8,128)S(1)} %pass.2), channel_id=1, source_target_pairs={{0,1},{1,0},{2,3},{3,2},{4,5},{5,4},{6,7},{7,6},{8,9},{9,8},{10,11... | collective-permute-start | bytes 294920 | tf_op jit(solution)/shard_map/ppermute | solution.py:274
  12.0 1.5 %collective-permute-start.5 = (f32[2,192,128]{2,1,0:T(8,128)S(1)}, f32[2,192,128]{2,1,0:T(8,128)S(1)}, u32[]{:S(2)}, u32[]{:S(2)}) collective-permute-start(f32[2,192,128]{2,1,0:T(8,128)S(1)} %pass.3), channel_id=1, source_target_pairs={{0,1},{1,0},{2,3},{3,2},{4,5},{5,4},{6,7},{7,6},{8,9},{9,8},{10,11... | collective-permute-start | bytes 589832 | tf_op jit(solution)/shard_map/ppermute | solution.py:274
  15.2 5.0 %collective-permute-start.6 = (f32[160,128]{1,0:T(8,128)S(1)}, f32[160,128]{1,0:T(8,128)S(1)}, u32[]{:S(2)}, u32[]{:S(2)}) collective-permute-start(f32[160,128]{1,0:T(8,128)S(1)} %get-tuple-element.27.refs_1_), channel_id=1, source_target_pairs={{0,2},{1,3},{2,0},{3,1},{4,6},{5,7},{6,4},{7,5},{8,10},{9,11},{10,... | collective-permute-start | bytes 245768 | tf_op jit(solution)/shard_map/ppermute | solution.py:274
  15.8 5.2 %collective-permute-start.7 = (f32[160,128]{1,0:T(8,128)S(1)}, f32[160,128]{1,0:T(8,128)S(1)}, u32[]{:S(2)}, u32[]{:S(2)}) collective-permute-start(f32[160,128]{1,0:T(8,128)S(1)} %get-tuple-element.27.refs_1_), channel_id=1, source_target_pairs={{0,4},{1,5},{2,6},{3,7},{4,0},{5,1},{6,2},{7,3},{8,12},{9,13},{10,... | collective-permute-start | bytes 245768 | tf_op jit(solution)/shard_map/ppermute | solution.py:274
  17.3 5.3 %collective-permute-start.8 = (f32[160,128]{1,0:T(8,128)S(1)}, f32[160,128]{1,0:T(8,128)S(1)}, u32[]{:S(2)}, u32[]{:S(2)}) collective-permute-start(f32[160,128]{1,0:T(8,128)S(1)} %get-tuple-element.27.refs_1_), channel_id=1, source_target_pairs={{0,6},{1,7},{2,4},{3,5},{4,2},{5,3},{6,0},{7,1},{8,14},{9,15},{10,... | collective-permute-start | bytes 245768 | tf_op jit(solution)/shard_map/ppermute | solution.py:274
  22.8 3.2 %collective-permute-start.11 = (f32[4,128,128]{2,1,0:T(8,128)S(1)}, f32[4,128,128]{2,1,0:T(8,128)S(1)}, u32[]{:S(2)}, u32[]{:S(2)}) collective-permute-start(f32[4,128,128]{2,1,0:T(8,128)S(1)} %get-tuple-element.33), channel_id=1, source_target_pairs={{0,1},{1,0},{2,3},{3,2},{4,5},{5,4},{6,7},{7,6},{8,9},{9,8},{10,11... | collective-permute-start | bytes 786440 | tf_op jit(solution)/shard_map/ppermute | solution.py:274
  22.8 1.6 %collective-permute-start.9 = (f32[40,128]{1,0:T(8,128)S(1)}, f32[40,128]{1,0:T(8,128)S(1)}, u32[]{:S(2)}, u32[]{:S(2)}) collective-permute-start(f32[40,128]{1,0:T(8,128)S(1)} %get-tuple-element.32), channel_id=1, source_target_pairs={{0,1},{1,0},{2,3},{3,2},{4,5},{5,4},{6,7},{7,6},{8,9},{9,8},{10,11... | collective-permute-start | bytes 61448 | tf_op jit(solution)/shard_map/ppermute | solution.py:274
  24.4 3.8 %collective-permute-start.10 = (f32[40,128]{1,0:T(8,128)S(1)}, f32[40,128]{1,0:T(8,128)S(1)}, u32[]{:S(2)}, u32[]{:S(2)}) collective-permute-start(f32[40,128]{1,0:T(8,128)S(1)} %join.2.mine), channel_id=1, source_target_pairs={{0,8},{8,0},{16,24},{24,16},{1,9},{9,1},{17,25},{25,17},{2,10},{10... | collective-permute-start | bytes 61448 | tf_op jit(solution)/shard_map/ppermute | solution.py:274
  28.2 4.7 %collective-permute-start.12 = (f32[40,128]{1,0:T(8,128)S(1)}, f32[40,128]{1,0:T(8,128)S(1)}, u32[]{:S(2)}, u32[]{:S(2)}) collective-permute-start(f32[40,128]{1,0:T(8,128)S(1)} %join.3.refs_3_.refs_0_), channel_id=1, source_target_pairs={{0,16},{8,24},{16,0},{24,8},{1,17},{9,25},{17,1},{25,9},{2,18},{10... | collective-permute-start | bytes 61448 | tf_op jit(solution)/shard_map/ppermute | solution.py:274

commit v5 on v4

--- a/solution.py
+++ b/solution.py
@@ -8,7 +8,7 @@
 from jax.sharding import PartitionSpec as P
 
 LANES = 128
-SLOTS = 8
+CAP_TILES = 4
 WIDE = 256
 NT = (((1,), (1,)), ((), ()))
 F32 = jnp.float32
@@ -17,6 +17,10 @@
 HBM = pl.BlockSpec(memory_space=pltpu.HBM)
 SMEM = pl.BlockSpec(memory_space=pltpu.SMEM)
 PARAMS = pltpu.CompilerParams(vmem_limit_bytes=16 * 1024 * 1024)
+
+
+def up8(rows):
+    return (rows + 7) // 8 * 8
 
 
 def in_hbm(x):
@@ -104,10 +108,63 @@
         copy.wait()
 
 
+def order_kernel(index, coef, _, tile_at, lane_at, coef_out, source_out, left, right, *, owners, span, cap):
+    params, tile_total, _ = coef.shape
+    slots = tile_at.shape[0]
+    ids = index[...]
+    owner = lax.div(ids, span)
+    mask = jnp.concatenate([jnp.where(owner == o, 1.0, 0.0) for o in range(owners)], axis=0)
+    rows = mask.shape[0]
+    half = mask.astype(BF16)
+    row_ids = lax.broadcasted_iota(jnp.int32, (LANES, LANES), 0)
+    col_ids = lax.broadcasted_iota(jnp.int32, (LANES, LANES), 1)
+    upper = jnp.where(row_ids < col_ids, 1.0, 0.0).astype(BF16)
+    inside = jnp.dot(half, upper, preferred_element_type=F32)
+    counts = jnp.dot(half, jnp.ones((LANES, LANES), BF16), preferred_element_type=F32)
+    one = lax.broadcasted_iota(jnp.int32, (rows, rows), 0)
+    two = lax.broadcasted_iota(jnp.int32, (rows, rows), 1)
+    earlier = (lax.div(one, tile_total) == lax.div(two, tile_total)) & (two < one)
+    earlier = jnp.where(earlier, 1.0, 0.0).astype(BF16)
+    rank = inside + jnp.dot(earlier, counts.astype(BF16), preferred_element_type=F32)
+    rank = mask * rank
+    total = rank[:tile_total]
+    for o in range(1, owners):
+        total = total + rank[o * tile_total : (o + 1) * tile_total]
+    slot = owner * cap + total.astype(jnp.int32)
+    high = lax.div(slot, LANES).astype(F32)
+    low = lax.rem(slot, LANES).astype(F32)
+    high_ids = lax.broadcasted_iota(jnp.int32, (slots, LANES), 0).astype(BF16)
+    low_ids = lax.broadcasted_iota(jnp.int32, (LANES, LANES), 0).astype(BF16)
+    lanes = lax.broadcasted_iota(jnp.int32, (slots, LANES), 1).astype(BF16)
+    unit, zero = jnp.ones((), BF16), jnp.zeros((), BF16)
+    for t in range(tile_total):
+        at = slice(t * LANES, (t + 1) * LANES)
+        hit = high_ids == jnp.broadcast_to(high[t : t + 1], (slots, LANES)).astype(BF16)
+        left[:slots, at] = jnp.where(hit, jnp.full((), t + 1, BF16), zero)
+        left[slots:, at] = jnp.where(hit, lanes, zero)
+        right[:, at] = jnp.where(
+            low_ids == jnp.broadcast_to(low[t : t + 1], (LANES, LANES)).astype(BF16), unit, zero
+        )
+    place = lax.dot_general(left[...], right[...], NT, preferred_element_type=F32).astype(jnp.int32)
+    tile, lane = place[:slots] - 1, place[slots:]
+    tile_at[...] = tile
+    lane_at[...] = lane
+    ordered = [jnp.zeros((slots, LANES), F32) for _ in range(params)] + [jnp.full((slots, LANES), -1.0, F32)]
+    for t in range(tile_total):
+        hit = tile == t
+        for k in range(params + 1):
+            row = coef[k, t : t + 1, :] if k < params else ids[t : t + 1].astype(F32)
+            found = jnp.take_along_axis(jnp.broadcast_to(row, (slots, LANES)), lane, axis=1)
+            ordered[k] = jnp.where(hit, found, ordered[k])
+    for k in range(params):
+        coef_out[k] = ordered[k]
+    source_out[...] = ordered[params]
+
+
 def project_kernel(*refs, seg_rows, offsets, late):
-    me, seg_in, count_in, tiles, before, index, coef, weight, *refs = refs
+    me, seg_in, count_in, tiles, before, index, coef, weight, tile_at, lane_at, coef_at, source_at, *refs = refs
     tables, refs = refs[: len(offsets)], refs[len(offsets) :]
-    projected, sent, seg, count, lines, sems = refs
+    projected, sent, seg, count, used, lines, sems = refs
     params, tile_total, width = coef.shape
     folds = tiles.shape[2] // LANES
     base = tables[0].shape[0] - folds * seg_rows
@@ -144,85 +201,84 @@
     value = jnp.where(live, total, 0.0)
     weighted = weight[...] * value
     projected[...] = value
-    for k in range(params):
-        sent[pl.ds(k, tile_total, stride=SLOTS), :] = coef[k] * weighted
-    sent[pl.ds(params, tile_total, stride=SLOTS), :] = ids.astype(F32)
-    names = rows_of([seg[t] for t in range(tile_total)], ids.shape)
-    sent[pl.ds(params + 1, tile_total, stride=SLOTS), :] = names.astype(F32)
-    sent[pl.ds(params + 2, tile_total, stride=SLOTS), :] = value * weighted
+    owners = len(offsets)
+    slots = tile_at.shape[0]
+    depth = sent.shape[0] // owners
+    share = slots // owners
+    tile, lane = tile_at[...], lane_at[...]
+    ordered = jnp.zeros(tile.shape, F32)
+    for t in range(tile_total):
+        row = jnp.broadcast_to(weighted[t : t + 1], tile.shape)
+        ordered = jnp.where(tile == t, jnp.take_along_axis(row, lane, axis=1), ordered)
+    grads_from = up8((params + 1) * share)
+    names_from = grads_from + folds * CAP_TILES
+    curve = jnp.sum(value * weighted, axis=0, keepdims=True)
+    for o in range(owners):
+        used[o] = 0
+        sent[pl.ds(o * depth + grads_from, folds * CAP_TILES), :] = jnp.zeros((folds * CAP_TILES, LANES), F32)
+        sent[pl.ds(o * depth + names_from, CAP_TILES), :] = jnp.full((CAP_TILES, LANES), -1.0, F32)
+        sent[pl.ds(o * depth + names_from + CAP_TILES, 1), :] = curve
+    for k in range(params + 1):
+        values = coef_at[k] * ordered if k < params else source_at[...]
+        for o in range(owners):
+            sent[pl.ds(o * depth + k * share, share), :] = values[o * share : (o + 1) * share]
     columns = weighted.T
-    base = tile_total * SLOTS
     for t in range(tile_total):
+        s = seg[t]
+        owner = lax.div(s, seg_rows)
+        place = used[owner]
+        used[owner] = place + 1
+        start = owner * depth + place
         grad = jnp.sum(tiles[t] * columns[:, t : t + 1], axis=0, keepdims=True)
         for c in range(folds):
-            sent[pl.ds(base + c * tile_total + t, 1), :] = grad[:, c * LANES : (c + 1) * LANES]
-
-
-def attitude_kernel(*refs, params, tile_total, seg_rows, folds):
-    me, *blocks, _, mine, other, packed = refs
-    core = lax.rem(me[0], 2)
-    lane = lax.broadcasted_iota(jnp.int32, (tile_total, LANES), 1)
-    first = (me[0] - core) * seg_rows
-    base = tile_total * SLOTS
-    group = LANES // tile_total
-    sums = [jnp.zeros((2 * seg_rows, LANES), F32) for _ in range(folds)]
-    curve = jnp.zeros((tile_total, LANES), F32)
-    for g in range(0, len(blocks), group):
-        members = blocks[g : g + group]
-        hits = []
-        for got in members:
-            name = got[pl.ds(params + 1, tile_total, stride=SLOTS), :].astype(jnp.int32)
-            hits.append(jnp.where(name - first == lane, 1.0, 0.0))
-            curve = curve + got[pl.ds(params + 2, tile_total, stride=SLOTS), :]
-        pick = jnp.concatenate(hits, axis=0).T[: 2 * seg_rows].astype(BF16)
+            sent[pl.ds(start + grads_from + c * CAP_TILES, 1), :] = grad[:, c * LANES : (c + 1) * LANES]
+        sent[pl.ds(start + names_from, 1), :] = jnp.full((1, LANES), s, jnp.int32).astype(F32)
+
+
+def attitude_kernel(me, got, part, *, owners, grads_from, seg_rows, folds):
+    depth = got.shape[0] // owners
+    names_from = grads_from + folds * CAP_TILES
+    lane = lax.broadcasted_iota(jnp.int32, (owners, LANES), 1)
+    first = me[0] * seg_rows
+    hits, grads = [], [[] for _ in range(folds)]
+    for r in range(CAP_TILES):
+        name = got[pl.ds(names_from + r, owners, stride=depth), :].astype(jnp.int32)
+        hits.append(jnp.where(name - first == lane, 1.0, 0.0))
         for c in range(folds):
-            grads = jnp.concatenate(
-                [got[pl.ds(base + c * tile_total, tile_total), :] for got in members], axis=0
-            )
-            for piece in halves(grads):
-                sums[c] = sums[c] + jnp.dot(pick, piece, preferred_element_type=F32)
-    even = core == 0
+            grads[c].append(got[pl.ds(grads_from + c * CAP_TILES + r, owners, stride=depth), :])
+    pick = jnp.concatenate(hits, axis=0).T[:seg_rows].astype(BF16)
     for c in range(folds):
-        low, high = sums[c][:seg_rows], sums[c][seg_rows:]
-        mine[pl.ds(c * seg_rows, seg_rows), :] = jnp.where(even, low, high)
-        other[pl.ds(c * seg_rows, seg_rows), :] = jnp.where(even, high, low)
+        total = jnp.zeros((seg_rows, LANES), F32)
+        for piece in halves(jnp.concatenate(grads[c], axis=0)):
+            total = total + jnp.dot(pick, piece, preferred_element_type=F32)
+        part[pl.ds(c * seg_rows, seg_rows), :] = total
+    curve = got[pl.ds(names_from + CAP_TILES, owners, stride=depth), :]
     whole = jnp.sum(jnp.sum(curve, axis=0, keepdims=True), axis=1, keepdims=True)
-    whole = jnp.broadcast_to(whole, (8, LANES))
-    mine[pl.ds(folds * seg_rows, 8), :] = whole
-    other[pl.ds(folds * seg_rows, 8), :] = whole
-    for q, got in enumerate(blocks):
-        packed[q] = got[:base, :]
+    part[pl.ds(folds * seg_rows, 8), :] = jnp.broadcast_to(whole, (8, LANES))
 
 
 def join_kernel(mine, other, _, part):
     part[...] = mine[...] + other[...]
 
 
-def source_kernel(*refs, params, tile_total, span, singles, starts, ends, carries, many_range):
-    me, *refs = refs
-    if ends:
-        *refs, token, left, right = refs
-        token[...] = jnp.zeros_like(token)
-        refs += [left, right]
-    left, right = refs[-2:]
-    refs = refs[:-2]
-    if carries:
-        refs[-1][...] = refs[-3][...]
-        refs = refs[:-3] + refs[-2:-1]
-    target = refs.pop()
-    if not starts:
-        acc = refs.pop(0)
+def source_kernel(me, got, held, out, kept, token, left, right, *, owners, share):
+    params, span = out.shape
+    depth = got.shape[0] // owners
+    kept[...] = held[...]
+    token[...] = jnp.zeros_like(token)
     high_total = span // WIDE
-    depth = params * high_total
     high_ids = lax.broadcasted_iota(jnp.int32, (high_total, LANES), 0).astype(BF16)
     low_ids = lax.broadcasted_iota(jnp.int32, (WIDE, LANES), 0).astype(BF16)
     one, zero = jnp.ones((), BF16), jnp.zeros((), BF16)
-
-    def product(tiles_of):
-        for t in range(tile_total):
+    half = params * high_total
+    group = right.shape[1] // LANES
+    places = [o * depth + h for o in range(owners) for h in range(share)]
+    total = jnp.zeros((2 * half, WIDE), F32)
+    for g in range(0, len(places), group):
+        for t, place in enumerate(places[g : g + group]):
             at = slice(t * LANES, (t + 1) * LANES)
-            tile = tiles_of(t)
-            local = tile[params : params + 1].astype(jnp.int32) - me[0] * span
+            rows = [got[place + k * share : place + k * share + 1, :] for k in range(params + 1)]
+            local = rows[params].astype(jnp.int32) - me[0] * span
             high = lax.shift_right_arithmetic(local, 8)
             high = jnp.where((high >= 0) & (high < high_total), high, high_total).astype(F32)
             low = lax.bitwise_and(local, WIDE - 1).astype(F32)
@@ -230,30 +286,14 @@
             right[:, at] = jnp.where(low_ids == low, one, zero)
             hit = high_ids == jnp.broadcast_to(high, (high_total, LANES)).astype(BF16)
             for k in range(params):
-                for p, piece in enumerate(halves(jnp.broadcast_to(tile[k : k + 1], (high_total, LANES)))):
-                    row = p * depth + k * high_total
+                for p, piece in enumerate(halves(jnp.broadcast_to(rows[k], (high_total, LANES)))):
+                    row = p * half + k * high_total
                     left[row : row + high_total, at] = jnp.where(hit, piece, zero)
-        return lax.dot_general(left[...], right[...], NT, preferred_element_type=F32)
-
-    total = jnp.zeros((2 * depth, WIDE), F32) if starts else acc[...]
-    for got in refs[:singles]:
-        total = total + product(lambda t: got[t * SLOTS : (t + 1) * SLOTS, :])
-    if many_range:
-        many = refs[singles]
-
-        def step(d, total):
-            return total + product(lambda t: many[d, t * SLOTS : (t + 1) * SLOTS, :])
-
-        total = lax.fori_loop(*many_range, step, total)
-    if ends:
-        for k in range(params):
-            for h in range(high_total):
-                row = k * high_total + h
-                target[k : k + 1, h * WIDE : (h + 1) * WIDE] = (
-                    total[row : row + 1, :] + total[depth + row : depth + row + 1, :]
-                )
-    else:
-        target[...] = total
+        total = total + lax.dot_general(left[...], right[...], NT, preferred_element_type=F32)
+    for k in range(params):
+        for h in range(high_total):
+            row = k * high_total + h
+            out[k : k + 1, h * WIDE : (h + 1) * WIDE] = total[row : row + 1, :] + total[half + row : half + row + 1, :]
 
 
 def finish_kernel(*refs, seg_rows, folds):
@@ -341,23 +381,47 @@
     first_pair = swapped(passed([2], picked), "tm", tm, 1)
     tables[3] = first_pair[0]
     picked = pick([1, 2], picked)
-    others = swapped(passed(far, picked), "tm", tm, 1)
+    slots = 2 * tile_total
+    places = jax.ShapeDtypeStruct((slots, LANES), jnp.int32)
+    tile_at, lane_at, coef_at, source_at = pl.pallas_call(
+        functools.partial(order_kernel, owners=tm, span=span, cap=slots * LANES // tm),
+        out_shape=(
+            places,
+            places,
+            jax.ShapeDtypeStruct((params, slots, LANES), F32),
+            jax.ShapeDtypeStruct((slots, LANES), F32),
+        ),
+        in_specs=[VMEM] * 3,
+        out_specs=(VMEM,) * 4,
+        scratch_shapes=[
+            pltpu.VMEM((2 * slots, tile_total * LANES), BF16),
+            pltpu.VMEM((LANES, tile_total * LANES), BF16),
+        ],
+        compiler_params=PARAMS,
+        cost_estimate=cost(1.5),
+        name="order",
+    )(index, coef, picked)
+    others = swapped(passed(far, tile_at), "tm", tm, 1)
     for q, offset in enumerate(far):
         tables[offset + 1] = others[q]
     picked = pick([3, *far], picked)
     late = [o + 1 for o in across[1:]]
     offsets = sorted(tables)
+    share = slots // tm
+    grads_from = up8((params + 1) * share)
+    depth = up8(grads_from + (folds + 1) * CAP_TILES + 1)
     projected, sent = pl.pallas_call(
         functools.partial(project_kernel, seg_rows=seg_rows, offsets=offsets, late=late),
         out_shape=(
             jax.ShapeDtypeStruct((tile_total, row_count), F32),
-            jax.ShapeDtypeStruct((tile_total * (SLOTS + folds), LANES), F32),
+            jax.ShapeDtypeStruct((tm * depth, LANES), F32),
         ),
-        in_specs=[SMEM] + [HBM] * 2 + [VMEM] * (5 + tm),
+        in_specs=[SMEM] + [HBM] * 2 + [VMEM] * (9 + tm),
         out_specs=(VMEM, VMEM),
         scratch_shapes=[
             pltpu.SMEM(tile_seg.shape, jnp.int32),
             pltpu.SMEM(tile_count.shape, jnp.int32),
+            pltpu.SMEM((tm,), jnp.int32),
             pltpu.VMEM((tm, folds * seg_rows, LANES), F32),
             pltpu.SemaphoreType.DMA((2,)),
         ],
@@ -371,89 +435,54 @@
         index,
         coef,
         weight,
+        tile_at,
+        lane_at,
+        coef_at,
+        source_at,
         *[tables[o] for o in offsets],
     )
 
-    blocks = [swapped(sent, "tm", tm, offset) for offset in across]
+    got = lax.all_to_all(sent.reshape(tm, depth, LANES), "tm", 0, 0).reshape(tm * depth, LANES)
     part_shape = jax.ShapeDtypeStruct((folds * seg_rows + 8, LANES), F32)
-    depth = params * (span // WIDE)
-    sum_shape = jax.ShapeDtypeStruct((2 * depth, WIDE), F32)
-
-    def source(before, singles, many=None, many_range=(), carried=None, after=None, out=sum_shape):
-        operands = [x for x in (before, *singles, many, after, carried) if x is not None]
-        ends = out is not sum_shape
-        copied = () if carried is None else (jax.ShapeDtypeStruct(carried.shape, F32),)
-        if ends:
-            copied = (jax.ShapeDtypeStruct((8, LANES), F32),)
-        return pl.pallas_call(
-            functools.partial(
-                source_kernel,
-                params=params,
-                tile_total=tile_total,
-                span=span,
-                singles=len(singles),
-                starts=before is None,
-                ends=ends,
-                many_range=many_range,
-                carries=carried is not None,
-            ),
-            out_shape=(out, *copied),
-            in_specs=[SMEM] + [VMEM] * len(operands),
-            out_specs=(VMEM,) * (1 + len(copied)),
-            scratch_shapes=[
-                pltpu.VMEM((2 * depth, tile_total * LANES), BF16),
-                pltpu.VMEM((WIDE, tile_total * LANES), BF16),
-            ],
-            compiler_params=PARAMS,
-            cost_estimate=cost(0.8 * (len(singles) + (len(range(*many_range)) if many_range else 0))),
-            name="source",
-        )(me, *operands)
-
-    def join(one, two, after):
-        return pl.pallas_call(
-            join_kernel,
-            out_shape=part_shape,
-            in_specs=[VMEM] * 3,
-            out_specs=VMEM,
-            compiler_params=PARAMS,
-            name="join",
-        )(one, two, after)
-
-    sums, projected = source(None, [sent], carried=projected)
-    (sums,) = source(sums, blocks[:1])
-    mine, other, packed = pl.pallas_call(
-        functools.partial(
-            attitude_kernel, params=params, tile_total=tile_total, seg_rows=seg_rows, folds=folds
+    part = pl.pallas_call(
+        functools.partial(attitude_kernel, owners=tm, grads_from=grads_from, seg_rows=seg_rows, folds=folds),
+        out_shape=part_shape,
+        in_specs=[SMEM, VMEM],
+        out_specs=VMEM,
+        compiler_params=PARAMS,
+        name="attitude",
+    )(me, got)
+    half = params * (span // WIDE)
+    src_normal, projected, token = pl.pallas_call(
+        functools.partial(source_kernel, owners=tm, share=share),
+        out_shape=(
+            jax.ShapeDtypeStruct((params, span), F32),
+            jax.ShapeDtypeStruct((tile_total, row_count), F32),
+            jax.ShapeDtypeStruct((8, LANES), F32),
         ),
-        out_shape=(
-            part_shape,
-            part_shape,
-            jax.ShapeDtypeStruct((tm // 2, tile_total * SLOTS, LANES), F32),
-        ),
-        in_specs=[SMEM] + [VMEM] * (tm // 2 + 1),
+        in_specs=[SMEM] + [VMEM] * 2,
         out_specs=(VMEM,) * 3,
-        compiler_params=PARAMS,
-        name="attitude",
-    )(me, sent, *blocks, sums)
-    other = swapped(other, "tm", tm, 1)
-    packed = swapped(packed, "tm", tm, 1)
-    (sums,) = source(sums, blocks[1:2])
-    part = join(mine, other, sums)
-    half = tm // 4
-    ranges = [(0, half), (half, tm // 2)]
-    singles = blocks[2:]
+        scratch_shapes=[
+            pltpu.VMEM((2 * half, tile_total * LANES), BF16),
+            pltpu.VMEM((WIDE, tile_total * LANES), BF16),
+        ],
+        compiler_params=PARAMS,
+        cost_estimate=cost(2.0),
+        name="source",
+    )(me, got, projected)
     step = 1
     while step < sky:
         moved = swapped(part, "sky", sky, step)
         step *= 2
         if step < sky:
-            if ranges[1:]:
-                (sums,) = source(sums, singles, packed, ranges.pop(0), after=None)
-                singles = []
-            part = join(part, moved, sums)
-    src_normal, token = source(
-        sums, singles, packed, (ranges[0][0], tm // 2), after=part, out=jax.ShapeDtypeStruct((params, span), F32)
-    )
+            part = pl.pallas_call(
+                join_kernel,
+                out_shape=part_shape,
+                in_specs=[VMEM] * 3,
+                out_specs=VMEM,
+                compiler_params=PARAMS,
+                name="join",
+            )(part, moved, token)
     att_normal, curvature = pl.pallas_call(
         functools.partial(finish_kernel, seg_rows=seg_rows, folds=folds),
         out_shape=(

time: 33.7 us -> 33.3 us (0.988)
  blocking collectives: 0 us -> 8.45 us
  starting transfers between devices: 13.1 us -> 9.07 us
  Pallas kernels: 13.3 us -> 10.3 us
  waiting for transfers between devices: 6.3 us -> 4.54 us
    all_to_all x0 -> x1, blocking collectives: none -> 8.45 us  [per_device(): lax.all_to_all(sent.reshape(tm, depth, LANES), 'tm', 0, 0)]
    ppermute x13 -> x8, starting transfers between devices: 13.1 us -> 9.07 us  [swapped(): return lax.ppermute(x, axis, [(i, i ^ offset) for i in range(size)])]
    pallas_call x8 -> x4, Pallas kernels: 6.54 us -> 3.36 us  [the longest x1 1.87 us: per_device(): pl.pallas_call(functools.partial(source_kernel, owners=tm, share=share),...]
    ppermute x13 -> x8, waiting for transfers between devices: 6.3 us -> 4.54 us  [swapped(): return lax.ppermute(x, axis, [(i, i ^ offset) for i in range(size)])]
  transfers between devices with their start and end apart: 13 -> 8, of which waited for: 9 -> 5; matrix products, arithmetic and copies ran while one was open for 0% -> 0% of each run, Pallas kernels for 29% -> 20%
where the time goes in v5:
time: 33.3 us; the launch traced here: 33.1 us
  Pallas kernels  10.3 us (31%)
  starting transfers between devices  9.07 us (27%)
  blocking collectives  8.45 us (25%)
  waiting for transfers between devices  4.54 us (14%)
  between operations  0.72 us (2%)
    ppermute x8, starting transfers between devices, swapped(): return lax.ppermute(x, axis, [(i, i ^ offset) for i in range(size)])  9.07 us
    all_to_all x1, blocking collectives, per_device(): lax.all_to_all(sent.reshape(tm, depth, LANES), 'tm', 0, 0)  8.45 us
    ppermute x8, waiting for transfers between devices, swapped(): return lax.ppermute(x, axis, [(i, i ^ offset) for i in range(size)])  4.54 us
    pallas_call x2, Pallas kernels, pick(): pl.pallas_call(functools.partial(pick_kernel, params=params, offsets=offs...  1.88 us
    pallas_call x1, Pallas kernels, per_device(): pl.pallas_call(functools.partial(source_kernel, owners=tm, share=share),...  1.87 us
    pallas_call x1, Pallas kernels, per_device(): pl.pallas_call(functools.partial(project_kernel, seg_rows=seg_rows, offse...  1.8 us
    pallas_call x1, Pallas kernels, per_device(): pl.pallas_call(functools.partial(pick_kernel, params=params, offsets=earl...  1.61 us
    pallas_call x1, Pallas kernels, per_device(): pl.pallas_call(functools.partial(order_kernel, owners=tm, span=span, cap=...  1.3 us
  transfers between devices with their start and end apart: 8, of which 5 were waited for; matrix products, arithmetic and copies ran while one was open for 0% of the time, Pallas kernels for 20%

profile of v5, /device:TPU:0, one launch (start us, length us, event | category | flops | bytes accessed | tf_op | source)
XLA Modules:
  0.0 33.1 jit_solution(17252207139800009347)
XLA Ops:
  0.6 1.0 %pack.1 = (f32[192,128]{1,0:T(8,128)S(1)}, s32[16,128]{1,0:T(8,128)S(1)}, f32[5,16,128]{2,1,0:T(8,128)S(1)}, f32[16,128]{1,0:T(8,128)S(1)}) custom-call(f32[5,4096]{1,0:T(8,128)} %source.2, f32[16,256]{1,0:T(8,128)} %attitude.2, s32[16,128]{1,0:T(8,128)} %index.1, f32[5,16,128]{2,1,0:T(8,128)} %coef.1, f32[16,128]{1,0:T(8,128)} %weight.1), custom_call_target="tpu_custom_call" | custom-call | tf_op jit(solution)/shard_map/pack/pallas_call | solution.py:325
  1.6 3.0 %collective-permute-start = (f32[192,128]{1,0:T(8,128)S(1)}, f32[192,128]{1,0:T(8,128)S(1)}, u32[]{:S(2)}, u32[]{:S(2)}) collective-permute-start(f32[192,128]{1,0:T(8,128)S(1)} %get-tuple-element.22.refs_2_.refs_12_), channel_id=1, source_target_pairs={{0,2},{1,3},{2,0},{3,1},{4,6},{5,7},{6,4},{7,5},{8,10},{9,11},{10,... | collective-permute-start | bytes 294920 | tf_op jit(solution)/shard_map/ppermute | solution.py:314
  4.6 0.0 collective-permute-start.4
  4.6 1.5 %collective-permute-start.2 = (f32[192,128]{1,0:T(8,128)S(1)}, f32[192,128]{1,0:T(8,128)S(1)}, u32[]{:S(2)}, u32[]{:S(2)}) collective-permute-start(f32[192,128]{1,0:T(8,128)S(1)} %get-tuple-element.22.refs_2_.refs_12_), channel_id=1, source_target_pairs={{0,4},{1,5},{2,6},{3,7},{4,0},{5,1},{6,2},{7,3},{8,12},{9,13},{10,... | collective-permute-start | bytes 294920 | tf_op jit(solution)/shard_map/ppermute | solution.py:314
  6.2 0.1 collective-permute-start.3
  6.3 1.6 %pick.3 = (f32[80,128]{1,0:T(8,128)S(1)}, f32[16,128,256]{2,1,0:T(8,128)S(1)}) custom-call(s32[1]{0:T(128)} %bitcast.refs_0_.me, s32[16,128]{1,0:T(8,128)S(1)} %get-tuple-element.21.refs_1_.index.refs_5_, f32[192,128]{1,0:T(8,128)S(1)} %get-tuple-element.22.refs_2_.refs_12_, f32[16,128,256]{2,1,0:T(8,128)} %refs_3_.1), custom_call_target="tpu_custom_call" | custom-call | flops 1600000000 | bytes 1 | tf_op jit(solution)/shard_map/pick/pallas_call | solution.py:360
  7.9 0.0 collective-permute-done.refs_0_.refs_3_.refs_14_
  7.9 0.2 collective-permute-start.1
  8.1 0.0 collective-permute-done.4.refs_2_.refs_13_
  8.1 0.8 %pick.4.refs_5_._ = f32[80,128]{1,0:T(8,128)S(1)} custom-call(s32[1]{0:T(128)} %bitcast.refs_0_.me, s32[16,128]{1,0:T(8,128)S(1)} %get-tuple-element.21.refs_1_.index.refs_5_, f32[192,128]{1,0:T(8,128)S(1)} %collective-permute-done.4.refs_2_.refs_13_, f32[192,128]{1,0:T(8,128)S(1)} %collective-permute-done.refs_0_.refs_3_.refs_14_, ...), custom_call_target="tpu_custom_call" | custom-call | flops 800000000 | bytes 1 | tf_op jit(solution)/shard_map/pick/pallas_call | solution.py:349
  8.9 1.3 %order.1 = (s32[32,128]{1,0:T(8,128)S(1)}, s32[32,128]{1,0:T(8,128)S(1)}, f32[5,32,128]{2,1,0:T(8,128)S(1)}, f32[32,128]{1,0:T(8,128)S(1)}) custom-call(s32[16,128]{1,0:T(8,128)S(1)} %get-tuple-element.21.refs_1_.index.refs_5_, f32[5,16,128]{2,1,0:T(8,128)S(1)} %get-tuple-element.25.coef.refs_6_, f32[80,128]{1,0:T(8,128)S(1)} %pick.4.refs_5_._), custom_call_target="tpu_custom_call" | custom-call | flops 1500000000 | bytes 1 | tf_op jit(solution)/shard_map/order/pallas_call | solution.py:386
  10.2 0.8 %collective-permute-done.2.refs_3_.refs_0_.refs_16_ = f32[192,128]{1,0:T(8,128)S(1)} collective-permute-done((f32[192,128]{1,0:T(8,128)S(1)}, f32[192,128]{1,0:T(8,128)S(1)}, u32[]{:S(2)}, u32[]{:S(2)}) %collective-permute-start.2) | collective-permute-done | bytes 98336 | tf_op jit(solution)/shard_map/ppermute | solution.py:314
  11.0 1.0 %collective-permute-done.3.refs_4_.refs_1_.refs_18_ = f32[192,128]{1,0:T(8,128)S(1)} collective-permute-done((f32[192,128]{1,0:T(8,128)S(1)}, f32[192,128]{1,0:T(8,128)S(1)}, u32[]{:S(2)}, u32[]{:S(2)}) %collective-permute-start.3) | collective-permute-done | bytes 98336 | tf_op jit(solution)/shard_map/ppermute | solution.py:314
  12.0 0.1 collective-permute-start.5
  12.1 0.0 collective-permute-done.1
  12.1 1.1 %pick.5.refs_4_ = f32[80,128]{1,0:T(8,128)S(1)} custom-call(s32[1]{0:T(128)} %bitcast.refs_0_.me, s32[16,128]{1,0:T(8,128)S(1)} %get-tuple-element.21.refs_1_.index.refs_5_, f32[192,128]{1,0:T(8,128)S(1)} %bitcast.12, f32[192,128]{1,0:T(8,128)S(1)} %collective-permute-done.2.refs_3_.refs_0_.refs_16_, ...), custom_call_target="tpu_custom_call" | custom-call | flops 1200000000 | bytes 1 | tf_op jit(solution)/shard_map/pick/pallas_call | solution.py:349
  13.2 0.3 collective-permute-done.5
  13.5 1.8 %project.1 = (f32[16,128]{1,0:T(8,128)S(1)}, f32[320,128]{1,0:T(8,128)S(1)}) custom-call(s32[1]{0:T(128)} %bitcast.refs_0_.me, s32[16]{0:T(128)} %refs_1_.1, s32[16]{0:T(128)} %refs_2_.1, f32[16,128,256]{2,1,0:T(8,128)S(1)} %get-tuple-element.23.refs_3_, f32[80,128]{1,0:T(8,128)S(1)} %pick.5.refs_4_, s32[16,128]{1,0:T(8,128)S(1)} %get-tuple-element.21.refs_1_.index.refs_5_, ...), custom_call_target="tpu_custom_call" | custom-call | tf_op jit(solution)/shard_map/project/pallas_call | solution.py:413
  15.3 8.4 %all_to_all.5 = f32[8,40,128]{2,1,0:T(8,128)S(1)} all-to-all(f32[8,40,128]{2,1,0:T(8,128)S(1)} %bitcast.11), channel_id=1, replica_groups=mesh['sky'=4,'tm'=8] {'tm'}, dimensions={0} | all-to-all | bytes 327680 | tf_op jit(solution)/shard_map/all_to_all | solution.py:445
  23.8 0.2 attitude.3.mine
  24.0 1.6 %collective-permute-start.6 = (f32[40,128]{1,0:T(8,128)S(1)}, f32[40,128]{1,0:T(8,128)S(1)}, u32[]{:S(2)}, u32[]{:S(2)}) collective-permute-start(f32[40,128]{1,0:T(8,128)S(1)} %attitude.3.mine), channel_id=1, source_target_pairs={{0,8},{8,0},{16,24},{24,16},{1,9},{9,1},{17,25},{25,17},{2,10},{10... | collective-permute-start | bytes 61448 | tf_op jit(solution)/shard_map/ppermute | solution.py:314
  25.6 1.9 %source.3 = (f32[5,4096]{1,0:T(8,128)}, f32[16,128]{1,0:T(8,128)}, f32[8,128]{1,0:T(8,128)S(1)}) custom-call(s32[1]{0:T(128)} %bitcast.refs_0_.me, f32[320,128]{1,0:T(8,128)S(1)} %bitcast.10, f32[16,128]{1,0:T(8,128)S(1)} %get-tuple-element.32.held), custom_call_target="tpu_custom_call" | custom-call | flops 2000000000 | bytes 1 | tf_op jit(solution)/shard_map/source/pallas_call | solution.py:456
  27.4 0.3 collective-permute-done.6.other
  27.8 2.6 %collective-permute-start.7 = (f32[40,128]{1,0:T(8,128)S(1)}, f32[40,128]{1,0:T(8,128)S(1)}, u32[]{:S(2)}, u32[]{:S(2)}) collective-permute-start(f32[40,128]{1,0:T(8,128)S(1)} %join.1.refs_0_), channel_id=1, source_target_pairs={{0,16},{8,24},{16,0},{24,8},{1,17},{9,25},{17,1},{25,9},{2,18},{10... | collective-permute-start | bytes 61448 | tf_op jit(solution)/shard_map/ppermute | solution.py:314
  30.4 2.1 %collective-permute-done.7.refs_1_ = f32[40,128]{1,0:T(8,128)S(1)} collective-permute-done((f32[40,128]{1,0:T(8,128)S(1)}, f32[40,128]{1,0:T(8,128)S(1)}, u32[]{:S(2)}, u32[]{:S(2)}) %collective-permute-start.7) | collective-permute-done | bytes 20512 | tf_op jit(solution)/shard_map/ppermute | solution.py:314
  32.4 0.6 %finish.1 = (f32[16,256]{1,0:T(8,128)}, f32[1,1]{1,0:T(1,128)}) custom-call(f32[40,128]{1,0:T(8,128)S(1)} %join.1.refs_0_, f32[40,128]{1,0:T(8,128)S(1)} %collective-permute-done.7.refs_1_, f32[8,128]{1,0:T(8,128)S(1)} %get-tuple-element.34._.refs_2_), custom_call_target="tpu_custom_call" | custom-call | tf_op jit(solution)/shard_map/finish/pallas_call | solution.py:486
  (4 shorter events, 0.0 us)
Async XLA Ops:
  1.6 6.3 %collective-permute-start = (f32[192,128]{1,0:T(8,128)S(1)}, f32[192,128]{1,0:T(8,128)S(1)}, u32[]{:S(2)}, u32[]{:S(2)}) collective-permute-start(f32[192,128]{1,0:T(8,128)S(1)} %get-tuple-element.22.refs_2_.refs_12_), channel_id=1, source_target_pairs={{0,2},{1,3},{2,0},{3,1},{4,6},{5,7},{6,4},{7,5},{8,10},{9,11},{10,... | collective-permute-start | bytes 294920 | tf_op jit(solution)/shard_map/ppermute | solution.py:314
  4.6 3.5 %collective-permute-start.4 = (f32[192,128]{1,0:T(8,128)S(1)}, f32[192,128]{1,0:T(8,128)S(1)}, u32[]{:S(2)}, u32[]{:S(2)}) collective-permute-start(f32[192,128]{1,0:T(8,128)S(1)} %get-tuple-element.22.refs_2_.refs_12_), channel_id=1, source_target_pairs={{0,1},{1,0},{2,3},{3,2},{4,5},{5,4},{6,7},{7,6},{8,9},{9,8},{10,11... | collective-permute-start | bytes 294920 | tf_op jit(solution)/shard_map/ppermute | solution.py:314
  4.6 6.4 %collective-permute-start.2 = (f32[192,128]{1,0:T(8,128)S(1)}, f32[192,128]{1,0:T(8,128)S(1)}, u32[]{:S(2)}, u32[]{:S(2)}) collective-permute-start(f32[192,128]{1,0:T(8,128)S(1)} %get-tuple-element.22.refs_2_.refs_12_), channel_id=1, source_target_pairs={{0,4},{1,5},{2,6},{3,7},{4,0},{5,1},{6,2},{7,3},{8,12},{9,13},{10,... | collective-permute-start | bytes 294920 | tf_op jit(solution)/shard_map/ppermute | solution.py:314
  6.2 5.8 %collective-permute-start.3 = (f32[192,128]{1,0:T(8,128)S(1)}, f32[192,128]{1,0:T(8,128)S(1)}, u32[]{:S(2)}, u32[]{:S(2)}) collective-permute-start(f32[192,128]{1,0:T(8,128)S(1)} %get-tuple-element.22.refs_2_.refs_12_), channel_id=1, source_target_pairs={{0,6},{1,7},{2,4},{3,5},{4,2},{5,3},{6,0},{7,1},{8,14},{9,15},{10,... | collective-permute-start | bytes 294920 | tf_op jit(solution)/shard_map/ppermute | solution.py:314
  7.9 4.2 %collective-permute-start.1 = (f32[1,192,128]{2,1,0:T(8,128)S(1)}, f32[1,192,128]{2,1,0:T(8,128)S(1)}, u32[]{:S(2)}, u32[]{:S(2)}) collective-permute-start(f32[1,192,128]{2,1,0:T(8,128)S(1)} %pass.2), channel_id=1, source_target_pairs={{0,1},{1,0},{2,3},{3,2},{4,5},{5,4},{6,7},{7,6},{8,9},{9,8},{10,11... | collective-permute-start | bytes 294920 | tf_op jit(solution)/shard_map/ppermute | solution.py:314
  12.0 1.5 %collective-permute-start.5 = (f32[2,192,128]{2,1,0:T(8,128)S(1)}, f32[2,192,128]{2,1,0:T(8,128)S(1)}, u32[]{:S(2)}, u32[]{:S(2)}) collective-permute-start(f32[2,192,128]{2,1,0:T(8,128)S(1)} %pass.3), channel_id=1, source_target_pairs={{0,1},{1,0},{2,3},{3,2},{4,5},{5,4},{6,7},{7,6},{8,9},{9,8},{10,11... | collective-permute-start | bytes 589832 | tf_op jit(solution)/shard_map/ppermute | solution.py:314
  24.0 3.8 %collective-permute-start.6 = (f32[40,128]{1,0:T(8,128)S(1)}, f32[40,128]{1,0:T(8,128)S(1)}, u32[]{:S(2)}, u32[]{:S(2)}) collective-permute-start(f32[40,128]{1,0:T(8,128)S(1)} %attitude.3.mine), channel_id=1, source_target_pairs={{0,8},{8,0},{16,24},{24,16},{1,9},{9,1},{17,25},{25,17},{2,10},{10... | collective-permute-start | bytes 61448 | tf_op jit(solution)/shard_map/ppermute | solution.py:314
  27.8 4.7 %collective-permute-start.7 = (f32[40,128]{1,0:T(8,128)S(1)}, f32[40,128]{1,0:T(8,128)S(1)}, u32[]{:S(2)}, u32[]{:S(2)}) collective-permute-start(f32[40,128]{1,0:T(8,128)S(1)} %join.1.refs_0_), channel_id=1, source_target_pairs={{0,16},{8,24},{16,0},{24,8},{1,17},{9,25},{17,1},{25,9},{2,18},{10... | collective-permute-start | bytes 61448 | tf_op jit(solution)/shard_map/ppermute | solution.py:314

commit v6 on v5

--- a/solution.py
+++ b/solution.py
@@ -222,14 +222,23 @@
         values = coef_at[k] * ordered if k < params else source_at[...]
         for o in range(owners):
             sent[pl.ds(o * depth + k * share, share), :] = values[o * share : (o + 1) * share]
-    columns = weighted.T
+    pieces = jnp.concatenate(halves(weighted), axis=0).astype(F32)
+    whose = lax.rem(lax.broadcasted_iota(jnp.int32, pieces.shape, 0), tile_total)
+    grads = jnp.zeros((2 * tile_total, tiles.shape[2]), F32)
+    rest = jnp.zeros((tile_total, tiles.shape[2]), F32)
+    for t in range(tile_total):
+        first, second = halves(tiles[t])
+        left = jnp.where(whose == t, pieces, 0.0).astype(BF16)
+        grads = grads + jnp.dot(left, first, preferred_element_type=F32)
+        rest = rest + jnp.dot(left[:tile_total], second, preferred_element_type=F32)
+    grads = grads[:tile_total] + grads[tile_total:] + rest
     for t in range(tile_total):
         s = seg[t]
         owner = lax.div(s, seg_rows)
         place = used[owner]
         used[owner] = place + 1
         start = owner * depth + place
-        grad = jnp.sum(tiles[t] * columns[:, t : t + 1], axis=0, keepdims=True)
+        grad = grads[t : t + 1]
         for c in range(folds):
             sent[pl.ds(start + grads_from + c * CAP_TILES, 1), :] = grad[:, c * LANES : (c + 1) * LANES]
         sent[pl.ds(start + names_from, 1), :] = jnp.full((1, LANES), s, jnp.int32).astype(F32)
@@ -255,10 +264,6 @@
     curve = got[pl.ds(names_from + CAP_TILES, owners, stride=depth), :]
     whole = jnp.sum(jnp.sum(curve, axis=0, keepdims=True), axis=1, keepdims=True)
     part[pl.ds(folds * seg_rows, 8), :] = jnp.broadcast_to(whole, (8, LANES))
-
-
-def join_kernel(mine, other, _, part):
-    part[...] = mine[...] + other[...]
 
 
 def source_kernel(me, got, held, out, kept, token, left, right, *, owners, share):
@@ -470,30 +475,19 @@
         cost_estimate=cost(2.0),
         name="source",
     )(me, got, projected)
-    step = 1
-    while step < sky:
-        moved = swapped(part, "sky", sky, step)
-        step *= 2
-        if step < sky:
-            part = pl.pallas_call(
-                join_kernel,
-                out_shape=part_shape,
-                in_specs=[VMEM] * 3,
-                out_specs=VMEM,
-                compiler_params=PARAMS,
-                name="join",
-            )(part, moved, token)
+    order = [*range(sky // 2, sky), *range(1, sky // 2)]
+    others = [swapped(part, "sky", sky, offset) for offset in order]
     att_normal, curvature = pl.pallas_call(
         functools.partial(finish_kernel, seg_rows=seg_rows, folds=folds),
         out_shape=(
             jax.ShapeDtypeStruct((seg_rows, cols), F32),
             jax.ShapeDtypeStruct((1, 1), F32),
         ),
-        in_specs=[VMEM] * 3,
+        in_specs=[VMEM] * (sky + 1),
         out_specs=(VMEM, SMEM),
         compiler_params=PARAMS,
         name="finish",
-    )(part, moved, token)
+    )(part, *others, token)
     return projected, att_normal, src_normal, curvature.reshape(())
 
 

time: 33.3 us -> 32.8 us (0.985)
    ppermute x8 -> x9, waiting for transfers between devices: 4.54 us -> 4.24 us  [swapped(): return lax.ppermute(x, axis, [(i, i ^ offset) for i in range(size)])]
    ppermute x8 -> x9, starting transfers between devices: 9.07 us -> 9.07 us  [swapped(): return lax.ppermute(x, axis, [(i, i ^ offset) for i in range(size)])]
  transfers between devices with their start and end apart: 8 -> 9, of which waited for: 5 -> 4; matrix products, arithmetic and copies ran while one was open for 0% -> 0% of each run, Pallas kernels for 20% -> 20%
where the time goes in v6:
time: 32.8 us; the launch traced here: 32.6 us
  Pallas kernels  10.1 us (31%)
  starting transfers between devices  9.07 us (28%)
  blocking collectives  8.45 us (26%)
  waiting for transfers between devices  4.24 us (13%)
  between operations  0.72 us (2%)
    ppermute x9, starting transfers between devices, swapped(): return lax.ppermute(x, axis, [(i, i ^ offset) for i in range(size)])  9.07 us
    all_to_all x1, blocking collectives, per_device(): lax.all_to_all(sent.reshape(tm, depth, LANES), 'tm', 0, 0)  8.45 us
    ppermute x9, waiting for transfers between devices, swapped(): return lax.ppermute(x, axis, [(i, i ^ offset) for i in range(size)])  4.24 us
    pallas_call x2, Pallas kernels, pick(): pl.pallas_call(functools.partial(pick_kernel, params=params, offsets=offs...  1.88 us
    pallas_call x1, Pallas kernels, per_device(): pl.pallas_call(functools.partial(source_kernel, owners=tm, share=share),...  1.87 us
    pallas_call x1, Pallas kernels, per_device(): pl.pallas_call(functools.partial(project_kernel, seg_rows=seg_rows, offse...  1.64 us
    pallas_call x1, Pallas kernels, per_device(): pl.pallas_call(functools.partial(pick_kernel, params=params, offsets=earl...  1.61 us
    pallas_call x1, Pallas kernels, per_device(): pl.pallas_call(functools.partial(order_kernel, owners=tm, span=span, cap=...  1.3 us
  transfers between devices with their start and end apart: 9, of which 4 were waited for; matrix products, arithmetic and copies ran while one was open for 0% of the time, Pallas kernels for 20%

profile of v6, /device:TPU:0, one launch (start us, length us, event | category | flops | bytes accessed | tf_op | source)
XLA Modules:
  0.0 32.6 jit_solution(7444187232931029214)
XLA Ops:
  0.6 1.0 %pack.1 = (f32[192,128]{1,0:T(8,128)S(1)}, s32[16,128]{1,0:T(8,128)S(1)}, f32[5,16,128]{2,1,0:T(8,128)S(1)}, f32[16,128]{1,0:T(8,128)S(1)}) custom-call(f32[5,4096]{1,0:T(8,128)} %source.2, f32[16,256]{1,0:T(8,128)} %attitude.2, s32[16,128]{1,0:T(8,128)} %index.1, f32[5,16,128]{2,1,0:T(8,128)} %coef.1, f32[16,128]{1,0:T(8,128)} %weight.1), custom_call_target="tpu_custom_call" | custom-call | tf_op jit(solution)/shard_map/pack/pallas_call | solution.py:330
  1.6 3.0 %collective-permute-start = (f32[192,128]{1,0:T(8,128)S(1)}, f32[192,128]{1,0:T(8,128)S(1)}, u32[]{:S(2)}, u32[]{:S(2)}) collective-permute-start(f32[192,128]{1,0:T(8,128)S(1)} %get-tuple-element.22.refs_2_.refs_12_), channel_id=1, source_target_pairs={{0,2},{1,3},{2,0},{3,1},{4,6},{5,7},{6,4},{7,5},{8,10},{9,11},{10,... | collective-permute-start | bytes 294920 | tf_op jit(solution)/shard_map/ppermute | solution.py:319
  4.6 0.0 collective-permute-start.4
  4.6 1.5 %collective-permute-start.2 = (f32[192,128]{1,0:T(8,128)S(1)}, f32[192,128]{1,0:T(8,128)S(1)}, u32[]{:S(2)}, u32[]{:S(2)}) collective-permute-start(f32[192,128]{1,0:T(8,128)S(1)} %get-tuple-element.22.refs_2_.refs_12_), channel_id=1, source_target_pairs={{0,4},{1,5},{2,6},{3,7},{4,0},{5,1},{6,2},{7,3},{8,12},{9,13},{10,... | collective-permute-start | bytes 294920 | tf_op jit(solution)/shard_map/ppermute | solution.py:319
  6.2 0.1 collective-permute-start.3
  6.3 1.6 %pick.3 = (f32[80,128]{1,0:T(8,128)S(1)}, f32[16,128,256]{2,1,0:T(8,128)S(1)}) custom-call(s32[1]{0:T(128)} %bitcast.refs_0_.me, s32[16,128]{1,0:T(8,128)S(1)} %get-tuple-element.21.refs_1_.index.refs_5_, f32[192,128]{1,0:T(8,128)S(1)} %get-tuple-element.22.refs_2_.refs_12_, f32[16,128,256]{2,1,0:T(8,128)} %refs_3_.1), custom_call_target="tpu_custom_call" | custom-call | flops 1600000000 | bytes 1 | tf_op jit(solution)/shard_map/pick/pallas_call | solution.py:365
  7.9 0.0 collective-permute-done.refs_0_.refs_3_.refs_14_
  7.9 0.2 collective-permute-start.1
  8.1 0.0 collective-permute-done.4.refs_2_.refs_13_
  8.1 0.8 %pick.4.refs_5_._ = f32[80,128]{1,0:T(8,128)S(1)} custom-call(s32[1]{0:T(128)} %bitcast.refs_0_.me, s32[16,128]{1,0:T(8,128)S(1)} %get-tuple-element.21.refs_1_.index.refs_5_, f32[192,128]{1,0:T(8,128)S(1)} %collective-permute-done.4.refs_2_.refs_13_, f32[192,128]{1,0:T(8,128)S(1)} %collective-permute-done.refs_0_.refs_3_.refs_14_, ...), custom_call_target="tpu_custom_call" | custom-call | flops 800000000 | bytes 1 | tf_op jit(solution)/shard_map/pick/pallas_call | solution.py:354
  8.9 1.3 %order.1 = (s32[32,128]{1,0:T(8,128)S(1)}, s32[32,128]{1,0:T(8,128)S(1)}, f32[5,32,128]{2,1,0:T(8,128)S(1)}, f32[32,128]{1,0:T(8,128)S(1)}) custom-call(s32[16,128]{1,0:T(8,128)S(1)} %get-tuple-element.21.refs_1_.index.refs_5_, f32[5,16,128]{2,1,0:T(8,128)S(1)} %get-tuple-element.25.coef.refs_6_, f32[80,128]{1,0:T(8,128)S(1)} %pick.4.refs_5_._), custom_call_target="tpu_custom_call" | custom-call | flops 1500000000 | bytes 1 | tf_op jit(solution)/shard_map/order/pallas_call | solution.py:391
  10.2 0.8 %collective-permute-done.2.refs_3_.refs_0_.refs_16_ = f32[192,128]{1,0:T(8,128)S(1)} collective-permute-done((f32[192,128]{1,0:T(8,128)S(1)}, f32[192,128]{1,0:T(8,128)S(1)}, u32[]{:S(2)}, u32[]{:S(2)}) %collective-permute-start.2) | collective-permute-done | bytes 98336 | tf_op jit(solution)/shard_map/ppermute | solution.py:319
  11.0 1.0 %collective-permute-done.3.refs_4_.refs_1_.refs_18_ = f32[192,128]{1,0:T(8,128)S(1)} collective-permute-done((f32[192,128]{1,0:T(8,128)S(1)}, f32[192,128]{1,0:T(8,128)S(1)}, u32[]{:S(2)}, u32[]{:S(2)}) %collective-permute-start.3) | collective-permute-done | bytes 98336 | tf_op jit(solution)/shard_map/ppermute | solution.py:319
  12.0 0.1 collective-permute-start.5
  12.1 0.0 collective-permute-done.1
  12.1 1.1 %pick.5.refs_4_ = f32[80,128]{1,0:T(8,128)S(1)} custom-call(s32[1]{0:T(128)} %bitcast.refs_0_.me, s32[16,128]{1,0:T(8,128)S(1)} %get-tuple-element.21.refs_1_.index.refs_5_, f32[192,128]{1,0:T(8,128)S(1)} %bitcast.12, f32[192,128]{1,0:T(8,128)S(1)} %collective-permute-done.2.refs_3_.refs_0_.refs_16_, ...), custom_call_target="tpu_custom_call" | custom-call | flops 1200000000 | bytes 1 | tf_op jit(solution)/shard_map/pick/pallas_call | solution.py:354
  13.2 0.3 collective-permute-done.5
  13.5 1.6 %project.1 = (f32[16,128]{1,0:T(8,128)S(1)}, f32[320,128]{1,0:T(8,128)S(1)}) custom-call(s32[1]{0:T(128)} %bitcast.refs_0_.me, s32[16]{0:T(128)} %refs_1_.1, s32[16]{0:T(128)} %refs_2_.1, f32[16,128,256]{2,1,0:T(8,128)S(1)} %get-tuple-element.23.refs_3_, f32[80,128]{1,0:T(8,128)S(1)} %pick.5.refs_4_, s32[16,128]{1,0:T(8,128)S(1)} %get-tuple-element.21.refs_1_.index.refs_5_, ...), custom_call_target="tpu_custom_call" | custom-call | tf_op jit(solution)/shard_map/project/pallas_call | solution.py:418
  15.2 8.4 %all_to_all.5 = f32[8,40,128]{2,1,0:T(8,128)S(1)} all-to-all(f32[8,40,128]{2,1,0:T(8,128)S(1)} %bitcast.11), channel_id=1, replica_groups=mesh['sky'=4,'tm'=8] {'tm'}, dimensions={0} | all-to-all | bytes 327680 | tf_op jit(solution)/shard_map/all_to_all | solution.py:450
  23.6 0.2 attitude.3.refs_0_
  23.8 2.6 %collective-permute-start.6 = (f32[40,128]{1,0:T(8,128)S(1)}, f32[40,128]{1,0:T(8,128)S(1)}, u32[]{:S(2)}, u32[]{:S(2)}) collective-permute-start(f32[40,128]{1,0:T(8,128)S(1)} %attitude.3.refs_0_), channel_id=1, source_target_pairs={{0,16},{8,24},{16,0},{24,8},{1,17},{9,25},{17,1},{25,9},{2,18},{10... | collective-permute-start | bytes 61448 | tf_op jit(solution)/shard_map/ppermute | solution.py:319
  26.4 1.3 %collective-permute-start.7 = (f32[40,128]{1,0:T(8,128)S(1)}, f32[40,128]{1,0:T(8,128)S(1)}, u32[]{:S(2)}, u32[]{:S(2)}) collective-permute-start(f32[40,128]{1,0:T(8,128)S(1)} %attitude.3.refs_0_), channel_id=1, source_target_pairs={{0,24},{8,16},{16,8},{24,0},{1,25},{9,17},{17,9},{25,1},{2,26},{10... | collective-permute-start | bytes 61448 | tf_op jit(solution)/shard_map/ppermute | solution.py:319
  27.8 0.2 collective-permute-start.8
  28.0 1.9 %source.3 = (f32[5,4096]{1,0:T(8,128)}, f32[16,128]{1,0:T(8,128)}, f32[8,128]{1,0:T(8,128)S(1)}) custom-call(s32[1]{0:T(128)} %bitcast.refs_0_.me, f32[320,128]{1,0:T(8,128)S(1)} %bitcast.10, f32[16,128]{1,0:T(8,128)S(1)} %get-tuple-element.32.held), custom_call_target="tpu_custom_call" | custom-call | flops 2000000000 | bytes 1 | tf_op jit(solution)/shard_map/source/pallas_call | solution.py:461
  29.9 0.0 collective-permute-done.6.refs_1_
  29.9 2.1 %collective-permute-done.7.refs_2_ = f32[40,128]{1,0:T(8,128)S(1)} collective-permute-done((f32[40,128]{1,0:T(8,128)S(1)}, f32[40,128]{1,0:T(8,128)S(1)}, u32[]{:S(2)}, u32[]{:S(2)}) %collective-permute-start.7) | collective-permute-done | bytes 20512 | tf_op jit(solution)/shard_map/ppermute | solution.py:319
  32.0 0.0 collective-permute-done.8.refs_3_
  32.0 0.6 %finish.1 = (f32[16,256]{1,0:T(8,128)}, f32[1,1]{1,0:T(1,128)}) custom-call(f32[40,128]{1,0:T(8,128)S(1)} %attitude.3.refs_0_, f32[40,128]{1,0:T(8,128)S(1)} %collective-permute-done.6.refs_1_, f32[40,128]{1,0:T(8,128)S(1)} %collective-permute-done.7.refs_2_, f32[40,128]{1,0:T(8,128)S(1)} %collective-permute-done.8.refs_3_, ...), custom_call_target="tpu_custom_call" | custom-call | tf_op jit(solution)/shard_map/finish/pallas_call | solution.py:480
  (3 shorter events, 0.0 us)
Async XLA Ops:
  1.6 6.3 %collective-permute-start = (f32[192,128]{1,0:T(8,128)S(1)}, f32[192,128]{1,0:T(8,128)S(1)}, u32[]{:S(2)}, u32[]{:S(2)}) collective-permute-start(f32[192,128]{1,0:T(8,128)S(1)} %get-tuple-element.22.refs_2_.refs_12_), channel_id=1, source_target_pairs={{0,2},{1,3},{2,0},{3,1},{4,6},{5,7},{6,4},{7,5},{8,10},{9,11},{10,... | collective-permute-start | bytes 294920 | tf_op jit(solution)/shard_map/ppermute | solution.py:319
  4.6 3.5 %collective-permute-start.4 = (f32[192,128]{1,0:T(8,128)S(1)}, f32[192,128]{1,0:T(8,128)S(1)}, u32[]{:S(2)}, u32[]{:S(2)}) collective-permute-start(f32[192,128]{1,0:T(8,128)S(1)} %get-tuple-element.22.refs_2_.refs_12_), channel_id=1, source_target_pairs={{0,1},{1,0},{2,3},{3,2},{4,5},{5,4},{6,7},{7,6},{8,9},{9,8},{10,11... | collective-permute-start | bytes 294920 | tf_op jit(solution)/shard_map/ppermute | solution.py:319
  4.6 6.4 %collective-permute-start.2 = (f32[192,128]{1,0:T(8,128)S(1)}, f32[192,128]{1,0:T(8,128)S(1)}, u32[]{:S(2)}, u32[]{:S(2)}) collective-permute-start(f32[192,128]{1,0:T(8,128)S(1)} %get-tuple-element.22.refs_2_.refs_12_), channel_id=1, source_target_pairs={{0,4},{1,5},{2,6},{3,7},{4,0},{5,1},{6,2},{7,3},{8,12},{9,13},{10,... | collective-permute-start | bytes 294920 | tf_op jit(solution)/shard_map/ppermute | solution.py:319
  6.2 5.8 %collective-permute-start.3 = (f32[192,128]{1,0:T(8,128)S(1)}, f32[192,128]{1,0:T(8,128)S(1)}, u32[]{:S(2)}, u32[]{:S(2)}) collective-permute-start(f32[192,128]{1,0:T(8,128)S(1)} %get-tuple-element.22.refs_2_.refs_12_), channel_id=1, source_target_pairs={{0,6},{1,7},{2,4},{3,5},{4,2},{5,3},{6,0},{7,1},{8,14},{9,15},{10,... | collective-permute-start | bytes 294920 | tf_op jit(solution)/shard_map/ppermute | solution.py:319
  7.9 4.2 %collective-permute-start.1 = (f32[1,192,128]{2,1,0:T(8,128)S(1)}, f32[1,192,128]{2,1,0:T(8,128)S(1)}, u32[]{:S(2)}, u32[]{:S(2)}) collective-permute-start(f32[1,192,128]{2,1,0:T(8,128)S(1)} %pass.2), channel_id=1, source_target_pairs={{0,1},{1,0},{2,3},{3,2},{4,5},{5,4},{6,7},{7,6},{8,9},{9,8},{10,11... | collective-permute-start | bytes 294920 | tf_op jit(solution)/shard_map/ppermute | solution.py:319
  12.0 1.5 %collective-permute-start.5 = (f32[2,192,128]{2,1,0:T(8,128)S(1)}, f32[2,192,128]{2,1,0:T(8,128)S(1)}, u32[]{:S(2)}, u32[]{:S(2)}) collective-permute-start(f32[2,192,128]{2,1,0:T(8,128)S(1)} %pass.3), channel_id=1, source_target_pairs={{0,1},{1,0},{2,3},{3,2},{4,5},{5,4},{6,7},{7,6},{8,9},{9,8},{10,11... | collective-permute-start | bytes 589832 | tf_op jit(solution)/shard_map/ppermute | solution.py:319
  23.8 6.1 %collective-permute-start.6 = (f32[40,128]{1,0:T(8,128)S(1)}, f32[40,128]{1,0:T(8,128)S(1)}, u32[]{:S(2)}, u32[]{:S(2)}) collective-permute-start(f32[40,128]{1,0:T(8,128)S(1)} %attitude.3.refs_0_), channel_id=1, source_target_pairs={{0,16},{8,24},{16,0},{24,8},{1,17},{9,25},{17,1},{25,9},{2,18},{10... | collective-permute-start | bytes 61448 | tf_op jit(solution)/shard_map/ppermute | solution.py:319
  26.4 5.6 %collective-permute-start.7 = (f32[40,128]{1,0:T(8,128)S(1)}, f32[40,128]{1,0:T(8,128)S(1)}, u32[]{:S(2)}, u32[]{:S(2)}) collective-permute-start(f32[40,128]{1,0:T(8,128)S(1)} %attitude.3.refs_0_), channel_id=1, source_target_pairs={{0,24},{8,16},{16,8},{24,0},{1,25},{9,17},{17,9},{25,1},{2,26},{10... | collective-permute-start | bytes 61448 | tf_op jit(solution)/shard_map/ppermute | solution.py:319
  27.8 4.2 %collective-permute-start.8 = (f32[40,128]{1,0:T(8,128)S(1)}, f32[40,128]{1,0:T(8,128)S(1)}, u32[]{:S(2)}, u32[]{:S(2)}) collective-permute-start(f32[40,128]{1,0:T(8,128)S(1)} %attitude.3.refs_0_), channel_id=1, source_target_pairs={{0,8},{8,0},{16,24},{24,16},{1,9},{9,1},{17,25},{25,17},{2,10},{10... | collective-permute-start | bytes 61448 | tf_op jit(solution)/shard_map/ppermute | solution.py:319

commit v7 on v6

--- a/solution.py
+++ b/solution.py
@@ -32,22 +32,18 @@
     return high, (x - high.astype(F32)).astype(BF16)
 
 
-def rows_of(values, shape):
-    ids = lax.broadcasted_iota(jnp.int32, shape, 0)
-    out = jnp.zeros(shape, jnp.int32)
-    for t, value in enumerate(values):
-        out = jnp.where(ids == t, value, out)
-    return out
-
-
-def pack_kernel(source, attitude, index, coef, weight, directions, index_out, coef_out, weight_out, held, sems):
+def thirds(x):
+    high = x.astype(BF16)
+    return (high, *halves(x - high.astype(F32)))
+
+
+def pack_kernel(source, attitude, *refs):
+    small, (directions, *outs), (held, sems) = refs[:5], refs[5:11], refs[11:]
     params, span = source.shape
     seg_rows, cols = attitude.shape
     copies = [
         pltpu.make_async_copy(source, held, sems.at[0]),
-        pltpu.make_async_copy(index, index_out, sems.at[2]),
-        pltpu.make_async_copy(coef, coef_out, sems.at[3]),
-        pltpu.make_async_copy(weight, weight_out, sems.at[4]),
+        *[pltpu.make_async_copy(x, out, sems.at[1 + q]) for q, (x, out) in enumerate(zip(small, outs))],
     ]
     base = params * (span // LANES)
     for c in range(cols // LANES):
@@ -55,7 +51,7 @@
             pltpu.make_async_copy(
                 attitude.at[:, pl.ds(c * LANES, LANES)],
                 directions.at[pl.ds(base + c * seg_rows, seg_rows), :],
-                sems.at[5 + c],
+                sems.at[6 + c],
             )
         )
     for copy in copies:
@@ -67,19 +63,42 @@
         copy.wait()
 
 
-def gather(owner, table, ids, picked, params):
+def serve(owner, table, block, column, coef, total, share):
+    params = coef.shape[0]
     blocks = (table.shape[0] // (params * 8)) * 8
-    lane = lax.rem(ids, LANES)
-    block = lax.div(ids, LANES) - owner * blocks
-
-    picked = list(picked)
-    for b in range(blocks):
-        hit = block == b
+    parts = 8 // share
+    rows = pl.ds(pl.multiple_of(owner * 8, 8), 8)
+    here, lane = block[rows, :], column[rows, :]
+    part = lax.div(lax.broadcasted_iota(jnp.int32, here.shape, 0), share)
+    picked = [jnp.zeros(here.shape, F32) for _ in range(params)]
+    for b in range(blocks // parts):
+        hit = here == b
         for k in range(params):
-            row = table[b * params + k : b * params + k + 1, :]
-            found = jnp.take_along_axis(jnp.broadcast_to(row, ids.shape), lane, axis=1)
-            picked[k] = jnp.where(hit, found, picked[k])
-    return picked
+            line = None
+            for p in range(parts):
+                at = (p * (blocks // parts) + b) * params + k
+                row = jnp.broadcast_to(table[at : at + 1, :], here.shape)
+                line = row if line is None else jnp.where(part == p, row, line)
+            picked[k] = jnp.where(hit, jnp.take_along_axis(line, lane, axis=1), picked[k])
+    terms = jnp.zeros(here.shape, F32)
+    for k in range(params):
+        terms = terms + coef[k, rows, :] * picked[k]
+    total[rows, :] = terms
+
+
+def own_kernel(me, table, block, column, coef, tiles_in, total, tiles, sem, *, share):
+    copy = pltpu.make_async_copy(tiles_in, tiles, sem)
+    copy.start()
+    total[...] = jnp.zeros_like(total)
+    serve(me[0], table, block, column, coef, total, share)
+    copy.wait()
+
+
+def pick_kernel(*refs, offsets, share):
+    me, *tables, block, column, coef, before, total = refs
+    total[...] = before[...]
+    for offset, table in zip(offsets, tables):
+        serve(lax.bitwise_xor(me[0], offset), table, block, column, coef, total, share)
 
 
 def pass_kernel(*refs, count):
@@ -87,28 +106,8 @@
         refs[-1][q] = refs[q][...]
 
 
-def pick_kernel(*refs, params, offsets, first):
-    me, index, *refs = refs
-    ids = index[...]
-    rows = ids.shape[0]
-    tables, refs = refs[: len(offsets)], refs[len(offsets) :]
-    if first:
-        tiles_in, out, tiles, sem = refs
-        copy = pltpu.make_async_copy(tiles_in, tiles, sem)
-        copy.start()
-        picked = [jnp.zeros(ids.shape, F32) for _ in range(params)]
-    else:
-        before, out = refs
-        picked = [before[k * rows : (k + 1) * rows, :] for k in range(params)]
-    for offset, table in zip(offsets, tables):
-        picked = gather(lax.bitwise_xor(me[0], offset), table, ids, picked, params)
-    for k in range(params):
-        out[k * rows : (k + 1) * rows, :] = picked[k]
-    if first:
-        copy.wait()
-
-
-def order_kernel(index, coef, _, tile_at, lane_at, coef_out, source_out, left, right, *, owners, span, cap):
+def order_kernel(me, seg, count, index, coef, *refs, owners, span, cap, seg_rows):
+    tile_at, lane_at, coef_out, source_out, block, column, coef_by, row_at, rank_at, live, aim, fill, names, left, right = refs
     params, tile_total, _ = coef.shape
     slots = tile_at.shape[0]
     ids = index[...]
@@ -130,7 +129,10 @@
     total = rank[:tile_total]
     for o in range(1, owners):
         total = total + rank[o * tile_total : (o + 1) * tile_total]
-    slot = owner * cap + total.astype(jnp.int32)
+    place = total.astype(jnp.int32)
+    row_at[...] = owner * 8 + lax.div(place, LANES)
+    rank_at[...] = lax.rem(place, LANES)
+    slot = owner * cap + place
     high = lax.div(slot, LANES).astype(F32)
     low = lax.rem(slot, LANES).astype(F32)
     high_ids = lax.broadcasted_iota(jnp.int32, (slots, LANES), 0).astype(BF16)
@@ -159,52 +161,90 @@
     for k in range(params):
         coef_out[k] = ordered[k]
     source_out[...] = ordered[params]
+    source = ordered[params].astype(jnp.int32)
+    blocks, share = span // LANES, slots // owners
+    parts = 8 // share
+    within = jnp.where(source < 0, -blocks, lax.div(lax.rem(source, span), LANES))
+    across = jnp.where(source < 0, 0, lax.rem(source, LANES))
+    for o in range(owners):
+        rows, mine = slice(o * 8, (o + 1) * 8), slice(o * share, (o + 1) * share)
+        block[rows, :] = jnp.concatenate([within[mine] - p * (blocks // parts) for p in range(parts)], axis=0)
+        column[rows, :] = jnp.concatenate([across[mine]] * parts, axis=0)
+        for k in range(params):
+            coef_by[k, rows, :] = jnp.concatenate([ordered[k][mine]] * parts, axis=0)
+    square = (tile_total, tile_total)
+    one = lax.broadcasted_iota(jnp.int32, square, 0)
+    two = lax.broadcasted_iota(jnp.int32, square, 1)
+
+    def down_of(row):
+        return jnp.sum(jnp.where(one == two, jnp.broadcast_to(row, square), 0), axis=1, keepdims=True)
+
+    along, down = seg[...], down_of(seg[...])
+    owner_along, owner_down = lax.div(along, seg_rows), lax.div(down, seg_rows)
+    live[...] = jnp.where(
+        lax.broadcasted_iota(jnp.int32, ids.shape, 1) < jnp.broadcast_to(down_of(count[...]), ids.shape), 1.0, 0.0
+    )
+    line = lax.bitwise_xor(owner_down, me[0]) * seg_rows + lax.rem(down, seg_rows)
+    aim[...] = jnp.where(
+        lax.broadcasted_iota(jnp.int32, aim.shape, 1) == jnp.broadcast_to(line, aim.shape), 1.0, 0.0
+    )
+    same = jnp.broadcast_to(owner_down, square) == jnp.broadcast_to(owner_along, square)
+    ranks = jnp.sum(jnp.where(same & (one < two), 1, 0), axis=0, keepdims=True)
+    place = jnp.broadcast_to(owner_along * CAP_TILES + ranks, fill.shape)
+    filled = lax.broadcasted_iota(jnp.int32, fill.shape, 0) == place
+    fill[...] = jnp.where(filled, 1.0, 0.0)
+    named = jnp.sum(jnp.where(filled, jnp.broadcast_to(along + 1, fill.shape), 0), axis=1, keepdims=True) - 1
+    names[...] = jnp.broadcast_to(named, names.shape).astype(F32)
 
 
 def project_kernel(*refs, seg_rows, offsets, late):
-    me, seg_in, count_in, tiles, before, index, coef, weight, tile_at, lane_at, coef_at, source_at, *refs = refs
+    me, tiles, before, weight, tile_at, lane_at, coef_at, source_at, *refs = refs
+    block, column, coef_by, row_at, rank_at, live, aim, fill, names, *refs = refs
     tables, refs = refs[: len(offsets)], refs[len(offsets) :]
-    projected, sent, seg, count, used, lines, sems = refs
-    params, tile_total, width = coef.shape
+    projected, sent, lines, served = refs
+    params, tile_total, width = coef_at.shape[0], *weight.shape
+    share = tile_at.shape[0] // len(offsets)
     folds = tiles.shape[2] // LANES
     base = tables[0].shape[0] - folds * seg_rows
-    copies = [
-        pltpu.make_async_copy(seg_in, seg, sems.at[0]),
-        pltpu.make_async_copy(count_in, count, sems.at[1]),
-    ]
-    for copy in copies:
-        copy.start()
-    ids = index[...]
-    picked = [before[k * tile_total : (k + 1) * tile_total, :] for k in range(params)]
+    served[...] = before[...]
     for offset, table in zip(offsets, tables):
-        lines[offset] = table[base:, :]
+        for c in range(folds):
+            lines[offset * seg_rows : (offset + 1) * seg_rows, c * LANES : (c + 1) * LANES] = table[
+                base + c * seg_rows : base + (c + 1) * seg_rows, :
+            ]
         if offset in late:
-            picked = gather(lax.bitwise_xor(me[0], offset), table, ids, picked, params)
-    for copy in copies:
-        copy.wait()
-    row_ids = lax.broadcasted_iota(jnp.int32, ids.shape, 0)
-    total = jnp.zeros(ids.shape, F32)
+            serve(lax.bitwise_xor(me[0], offset), table, block, column, coef_by, served, share)
+    shape = weight.shape
+    row, rank = row_at[...], rank_at[...]
+    total = jnp.zeros(shape, F32)
+    for o in range(len(offsets)):
+        for h in range(share):
+            line = served[o * 8 + h : o * 8 + h + 1, :]
+            for p in range(1, 8 // share):
+                at = o * 8 + p * share + h
+                line = line + served[at : at + 1, :]
+            found = jnp.take_along_axis(jnp.broadcast_to(line, shape), rank, axis=1)
+            total = jnp.where(row == o * 8 + h, found, total)
+    hit = aim[...].astype(BF16)
+    directions = jnp.zeros((tile_total, folds * LANES), F32)
+    for piece in thirds(lines[...]):
+        directions = directions + jnp.dot(hit, piece, preferred_element_type=F32)
+    row_ids = lax.broadcasted_iota(jnp.int32, shape, 0)
+    tile_part = jnp.zeros(shape, F32)
     for t in range(tile_total):
-        s = seg[t]
-        place, local = lax.bitwise_xor(lax.div(s, seg_rows), me[0]), lax.rem(s, seg_rows)
         folded = None
         for c in range(folds):
-            direction = lines[place, pl.ds(c * seg_rows + local, 1), :]
-            product = tiles[t, :, c * LANES : (c + 1) * LANES] * direction
+            part = slice(c * LANES, (c + 1) * LANES)
+            product = tiles[t, :, part] * directions[t : t + 1, part]
             folded = product if folded is None else folded + product
-        total = jnp.where(row_ids == t, jnp.sum(folded.T, axis=0, keepdims=True), total)
-    for k in range(params):
-        total = total + coef[k] * picked[k]
-    live = lax.broadcasted_iota(jnp.int32, ids.shape, 1) < rows_of(
-        [count[t] for t in range(tile_total)], ids.shape
-    )
-    value = jnp.where(live, total, 0.0)
+        tile_part = jnp.where(row_ids == t, jnp.sum(folded.T, axis=0, keepdims=True), tile_part)
+    total = total + tile_part
+    value = jnp.where(live[...] > 0.5, total, 0.0)
     weighted = weight[...] * value
     projected[...] = value
     owners = len(offsets)
     slots = tile_at.shape[0]
     depth = sent.shape[0] // owners
-    share = slots // owners
     tile, lane = tile_at[...], lane_at[...]
     ordered = jnp.zeros(tile.shape, F32)
     for t in range(tile_total):
@@ -213,11 +253,6 @@
     grads_from = up8((params + 1) * share)
     names_from = grads_from + folds * CAP_TILES
     curve = jnp.sum(value * weighted, axis=0, keepdims=True)
-    for o in range(owners):
-        used[o] = 0
-        sent[pl.ds(o * depth + grads_from, folds * CAP_TILES), :] = jnp.zeros((folds * CAP_TILES, LANES), F32)
-        sent[pl.ds(o * depth + names_from, CAP_TILES), :] = jnp.full((CAP_TILES, LANES), -1.0, F32)
-        sent[pl.ds(o * depth + names_from + CAP_TILES, 1), :] = curve
     for k in range(params + 1):
         values = coef_at[k] * ordered if k < params else source_at[...]
         for o in range(owners):
@@ -232,16 +267,16 @@
         grads = grads + jnp.dot(left, first, preferred_element_type=F32)
         rest = rest + jnp.dot(left[:tile_total], second, preferred_element_type=F32)
     grads = grads[:tile_total] + grads[tile_total:] + rest
-    for t in range(tile_total):
-        s = seg[t]
-        owner = lax.div(s, seg_rows)
-        place = used[owner]
-        used[owner] = place + 1
-        start = owner * depth + place
-        grad = grads[t : t + 1]
+    place = fill[...].astype(BF16)
+    placed = jnp.zeros((fill.shape[0], folds * LANES), F32)
+    for piece in halves(grads):
+        placed = placed + jnp.dot(place, piece, preferred_element_type=F32)
+    for o in range(owners):
+        rows = slice(o * CAP_TILES, (o + 1) * CAP_TILES)
         for c in range(folds):
-            sent[pl.ds(start + grads_from + c * CAP_TILES, 1), :] = grad[:, c * LANES : (c + 1) * LANES]
-        sent[pl.ds(start + names_from, 1), :] = jnp.full((1, LANES), s, jnp.int32).astype(F32)
+            sent[pl.ds(o * depth + grads_from + c * CAP_TILES, CAP_TILES), :] = placed[rows, c * LANES : (c + 1) * LANES]
+        sent[pl.ds(o * depth + names_from, CAP_TILES), :] = names[rows, :]
+        sent[pl.ds(o * depth + names_from + CAP_TILES, 1), :] = curve
 
 
 def attitude_kernel(me, got, part, *, owners, grads_from, seg_rows, folds):
@@ -324,54 +359,31 @@
     params, span = src_dir.shape
     seg_rows = att_dir.shape[0]
     folds = cols // LANES
-    across = range(2, tm, 2)
+    across = range(3, tm, 2)
     me = lax.axis_index("tm").astype(jnp.int32).reshape(1)
 
-    directions, index, coef, weight = pl.pallas_call(
+    directions, index, coef, weight, seg, count = pl.pallas_call(
         pack_kernel,
         out_shape=(
             jax.ShapeDtypeStruct((params * (span // LANES) + folds * seg_rows, LANES), F32),
             jax.ShapeDtypeStruct(src_index.shape, src_index.dtype),
             jax.ShapeDtypeStruct(src_coef.shape, F32),
             jax.ShapeDtypeStruct(obs_weight.shape, F32),
+            jax.ShapeDtypeStruct((1, tile_total), jnp.int32),
+            jax.ShapeDtypeStruct((1, tile_total), jnp.int32),
         ),
-        in_specs=[HBM] * 5,
-        out_specs=(VMEM,) * 4,
-        scratch_shapes=[pltpu.VMEM((params, span), F32), pltpu.SemaphoreType.DMA((5 + folds,))],
+        in_specs=[HBM] * 7,
+        out_specs=(VMEM,) * 6,
+        scratch_shapes=[pltpu.VMEM((params, span), F32), pltpu.SemaphoreType.DMA((6 + folds,))],
         compiler_params=PARAMS,
         name="pack",
-    )(*map(in_hbm, (src_dir, att_dir, src_index, src_coef, obs_weight)))
+    )(*map(in_hbm, (src_dir, att_dir, src_index, src_coef, obs_weight, *(x.reshape(1, -1) for x in (tile_seg, tile_count)))))
 
     far = list(across[1:])
     tables = {0: directions}
     for offset in across:
         tables[offset] = swapped(directions, "tm", tm, offset)
     tables[1] = swapped(directions, "tm", tm, 1)
-
-    picked_shape = jax.ShapeDtypeStruct((params * tile_total, row_count), F32)
-
-    def pick(offsets, before):
-        return pl.pallas_call(
-            functools.partial(pick_kernel, params=params, offsets=offsets, first=False),
-            out_shape=picked_shape,
-            in_specs=[SMEM] + [VMEM] * (len(offsets) + 2),
-            out_specs=VMEM,
-            compiler_params=PARAMS,
-            cost_estimate=cost(0.4 * len(offsets)),
-            name="pick",
-        )(me, index, *[tables[o] for o in offsets], before)
-
-    early = [0]
-    picked, tiles_held = pl.pallas_call(
-        functools.partial(pick_kernel, params=params, offsets=early, first=True),
-        out_shape=(picked_shape, jax.ShapeDtypeStruct(tiles.shape, F32)),
-        in_specs=[SMEM] + [VMEM] * (len(early) + 1) + [HBM],
-        out_specs=(VMEM, VMEM),
-        scratch_shapes=[pltpu.SemaphoreType.DMA],
-        compiler_params=PARAMS,
-        cost_estimate=cost(1.6),
-        name="pick",
-    )(me, index, *[tables[o] for o in early], in_hbm(tiles))
 
     def passed(offsets, after):
         return pl.pallas_call(
@@ -383,21 +395,30 @@
             name="pass",
         )(*[tables[o] for o in offsets], after)
 
-    first_pair = swapped(passed([2], picked), "tm", tm, 1)
-    tables[3] = first_pair[0]
-    picked = pick([1, 2], picked)
     slots = 2 * tile_total
+    share = slots // tm
     places = jax.ShapeDtypeStruct((slots, LANES), jnp.int32)
-    tile_at, lane_at, coef_at, source_at = pl.pallas_call(
-        functools.partial(order_kernel, owners=tm, span=span, cap=slots * LANES // tm),
+    by_owner = jax.ShapeDtypeStruct((tm * 8, LANES), jnp.int32)
+    by_tile = jax.ShapeDtypeStruct(src_index.shape, jnp.int32)
+    tile_at, lane_at, coef_at, source_at, block, column, coef_by, row_at, rank_at, *extra = pl.pallas_call(
+        functools.partial(order_kernel, owners=tm, span=span, cap=share * LANES, seg_rows=seg_rows),
         out_shape=(
             places,
             places,
             jax.ShapeDtypeStruct((params, slots, LANES), F32),
             jax.ShapeDtypeStruct((slots, LANES), F32),
+            by_owner,
+            by_owner,
+            jax.ShapeDtypeStruct((params, tm * 8, LANES), F32),
+            by_tile,
+            by_tile,
+            jax.ShapeDtypeStruct(src_index.shape, F32),
+            jax.ShapeDtypeStruct((tile_total, tm * seg_rows), F32),
+            jax.ShapeDtypeStruct((tm * CAP_TILES, tile_total), F32),
+            jax.ShapeDtypeStruct((tm * CAP_TILES, LANES), F32),
         ),
-        in_specs=[VMEM] * 3,
-        out_specs=(VMEM,) * 4,
+        in_specs=[SMEM] + [VMEM] * 4,
+        out_specs=(VMEM,) * 13,
         scratch_shapes=[
             pltpu.VMEM((2 * slots, tile_total * LANES), BF16),
             pltpu.VMEM((LANES, tile_total * LANES), BF16),
@@ -405,14 +426,39 @@
         compiler_params=PARAMS,
         cost_estimate=cost(1.5),
         name="order",
-    )(index, coef, picked)
-    others = swapped(passed(far, tile_at), "tm", tm, 1)
+    )(me, seg, count, index, coef)
+    picked_shape = jax.ShapeDtypeStruct((tm * 8, LANES), F32)
+    picked, tiles_held = pl.pallas_call(
+        functools.partial(own_kernel, share=share),
+        out_shape=(picked_shape, jax.ShapeDtypeStruct(tiles.shape, F32)),
+        in_specs=[SMEM] + [VMEM] * 4 + [HBM],
+        out_specs=(VMEM, VMEM),
+        scratch_shapes=[pltpu.SemaphoreType.DMA],
+        compiler_params=PARAMS,
+        cost_estimate=cost(1.6),
+        name="own",
+    )(me, directions, block, column, coef_by, in_hbm(tiles))
+
+    def pick(offsets, before):
+        return pl.pallas_call(
+            functools.partial(pick_kernel, offsets=offsets, share=share),
+            out_shape=picked_shape,
+            in_specs=[SMEM] + [VMEM] * (len(offsets) + 4),
+            out_specs=VMEM,
+            compiler_params=PARAMS,
+            cost_estimate=cost(0.4 * len(offsets)),
+            name="pick",
+        )(me, *[tables[o] for o in offsets], block, column, coef_by, before)
+
+    first_pair = swapped(passed([3], picked), "tm", tm, 1)
+    tables[2] = first_pair[0]
+    picked = pick([1, 3], picked)
+    others = swapped(passed(far, picked), "tm", tm, 1)
     for q, offset in enumerate(far):
-        tables[offset + 1] = others[q]
-    picked = pick([3, *far], picked)
-    late = [o + 1 for o in across[1:]]
+        tables[offset - 1] = others[q]
+    picked = pick([2, *far], picked)
+    late = [o - 1 for o in across[1:]]
     offsets = sorted(tables)
-    share = slots // tm
     grads_from = up8((params + 1) * share)
     depth = up8(grads_from + (folds + 1) * CAP_TILES + 1)
     projected, sent = pl.pallas_call(
@@ -421,29 +467,29 @@
             jax.ShapeDtypeStruct((tile_total, row_count), F32),
             jax.ShapeDtypeStruct((tm * depth, LANES), F32),
         ),
-        in_specs=[SMEM] + [HBM] * 2 + [VMEM] * (9 + tm),
+        in_specs=[SMEM] + [VMEM] * (16 + tm),
         out_specs=(VMEM, VMEM),
         scratch_shapes=[
-            pltpu.SMEM(tile_seg.shape, jnp.int32),
-            pltpu.SMEM(tile_count.shape, jnp.int32),
-            pltpu.SMEM((tm,), jnp.int32),
-            pltpu.VMEM((tm, folds * seg_rows, LANES), F32),
-            pltpu.SemaphoreType.DMA((2,)),
+            pltpu.VMEM((tm * seg_rows, folds * LANES), F32),
+            pltpu.VMEM((tm * 8, LANES), F32),
         ],
         compiler_params=PARAMS,
         name="project",
     )(
         me,
-        *map(in_hbm, (tile_seg, tile_count)),
         tiles_held,
         picked,
-        index,
-        coef,
         weight,
         tile_at,
         lane_at,
         coef_at,
         source_at,
+        block,
+        column,
+        coef_by,
+        row_at,
+        rank_at,
+        *extra,
         *[tables[o] for o in offsets],
     )
 

time: 32.8 us -> 32.5 us (level)
  Pallas kernels: 10.1 us -> 8.73 us
  starting transfers between devices: 9.07 us -> 9.57 us
  blocking collectives: 8.45 us -> 8.85 us
    pallas_call x3, Pallas kernels: 3.48 us -> 2.2 us  [the longest x1 1.62 us: per_device(): pl.pallas_call(functools.partial(own_kernel, share=share), out_shape=(pic...]
    ppermute x9, starting transfers between devices: 9.07 us -> 9.57 us  [swapped(): return lax.ppermute(x, axis, [(i, i ^ offset) for i in range(size)])]
    all_to_all x1, blocking collectives: 8.45 us -> 8.85 us  [per_device(): lax.all_to_all(sent.reshape(tm, depth, LANES), 'tm', 0, 0)]
  transfers between devices with their start and end apart: 9 -> 9, of which waited for: 4 -> 4; matrix products, arithmetic and copies ran while one was open for 0% -> 0% of each run, Pallas kernels for 20% -> 17%
where the time goes in v7:
time: 32.5 us; the launch traced here: 32.3 us
  starting transfers between devices  9.57 us (29%)
  blocking collectives  8.85 us (27%)
  Pallas kernels  8.73 us (27%)
  waiting for transfers between devices  4.46 us (14%)
  between operations  0.69 us (2%)
    ppermute x9, starting transfers between devices, swapped(): return lax.ppermute(x, axis, [(i, i ^ offset) for i in range(size)])  9.57 us
    all_to_all x1, blocking collectives, per_device(): lax.all_to_all(sent.reshape(tm, depth, LANES), 'tm', 0, 0)  8.85 us
    ppermute x9, waiting for transfers between devices, swapped(): return lax.ppermute(x, axis, [(i, i ^ offset) for i in range(size)])  4.46 us
    pallas_call x1, Pallas kernels, per_device(): pl.pallas_call(functools.partial(source_kernel, owners=tm, share=share),...  1.87 us
    pallas_call x1, Pallas kernels, per_device(): pl.pallas_call(functools.partial(own_kernel, share=share), out_shape=(pic...  1.62 us
    pallas_call x1, Pallas kernels, per_device(): pl.pallas_call(functools.partial(project_kernel, seg_rows=seg_rows, offse...  1.51 us
    pallas_call x1, Pallas kernels, per_device(): pl.pallas_call(functools.partial(order_kernel, owners=tm, span=span, cap=...  1.31 us
    pallas_call x1, Pallas kernels, per_device(): pl.pallas_call(pack_kernel, out_shape=(jax.ShapeDtypeStruct((params * (sp...  1 us
  transfers between devices with their start and end apart: 9, of which 4 were waited for; matrix products, arithmetic and copies ran while one was open for 0% of the time, Pallas kernels for 17%

profile of v7, /device:TPU:0, one launch (start us, length us, event | category | flops | bytes accessed | tf_op | source)
XLA Modules:
  0.0 32.3 jit_solution(995456600248764942)
XLA Ops:
  0.6 1.0 %pack.1 = (f32[192,128]{1,0:T(8,128)S(1)}, s32[16,128]{1,0:T(8,128)S(1)}, f32[5,16,128]{2,1,0:T(8,128)S(1)}, f32[16,128]{1,0:T(8,128)S(1)}, s32[1,16]{1,0:T(1,128)S(1)}, /*index=5*/s32[1,16]{1,0:T(1,128)S(1)}) custom-call(f32[5,4096]{1,0:T(8,128)} %source.2, f32[16,256]{1,0:T(8,128)} %attitude.2, s32[16,128]{1,0:T(8,128)} %refs_0_.1, f32[5,16,128]{2,1,0:T(8,128)} %refs_1_.1, ...), custom_call_target="tpu_custom_call" | custom-call | tf_op jit(solution)/shard_map/pack/pallas_call | solution.py:365
  1.6 2.4 %collective-permute-start = (f32[192,128]{1,0:T(8,128)S(1)}, f32[192,128]{1,0:T(8,128)S(1)}, u32[]{:S(2)}, u32[]{:S(2)}) collective-permute-start(f32[192,128]{1,0:T(8,128)S(1)} %get-tuple-element.32.table.refs_17_), channel_id=1, source_target_pairs={{0,3},{1,2},{2,1},{3,0},{4,7},{5,6},{6,5},{7,4},{8,11},{9,10},{10,... | collective-permute-start | bytes 294920 | tf_op jit(solution)/shard_map/ppermute | solution.py:354
  4.1 0.7 %collective-permute-start.4 = (f32[192,128]{1,0:T(8,128)S(1)}, f32[192,128]{1,0:T(8,128)S(1)}, u32[]{:S(2)}, u32[]{:S(2)}) collective-permute-start(f32[192,128]{1,0:T(8,128)S(1)} %get-tuple-element.32.table.refs_17_), channel_id=1, source_target_pairs={{0,1},{1,0},{2,3},{3,2},{4,5},{5,4},{6,7},{7,6},{8,9},{9,8},{10,11... | collective-permute-start | bytes 294920 | tf_op jit(solution)/shard_map/ppermute | solution.py:354
  4.8 1.1 %collective-permute-start.2 = (f32[192,128]{1,0:T(8,128)S(1)}, f32[192,128]{1,0:T(8,128)S(1)}, u32[]{:S(2)}, u32[]{:S(2)}) collective-permute-start(f32[192,128]{1,0:T(8,128)S(1)} %get-tuple-element.32.table.refs_17_), channel_id=1, source_target_pairs={{0,5},{1,4},{2,7},{3,6},{4,1},{5,0},{6,3},{7,2},{8,13},{9,12},{10,... | collective-permute-start | bytes 294920 | tf_op jit(solution)/shard_map/ppermute | solution.py:354
  5.9 0.1 collective-permute-start.3
  6.0 1.3 %order.1 = (s32[32,128]{1,0:T(8,128)S(1)}, s32[32,128]{1,0:T(8,128)S(1)}, f32[5,32,128]{2,1,0:T(8,128)S(1)}, f32[32,128]{1,0:T(8,128)S(1)}, s32[64,128]{1,0:T(8,...) custom-call(s32[1]{0:T(128)} %bitcast.me.refs_0_, ...), custom_call_target="tpu_custom_call" | custom-call | flops 1500000000 | bytes 1 | tf_op jit(solution)/shard_map/order/pallas_call | solution.py:403
  7.3 1.6 %own.1 = (f32[64,128]{1,0:T(8,128)S(1)}, f32[16,128,256]{2,1,0:T(8,128)S(1)}) custom-call(s32[1]{0:T(128)} %bitcast.me.refs_0_, f32[192,128]{1,0:T(8,128)S(1)} %get-tuple-element.32.table.refs_17_, s32[64,128]{1,0:T(8,128)S(1)} %get-tuple-element.37.block.refs_3_.refs_4_.refs_8_, s32[64,128]{1,0:T(8,128)S(1)} %get-tuple-element.38.column.refs_4_.refs_5_.refs_9_, ...), custom_call_target="tpu_custom_call" | custom-call | flops 1600000000 | bytes 1 | tf_op jit(solution)/shard_map/own/pallas_call | solution.py:431
  8.9 0.0 collective-permute-done.refs_0_.refs_2_.refs_20_
  9.0 0.5 %collective-permute-start.1 = (f32[1,192,128]{2,1,0:T(8,128)S(1)}, f32[1,192,128]{2,1,0:T(8,128)S(1)}, u32[]{:S(2)}, u32[]{:S(2)}) collective-permute-start(f32[1,192,128]{2,1,0:T(8,128)S(1)} %pass.2), channel_id=1, source_target_pairs={{0,1},{1,0},{2,3},{3,2},{4,5},{5,4},{6,7},{7,6},{8,9},{9,8},{10,11... | collective-permute-start | bytes 294920 | tf_op jit(solution)/shard_map/ppermute | solution.py:354
  9.5 0.0 collective-permute-done.4.refs_1_.refs_18_
  9.5 0.2 pick.2.refs_7_.refs_2_
  9.7 1.3 %collective-permute-done.2.refs_2_.refs_0_.refs_22_ = f32[192,128]{1,0:T(8,128)S(1)} collective-permute-done((f32[192,128]{1,0:T(8,128)S(1)}, f32[192,128]{1,0:T(8,128)S(1)}, u32[]{:S(2)}, u32[]{:S(2)}) %collective-permute-start.2) | collective-permute-done | bytes 98336 | tf_op jit(solution)/shard_map/ppermute | solution.py:354
  11.0 0.3 collective-permute-done.3.refs_3_.refs_1_.refs_24_
  11.3 0.5 %collective-permute-start.5 = (f32[2,192,128]{2,1,0:T(8,128)S(1)}, f32[2,192,128]{2,1,0:T(8,128)S(1)}, u32[]{:S(2)}, u32[]{:S(2)}) collective-permute-start(f32[2,192,128]{2,1,0:T(8,128)S(1)} %pass.3), channel_id=1, source_target_pairs={{0,1},{1,0},{2,3},{3,2},{4,5},{5,4},{6,7},{7,6},{8,9},{9,8},{10,11... | collective-permute-start | bytes 589832 | tf_op jit(solution)/shard_map/ppermute | solution.py:354
  11.9 0.0 collective-permute-done.1
  11.9 0.3 %pick.3.refs_2_ = f32[64,128]{1,0:T(8,128)S(1)} custom-call(s32[1]{0:T(128)} %bitcast.me.refs_0_, f32[192,128]{1,0:T(8,128)S(1)} %bitcast.14, f32[192,128]{1,0:T(8,128)S(1)} %collective-permute-done.2.refs_2_.refs_0_.refs_22_, f32[192,128]{1,0:T(8,128)S(1)} %collective-permute-done.3.refs_3_.refs_1_.refs_24_, ...), custom_call_target="tpu_custom_call" | custom-call | flops 1200000000 | bytes 1 | tf_op jit(solution)/shard_map/pick/pallas_call | solution.py:443
  12.2 0.7 %collective-permute-done.5 = f32[2,192,128]{2,1,0:T(8,128)S(1)} collective-permute-done((f32[2,192,128]{2,1,0:T(8,128)S(1)}, f32[2,192,128]{2,1,0:T(8,128)S(1)}, u32[]{:S(2)}, u32[]{:S(2)}) %collective-permute-start.5) | collective-permute-done | bytes 196640 | tf_op jit(solution)/shard_map/ppermute | solution.py:354
  13.0 1.5 %project.1 = (f32[16,128]{1,0:T(8,128)S(1)}, f32[320,128]{1,0:T(8,128)S(1)}) custom-call(s32[1]{0:T(128)} %bitcast.me.refs_0_, f32[16,128,256]{2,1,0:T(8,128)S(1)} %get-tuple-element.40.refs_1_, f32[64,128]{1,0:T(8,128)S(1)} %pick.3.refs_2_, f32[16,128]{1,0:T(8,128)S(1)} %get-tuple-element.42.refs_3_, s32[32,128]{1,0:T(8,128)S(1)} %get-tuple-element.43.refs_4_, ...), custom_call_target="tpu_custom_call" | custom-call | tf_op jit(solution)/shard_map/project/pallas_call | solution.py:464
  14.5 8.9 %all_to_all.5 = f32[8,40,128]{2,1,0:T(8,128)S(1)} all-to-all(f32[8,40,128]{2,1,0:T(8,128)S(1)} %bitcast.13), channel_id=1, replica_groups=mesh['sky'=4,'tm'=8] {'tm'}, dimensions={0} | all-to-all | bytes 327680 | tf_op jit(solution)/shard_map/all_to_all | solution.py:496
  23.3 0.2 attitude.3.refs_0_
  23.5 2.6 %collective-permute-start.6 = (f32[40,128]{1,0:T(8,128)S(1)}, f32[40,128]{1,0:T(8,128)S(1)}, u32[]{:S(2)}, u32[]{:S(2)}) collective-permute-start(f32[40,128]{1,0:T(8,128)S(1)} %attitude.3.refs_0_), channel_id=1, source_target_pairs={{0,16},{8,24},{16,0},{24,8},{1,17},{9,25},{17,1},{25,9},{2,18},{10... | collective-permute-start | bytes 61448 | tf_op jit(solution)/shard_map/ppermute | solution.py:354
  26.1 1.3 %collective-permute-start.7 = (f32[40,128]{1,0:T(8,128)S(1)}, f32[40,128]{1,0:T(8,128)S(1)}, u32[]{:S(2)}, u32[]{:S(2)}) collective-permute-start(f32[40,128]{1,0:T(8,128)S(1)} %attitude.3.refs_0_), channel_id=1, source_target_pairs={{0,24},{8,16},{16,8},{24,0},{1,25},{9,17},{17,9},{25,1},{2,26},{10... | collective-permute-start | bytes 61448 | tf_op jit(solution)/shard_map/ppermute | solution.py:354
  27.5 0.2 collective-permute-start.8
  27.7 1.9 %source.3 = (f32[5,4096]{1,0:T(8,128)}, f32[16,128]{1,0:T(8,128)}, f32[8,128]{1,0:T(8,128)S(1)}) custom-call(s32[1]{0:T(128)} %bitcast.me.refs_0_, f32[320,128]{1,0:T(8,128)S(1)} %bitcast.12, f32[16,128]{1,0:T(8,128)S(1)} %get-tuple-element.54.held), custom_call_target="tpu_custom_call" | custom-call | flops 2000000000 | bytes 1 | tf_op jit(solution)/shard_map/source/pallas_call | solution.py:507
  29.6 0.0 collective-permute-done.6.refs_1_
  29.6 2.1 %collective-permute-done.7.refs_2_ = f32[40,128]{1,0:T(8,128)S(1)} collective-permute-done((f32[40,128]{1,0:T(8,128)S(1)}, f32[40,128]{1,0:T(8,128)S(1)}, u32[]{:S(2)}, u32[]{:S(2)}) %collective-permute-start.7) | collective-permute-done | bytes 20512 | tf_op jit(solution)/shard_map/ppermute | solution.py:354
  31.7 0.0 collective-permute-done.8.refs_3_
  31.7 0.6 %finish.1 = (f32[16,256]{1,0:T(8,128)}, f32[1,1]{1,0:T(1,128)}) custom-call(f32[40,128]{1,0:T(8,128)S(1)} %attitude.3.refs_0_, f32[40,128]{1,0:T(8,128)S(1)} %collective-permute-done.6.refs_1_, f32[40,128]{1,0:T(8,128)S(1)} %collective-permute-done.7.refs_2_, f32[40,128]{1,0:T(8,128)S(1)} %collective-permute-done.8.refs_3_, ...), custom_call_target="tpu_custom_call" | custom-call | tf_op jit(solution)/shard_map/finish/pallas_call | solution.py:526
  (3 shorter events, 0.0 us)
Async XLA Ops:
  1.6 7.3 %collective-permute-start = (f32[192,128]{1,0:T(8,128)S(1)}, f32[192,128]{1,0:T(8,128)S(1)}, u32[]{:S(2)}, u32[]{:S(2)}) collective-permute-start(f32[192,128]{1,0:T(8,128)S(1)} %get-tuple-element.32.table.refs_17_), channel_id=1, source_target_pairs={{0,3},{1,2},{2,1},{3,0},{4,7},{5,6},{6,5},{7,4},{8,11},{9,10},{10,... | collective-permute-start | bytes 294920 | tf_op jit(solution)/shard_map/ppermute | solution.py:354
  4.1 5.4 %collective-permute-start.4 = (f32[192,128]{1,0:T(8,128)S(1)}, f32[192,128]{1,0:T(8,128)S(1)}, u32[]{:S(2)}, u32[]{:S(2)}) collective-permute-start(f32[192,128]{1,0:T(8,128)S(1)} %get-tuple-element.32.table.refs_17_), channel_id=1, source_target_pairs={{0,1},{1,0},{2,3},{3,2},{4,5},{5,4},{6,7},{7,6},{8,9},{9,8},{10,11... | collective-permute-start | bytes 294920 | tf_op jit(solution)/shard_map/ppermute | solution.py:354
  4.8 6.2 %collective-permute-start.2 = (f32[192,128]{1,0:T(8,128)S(1)}, f32[192,128]{1,0:T(8,128)S(1)}, u32[]{:S(2)}, u32[]{:S(2)}) collective-permute-start(f32[192,128]{1,0:T(8,128)S(1)} %get-tuple-element.32.table.refs_17_), channel_id=1, source_target_pairs={{0,5},{1,4},{2,7},{3,6},{4,1},{5,0},{6,3},{7,2},{8,13},{9,12},{10,... | collective-permute-start | bytes 294920 | tf_op jit(solution)/shard_map/ppermute | solution.py:354
  5.9 5.4 %collective-permute-start.3 = (f32[192,128]{1,0:T(8,128)S(1)}, f32[192,128]{1,0:T(8,128)S(1)}, u32[]{:S(2)}, u32[]{:S(2)}) collective-permute-start(f32[192,128]{1,0:T(8,128)S(1)} %get-tuple-element.32.table.refs_17_), channel_id=1, source_target_pairs={{0,7},{1,6},{2,5},{3,4},{4,3},{5,2},{6,1},{7,0},{8,15},{9,14},{10,... | collective-permute-start | bytes 294920 | tf_op jit(solution)/shard_map/ppermute | solution.py:354
  9.0 2.9 %collective-permute-start.1 = (f32[1,192,128]{2,1,0:T(8,128)S(1)}, f32[1,192,128]{2,1,0:T(8,128)S(1)}, u32[]{:S(2)}, u32[]{:S(2)}) collective-permute-start(f32[1,192,128]{2,1,0:T(8,128)S(1)} %pass.2), channel_id=1, source_target_pairs={{0,1},{1,0},{2,3},{3,2},{4,5},{5,4},{6,7},{7,6},{8,9},{9,8},{10,11... | collective-permute-start | bytes 294920 | tf_op jit(solution)/shard_map/ppermute | solution.py:354
  11.3 1.6 %collective-permute-start.5 = (f32[2,192,128]{2,1,0:T(8,128)S(1)}, f32[2,192,128]{2,1,0:T(8,128)S(1)}, u32[]{:S(2)}, u32[]{:S(2)}) collective-permute-start(f32[2,192,128]{2,1,0:T(8,128)S(1)} %pass.3), channel_id=1, source_target_pairs={{0,1},{1,0},{2,3},{3,2},{4,5},{5,4},{6,7},{7,6},{8,9},{9,8},{10,11... | collective-permute-start | bytes 589832 | tf_op jit(solution)/shard_map/ppermute | solution.py:354
  23.5 6.1 %collective-permute-start.6 = (f32[40,128]{1,0:T(8,128)S(1)}, f32[40,128]{1,0:T(8,128)S(1)}, u32[]{:S(2)}, u32[]{:S(2)}) collective-permute-start(f32[40,128]{1,0:T(8,128)S(1)} %attitude.3.refs_0_), channel_id=1, source_target_pairs={{0,16},{8,24},{16,0},{24,8},{1,17},{9,25},{17,1},{25,9},{2,18},{10... | collective-permute-start | bytes 61448 | tf_op jit(solution)/shard_map/ppermute | solution.py:354
  26.1 5.6 %collective-permute-start.7 = (f32[40,128]{1,0:T(8,128)S(1)}, f32[40,128]{1,0:T(8,128)S(1)}, u32[]{:S(2)}, u32[]{:S(2)}) collective-permute-start(f32[40,128]{1,0:T(8,128)S(1)} %attitude.3.refs_0_), channel_id=1, source_target_pairs={{0,24},{8,16},{16,8},{24,0},{1,25},{9,17},{17,9},{25,1},{2,26},{10... | collective-permute-start | bytes 61448 | tf_op jit(solution)/shard_map/ppermute | solution.py:354
  27.5 4.2 %collective-permute-start.8 = (f32[40,128]{1,0:T(8,128)S(1)}, f32[40,128]{1,0:T(8,128)S(1)}, u32[]{:S(2)}, u32[]{:S(2)}) collective-permute-start(f32[40,128]{1,0:T(8,128)S(1)} %attitude.3.refs_0_), channel_id=1, source_target_pairs={{0,8},{8,0},{16,24},{24,16},{1,9},{9,1},{17,25},{25,17},{2,10},{10... | collective-permute-start | bytes 61448 | tf_op jit(solution)/shard_map/ppermute | solution.py:354

commit v8 on v7

--- a/solution.py
+++ b/solution.py
@@ -30,11 +30,6 @@
 def halves(x):
     high = x.astype(BF16)
     return high, (x - high.astype(F32)).astype(BF16)
-
-
-def thirds(x):
-    high = x.astype(BF16)
-    return (high, *halves(x - high.astype(F32)))
 
 
 def pack_kernel(source, attitude, *refs):
@@ -86,12 +81,21 @@
     total[rows, :] = terms
 
 
-def own_kernel(me, table, block, column, coef, tiles_in, total, tiles, sem, *, share):
-    copy = pltpu.make_async_copy(tiles_in, tiles, sem)
-    copy.start()
+def own_kernel(me, table, block, column, coef, tiles_in, total, tiles, pieces, sems, *, share):
+    chunks = sems.shape[0]
+    each = tiles.shape[0] // chunks
+    copies = []
+    for q in range(chunks):
+        part = pl.ds(q * each, each)
+        copies.append(pltpu.make_async_copy(tiles_in.at[part], tiles.at[part], sems.at[q]))
+        copies[q].start()
     total[...] = jnp.zeros_like(total)
     serve(me[0], table, block, column, coef, total, share)
-    copy.wait()
+    for q in range(chunks):
+        copies[q].wait()
+        for t in range(q * each, (q + 1) * each):
+            depth = tiles.shape[1]
+            pieces[t, :depth, :], pieces[t, depth:, :] = halves(tiles[t])
 
 
 def pick_kernel(*refs, offsets, share):
@@ -190,15 +194,18 @@
     )
     same = jnp.broadcast_to(owner_down, square) == jnp.broadcast_to(owner_along, square)
     ranks = jnp.sum(jnp.where(same & (one < two), 1, 0), axis=0, keepdims=True)
-    place = jnp.broadcast_to(owner_along * CAP_TILES + ranks, fill.shape)
-    filled = lax.broadcasted_iota(jnp.int32, fill.shape, 0) == place
-    fill[...] = jnp.where(filled, 1.0, 0.0)
-    named = jnp.sum(jnp.where(filled, jnp.broadcast_to(along + 1, fill.shape), 0), axis=1, keepdims=True) - 1
+    wide = (names.shape[0], tile_total)
+    place = jnp.broadcast_to(owner_along * CAP_TILES + ranks, wide)
+    filled = lax.broadcasted_iota(jnp.int32, wide, 0) == place
+    ones = jnp.where(filled, 1.0, 0.0)
+    for t in range(tile_total):
+        fill[t] = jnp.broadcast_to(ones[:, t : t + 1], names.shape)
+    named = jnp.sum(jnp.where(filled, jnp.broadcast_to(along + 1, wide), 0), axis=1, keepdims=True) - 1
     names[...] = jnp.broadcast_to(named, names.shape).astype(F32)
 
 
 def project_kernel(*refs, seg_rows, offsets, late):
-    me, tiles, before, weight, tile_at, lane_at, coef_at, source_at, *refs = refs
+    me, tiles, pieces, before, weight, tile_at, lane_at, coef_at, source_at, *refs = refs
     block, column, coef_by, row_at, rank_at, live, aim, fill, names, *refs = refs
     tables, refs = refs[: len(offsets)], refs[len(offsets) :]
     projected, sent, lines, served = refs
@@ -227,7 +234,7 @@
             total = jnp.where(row == o * 8 + h, found, total)
     hit = aim[...].astype(BF16)
     directions = jnp.zeros((tile_total, folds * LANES), F32)
-    for piece in thirds(lines[...]):
+    for piece in halves(lines[...]):
         directions = directions + jnp.dot(hit, piece, preferred_element_type=F32)
     row_ids = lax.broadcasted_iota(jnp.int32, shape, 0)
     tile_part = jnp.zeros(shape, F32)
@@ -257,20 +264,19 @@
         values = coef_at[k] * ordered if k < params else source_at[...]
         for o in range(owners):
             sent[pl.ds(o * depth + k * share, share), :] = values[o * share : (o + 1) * share]
-    pieces = jnp.concatenate(halves(weighted), axis=0).astype(F32)
-    whose = lax.rem(lax.broadcasted_iota(jnp.int32, pieces.shape, 0), tile_total)
-    grads = jnp.zeros((2 * tile_total, tiles.shape[2]), F32)
-    rest = jnp.zeros((tile_total, tiles.shape[2]), F32)
+    high, low = (x.astype(F32) for x in halves(weighted))
+    places = fill.shape[1]
+    nothing = jnp.zeros((places, LANES), BF16)
+    sums = jnp.zeros((2 * places, folds * LANES), F32)
     for t in range(tile_total):
-        first, second = halves(tiles[t])
-        left = jnp.where(whose == t, pieces, 0.0).astype(BF16)
-        grads = grads + jnp.dot(left, first, preferred_element_type=F32)
-        rest = rest + jnp.dot(left[:tile_total], second, preferred_element_type=F32)
-    grads = grads[:tile_total] + grads[tile_total:] + rest
-    place = fill[...].astype(BF16)
-    placed = jnp.zeros((fill.shape[0], folds * LANES), F32)
-    for piece in halves(grads):
-        placed = placed + jnp.dot(place, piece, preferred_element_type=F32)
+        mask = fill[t]
+        one = (mask * high[t : t + 1]).astype(BF16)
+        two = (mask * low[t : t + 1]).astype(BF16)
+        left = jnp.concatenate(
+            [jnp.concatenate([one, one], axis=1), jnp.concatenate([two, nothing], axis=1)], axis=0
+        )
+        sums = sums + jnp.dot(left, pieces[t], preferred_element_type=F32)
+    placed = sums[:places] + sums[places:]
     for o in range(owners):
         rows = slice(o * CAP_TILES, (o + 1) * CAP_TILES)
         for c in range(folds):
@@ -359,7 +365,7 @@
     params, span = src_dir.shape
     seg_rows = att_dir.shape[0]
     folds = cols // LANES
-    across = range(3, tm, 2)
+    across = [*range(tm - 1, 2, -2)]
     me = lax.axis_index("tm").astype(jnp.int32).reshape(1)
 
     directions, index, coef, weight, seg, count = pl.pallas_call(
@@ -414,7 +420,7 @@
             by_tile,
             jax.ShapeDtypeStruct(src_index.shape, F32),
             jax.ShapeDtypeStruct((tile_total, tm * seg_rows), F32),
-            jax.ShapeDtypeStruct((tm * CAP_TILES, tile_total), F32),
+            jax.ShapeDtypeStruct((tile_total, tm * CAP_TILES, LANES), F32),
             jax.ShapeDtypeStruct((tm * CAP_TILES, LANES), F32),
         ),
         in_specs=[SMEM] + [VMEM] * 4,
@@ -428,12 +434,12 @@
         name="order",
     )(me, seg, count, index, coef)
     picked_shape = jax.ShapeDtypeStruct((tm * 8, LANES), F32)
-    picked, tiles_held = pl.pallas_call(
+    picked, tiles_held, pieces = pl.pallas_call(
         functools.partial(own_kernel, share=share),
-        out_shape=(picked_shape, jax.ShapeDtypeStruct(tiles.shape, F32)),
+        out_shape=(picked_shape, jax.ShapeDtypeStruct(tiles.shape, F32), jax.ShapeDtypeStruct((tile_total, 2 * row_count, cols), BF16)),
         in_specs=[SMEM] + [VMEM] * 4 + [HBM],
-        out_specs=(VMEM, VMEM),
-        scratch_shapes=[pltpu.SemaphoreType.DMA],
+        out_specs=(VMEM,) * 3,
+        scratch_shapes=[pltpu.SemaphoreType.DMA((4,))],
         compiler_params=PARAMS,
         cost_estimate=cost(1.6),
         name="own",
@@ -450,13 +456,13 @@
             name="pick",
         )(me, *[tables[o] for o in offsets], block, column, coef_by, before)
 
-    first_pair = swapped(passed([3], picked), "tm", tm, 1)
-    tables[2] = first_pair[0]
-    picked = pick([1, 3], picked)
+    first_pair = swapped(passed(across[:1], picked), "tm", tm, 1)
+    tables[across[0] - 1] = first_pair[0]
+    picked = pick([1, across[0]], picked)
     others = swapped(passed(far, picked), "tm", tm, 1)
     for q, offset in enumerate(far):
         tables[offset - 1] = others[q]
-    picked = pick([2, *far], picked)
+    picked = pick([across[0] - 1, *far], picked)
     late = [o - 1 for o in across[1:]]
     offsets = sorted(tables)
     grads_from = up8((params + 1) * share)
@@ -467,7 +473,7 @@
             jax.ShapeDtypeStruct((tile_total, row_count), F32),
             jax.ShapeDtypeStruct((tm * depth, LANES), F32),
         ),
-        in_specs=[SMEM] + [VMEM] * (16 + tm),
+        in_specs=[SMEM] + [VMEM] * (17 + tm),
         out_specs=(VMEM, VMEM),
         scratch_shapes=[
             pltpu.VMEM((tm * seg_rows, folds * LANES), F32),
@@ -478,6 +484,7 @@
     )(
         me,
         tiles_held,
+        pieces,
         picked,
         weight,
         tile_at,

time: 32.5 us -> 32.1 us (0.988)
  no operation moved by 1% of the time
where the time goes in v8:
time: 32.1 us; the launch traced here: 31.9 us
  starting transfers between devices  9.73 us (30%)
  blocking collectives  8.84 us (28%)
  Pallas kernels  8.49 us (26%)
  waiting for transfers between devices  4.15 us (13%)
  between operations  0.7 us (2%)
    ppermute x9, starting transfers between devices, swapped(): return lax.ppermute(x, axis, [(i, i ^ offset) for i in range(size)])  9.73 us
    all_to_all x1, blocking collectives, per_device(): lax.all_to_all(sent.reshape(tm, depth, LANES), 'tm', 0, 0)  8.84 us
    ppermute x9, waiting for transfers between devices, swapped(): return lax.ppermute(x, axis, [(i, i ^ offset) for i in range(size)])  4.15 us
    pallas_call x1, Pallas kernels, per_device(): pl.pallas_call(functools.partial(source_kernel, owners=tm, share=share),...  1.87 us
    pallas_call x1, Pallas kernels, per_device(): pl.pallas_call(functools.partial(own_kernel, share=share), out_shape=(pic...  1.65 us
    pallas_call x1, Pallas kernels, per_device(): pl.pallas_call(functools.partial(order_kernel, owners=tm, span=span, cap=...  1.34 us
    pallas_call x1, Pallas kernels, per_device(): pl.pallas_call(functools.partial(project_kernel, seg_rows=seg_rows, offse...  1.22 us
    pallas_call x1, Pallas kernels, per_device(): pl.pallas_call(pack_kernel, out_shape=(jax.ShapeDtypeStruct((params * (sp...  1 us
  transfers between devices with their start and end apart: 9, of which 4 were waited for; matrix products, arithmetic and copies ran while one was open for 0% of the time, Pallas kernels for 17%

profile of v8, /device:TPU:0, one launch (start us, length us, event | category | flops | bytes accessed | tf_op | source)
XLA Modules:
  0.0 31.9 jit_solution(1452988813923132439)
XLA Ops:
  0.6 1.0 %pack.1 = (f32[192,128]{1,0:T(8,128)S(1)}, s32[16,128]{1,0:T(8,128)S(1)}, f32[5,16,128]{2,1,0:T(8,128)S(1)}, f32[16,128]{1,0:T(8,128)S(1)}, s32[1,16]{1,0:T(1,128)S(1)}, /*index=5*/s32[1,16]{1,0:T(1,128)S(1)}) custom-call(f32[5,4096]{1,0:T(8,128)} %source.2, f32[16,256]{1,0:T(8,128)} %attitude.2, s32[16,128]{1,0:T(8,128)} %refs_0_.1, f32[5,16,128]{2,1,0:T(8,128)} %refs_1_.1, ...), custom_call_target="tpu_custom_call" | custom-call | tf_op jit(solution)/shard_map/pack/pallas_call | solution.py:371
  1.6 3.4 %collective-permute-start = (f32[192,128]{1,0:T(8,128)S(1)}, f32[192,128]{1,0:T(8,128)S(1)}, u32[]{:S(2)}, u32[]{:S(2)}) collective-permute-start(f32[192,128]{1,0:T(8,128)S(1)} %get-tuple-element.33.table.refs_18_), channel_id=1, source_target_pairs={{0,7},{1,6},{2,5},{3,4},{4,3},{5,2},{6,1},{7,0},{8,15},{9,14},{10,... | collective-permute-start | bytes 294920 | tf_op jit(solution)/shard_map/ppermute | solution.py:360
  5.0 0.7 %collective-permute-start.4 = (f32[192,128]{1,0:T(8,128)S(1)}, f32[192,128]{1,0:T(8,128)S(1)}, u32[]{:S(2)}, u32[]{:S(2)}) collective-permute-start(f32[192,128]{1,0:T(8,128)S(1)} %get-tuple-element.33.table.refs_18_), channel_id=1, source_target_pairs={{0,1},{1,0},{2,3},{3,2},{4,5},{5,4},{6,7},{7,6},{8,9},{9,8},{10,11... | collective-permute-start | bytes 294920 | tf_op jit(solution)/shard_map/ppermute | solution.py:360
  5.7 0.1 collective-permute-start.2
  5.8 0.2 collective-permute-start.3
  6.0 1.3 %order.1 = (s32[32,128]{1,0:T(8,128)S(1)}, s32[32,128]{1,0:T(8,128)S(1)}, f32[5,32,128]{2,1,0:T(8,128)S(1)}, f32[32,128]{1,0:T(8,128)S(1)}, s32[64,128]{1,0:T(8,...) custom-call(s32[1]{0:T(128)} %bitcast.me.refs_0_, ...), custom_call_target="tpu_custom_call" | custom-call | flops 1500000000 | bytes 1 | tf_op jit(solution)/shard_map/order/pallas_call | solution.py:409
  7.4 1.6 %own.1 = (f32[64,128]{1,0:T(8,128)S(1)}, f32[16,128,256]{2,1,0:T(8,128)S(1)}, bf16[16,256,256]{2,1,0:T(8,128)(2,1)S(1)}) custom-call(s32[1]{0:T(128)} %bitcast.me.refs_0_, f32[192,128]{1,0:T(8,128)S(1)} %get-tuple-element.33.table.refs_18_, s32[64,128]{1,0:T(8,128)S(1)} %get-tuple-element.38.block.refs_3_.refs_4_.refs_9_, ...), custom_call_target="tpu_custom_call" | custom-call | flops 1600000000 | bytes 1 | tf_op jit(solution)/shard_map/own/pallas_call | solution.py:437
  9.1 0.0 collective-permute-done.refs_0_.refs_2_.refs_25_
  9.1 0.5 %collective-permute-start.1 = (f32[1,192,128]{2,1,0:T(8,128)S(1)}, f32[1,192,128]{2,1,0:T(8,128)S(1)}, u32[]{:S(2)}, u32[]{:S(2)}) collective-permute-start(f32[1,192,128]{2,1,0:T(8,128)S(1)} %pass.2), channel_id=1, source_target_pairs={{0,1},{1,0},{2,3},{3,2},{4,5},{5,4},{6,7},{7,6},{8,9},{9,8},{10,11... | collective-permute-start | bytes 294920 | tf_op jit(solution)/shard_map/ppermute | solution.py:360
  9.6 0.0 collective-permute-done.4.refs_1_.refs_19_
  9.6 0.2 pick.2.refs_7_.refs_2_
  9.8 0.8 %collective-permute-done.2.refs_2_.refs_0_.refs_23_ = f32[192,128]{1,0:T(8,128)S(1)} collective-permute-done((f32[192,128]{1,0:T(8,128)S(1)}, f32[192,128]{1,0:T(8,128)S(1)}, u32[]{:S(2)}, u32[]{:S(2)}) %collective-permute-start.2) | collective-permute-done | bytes 98336 | tf_op jit(solution)/shard_map/ppermute | solution.py:360
  10.6 0.3 collective-permute-done.3.refs_3_.refs_1_.refs_21_
  11.0 0.3 collective-permute-start.5
  11.2 0.0 collective-permute-done.1
  11.2 0.3 %pick.3.refs_3_ = f32[64,128]{1,0:T(8,128)S(1)} custom-call(s32[1]{0:T(128)} %bitcast.me.refs_0_, f32[192,128]{1,0:T(8,128)S(1)} %bitcast.14, f32[192,128]{1,0:T(8,128)S(1)} %collective-permute-done.2.refs_2_.refs_0_.refs_23_, f32[192,128]{1,0:T(8,128)S(1)} %collective-permute-done.3.refs_3_.refs_1_.refs_21_, ...), custom_call_target="tpu_custom_call" | custom-call | flops 1200000000 | bytes 1 | tf_op jit(solution)/shard_map/pick/pallas_call | solution.py:449
  11.6 0.9 %collective-permute-done.5 = f32[2,192,128]{2,1,0:T(8,128)S(1)} collective-permute-done((f32[2,192,128]{2,1,0:T(8,128)S(1)}, f32[2,192,128]{2,1,0:T(8,128)S(1)}, u32[]{:S(2)}, u32[]{:S(2)}) %collective-permute-start.5) | collective-permute-done | bytes 196640 | tf_op jit(solution)/shard_map/ppermute | solution.py:360
  12.5 1.2 %project.1 = (f32[16,128]{1,0:T(8,128)S(1)}, f32[320,128]{1,0:T(8,128)S(1)}) custom-call(s32[1]{0:T(128)} %bitcast.me.refs_0_, f32[16,128,256]{2,1,0:T(8,128)S(1)} %get-tuple-element.41.refs_1_, bf16[16,256,256]{2,1,0:T(8,128)(2,1)S(1)} %get-tuple-element.42.refs_2_, f32[64,128]{1,0:T(8,128)S(1)} %pick.3.refs_3_, f32[16,128]{1,0:T(8,128)S(1)} %get-tuple-element.44.refs_4_, ...), custom_call_target="tpu_custom_call" | custom-call | tf_op jit(solution)/shard_map/project/pallas_call | solution.py:470
  13.7 8.8 %all_to_all.5 = f32[8,40,128]{2,1,0:T(8,128)S(1)} all-to-all(f32[8,40,128]{2,1,0:T(8,128)S(1)} %bitcast.13), channel_id=1, replica_groups=mesh['sky'=4,'tm'=8] {'tm'}, dimensions={0} | all-to-all | bytes 327680 | tf_op jit(solution)/shard_map/all_to_all | solution.py:503
  22.5 0.2 attitude.3.refs_0_
  22.7 3.0 %collective-permute-start.6 = (f32[40,128]{1,0:T(8,128)S(1)}, f32[40,128]{1,0:T(8,128)S(1)}, u32[]{:S(2)}, u32[]{:S(2)}) collective-permute-start(f32[40,128]{1,0:T(8,128)S(1)} %attitude.3.refs_0_), channel_id=1, source_target_pairs={{0,16},{8,24},{16,0},{24,8},{1,17},{9,25},{17,1},{25,9},{2,18},{10... | collective-permute-start | bytes 61448 | tf_op jit(solution)/shard_map/ppermute | solution.py:360
  25.7 1.3 %collective-permute-start.7 = (f32[40,128]{1,0:T(8,128)S(1)}, f32[40,128]{1,0:T(8,128)S(1)}, u32[]{:S(2)}, u32[]{:S(2)}) collective-permute-start(f32[40,128]{1,0:T(8,128)S(1)} %attitude.3.refs_0_), channel_id=1, source_target_pairs={{0,24},{8,16},{16,8},{24,0},{1,25},{9,17},{17,9},{25,1},{2,26},{10... | collective-permute-start | bytes 61448 | tf_op jit(solution)/shard_map/ppermute | solution.py:360
  27.1 0.2 collective-permute-start.8
  27.3 1.9 %source.3 = (f32[5,4096]{1,0:T(8,128)}, f32[16,128]{1,0:T(8,128)}, f32[8,128]{1,0:T(8,128)S(1)}) custom-call(s32[1]{0:T(128)} %bitcast.me.refs_0_, f32[320,128]{1,0:T(8,128)S(1)} %bitcast.12, f32[16,128]{1,0:T(8,128)S(1)} %get-tuple-element.56.held), custom_call_target="tpu_custom_call" | custom-call | flops 2000000000 | bytes 1 | tf_op jit(solution)/shard_map/source/pallas_call | solution.py:514
  29.2 0.0 collective-permute-done.6.refs_1_
  29.2 2.1 %collective-permute-done.7.refs_2_ = f32[40,128]{1,0:T(8,128)S(1)} collective-permute-done((f32[40,128]{1,0:T(8,128)S(1)}, f32[40,128]{1,0:T(8,128)S(1)}, u32[]{:S(2)}, u32[]{:S(2)}) %collective-permute-start.7) | collective-permute-done | bytes 20512 | tf_op jit(solution)/shard_map/ppermute | solution.py:360
  31.3 0.0 collective-permute-done.8.refs_3_
  31.3 0.6 %finish.1 = (f32[16,256]{1,0:T(8,128)}, f32[1,1]{1,0:T(1,128)}) custom-call(f32[40,128]{1,0:T(8,128)S(1)} %attitude.3.refs_0_, f32[40,128]{1,0:T(8,128)S(1)} %collective-permute-done.6.refs_1_, f32[40,128]{1,0:T(8,128)S(1)} %collective-permute-done.7.refs_2_, f32[40,128]{1,0:T(8,128)S(1)} %collective-permute-done.8.refs_3_, ...), custom_call_target="tpu_custom_call" | custom-call | tf_op jit(solution)/shard_map/finish/pallas_call | solution.py:533
  (3 shorter events, 0.0 us)
Async XLA Ops:
  1.6 7.4 %collective-permute-start = (f32[192,128]{1,0:T(8,128)S(1)}, f32[192,128]{1,0:T(8,128)S(1)}, u32[]{:S(2)}, u32[]{:S(2)}) collective-permute-start(f32[192,128]{1,0:T(8,128)S(1)} %get-tuple-element.33.table.refs_18_), channel_id=1, source_target_pairs={{0,7},{1,6},{2,5},{3,4},{4,3},{5,2},{6,1},{7,0},{8,15},{9,14},{10,... | collective-permute-start | bytes 294920 | tf_op jit(solution)/shard_map/ppermute | solution.py:360
  5.0 4.5 %collective-permute-start.4 = (f32[192,128]{1,0:T(8,128)S(1)}, f32[192,128]{1,0:T(8,128)S(1)}, u32[]{:S(2)}, u32[]{:S(2)}) collective-permute-start(f32[192,128]{1,0:T(8,128)S(1)} %get-tuple-element.33.table.refs_18_), channel_id=1, source_target_pairs={{0,1},{1,0},{2,3},{3,2},{4,5},{5,4},{6,7},{7,6},{8,9},{9,8},{10,11... | collective-permute-start | bytes 294920 | tf_op jit(solution)/shard_map/ppermute | solution.py:360
  5.7 4.9 %collective-permute-start.2 = (f32[192,128]{1,0:T(8,128)S(1)}, f32[192,128]{1,0:T(8,128)S(1)}, u32[]{:S(2)}, u32[]{:S(2)}) collective-permute-start(f32[192,128]{1,0:T(8,128)S(1)} %get-tuple-element.33.table.refs_18_), channel_id=1, source_target_pairs={{0,5},{1,4},{2,7},{3,6},{4,1},{5,0},{6,3},{7,2},{8,13},{9,12},{10,... | collective-permute-start | bytes 294920 | tf_op jit(solution)/shard_map/ppermute | solution.py:360
  5.8 5.1 %collective-permute-start.3 = (f32[192,128]{1,0:T(8,128)S(1)}, f32[192,128]{1,0:T(8,128)S(1)}, u32[]{:S(2)}, u32[]{:S(2)}) collective-permute-start(f32[192,128]{1,0:T(8,128)S(1)} %get-tuple-element.33.table.refs_18_), channel_id=1, source_target_pairs={{0,3},{1,2},{2,1},{3,0},{4,7},{5,6},{6,5},{7,4},{8,11},{9,10},{10,... | collective-permute-start | bytes 294920 | tf_op jit(solution)/shard_map/ppermute | solution.py:360
  9.1 2.1 %collective-permute-start.1 = (f32[1,192,128]{2,1,0:T(8,128)S(1)}, f32[1,192,128]{2,1,0:T(8,128)S(1)}, u32[]{:S(2)}, u32[]{:S(2)}) collective-permute-start(f32[1,192,128]{2,1,0:T(8,128)S(1)} %pass.2), channel_id=1, source_target_pairs={{0,1},{1,0},{2,3},{3,2},{4,5},{5,4},{6,7},{7,6},{8,9},{9,8},{10,11... | collective-permute-start | bytes 294920 | tf_op jit(solution)/shard_map/ppermute | solution.py:360
  11.0 1.5 %collective-permute-start.5 = (f32[2,192,128]{2,1,0:T(8,128)S(1)}, f32[2,192,128]{2,1,0:T(8,128)S(1)}, u32[]{:S(2)}, u32[]{:S(2)}) collective-permute-start(f32[2,192,128]{2,1,0:T(8,128)S(1)} %pass.3), channel_id=1, source_target_pairs={{0,1},{1,0},{2,3},{3,2},{4,5},{5,4},{6,7},{7,6},{8,9},{9,8},{10,11... | collective-permute-start | bytes 589832 | tf_op jit(solution)/shard_map/ppermute | solution.py:360
  22.7 6.4 %collective-permute-start.6 = (f32[40,128]{1,0:T(8,128)S(1)}, f32[40,128]{1,0:T(8,128)S(1)}, u32[]{:S(2)}, u32[]{:S(2)}) collective-permute-start(f32[40,128]{1,0:T(8,128)S(1)} %attitude.3.refs_0_), channel_id=1, source_target_pairs={{0,16},{8,24},{16,0},{24,8},{1,17},{9,25},{17,1},{25,9},{2,18},{10... | collective-permute-start | bytes 61448 | tf_op jit(solution)/shard_map/ppermute | solution.py:360
  25.7 5.6 %collective-permute-start.7 = (f32[40,128]{1,0:T(8,128)S(1)}, f32[40,128]{1,0:T(8,128)S(1)}, u32[]{:S(2)}, u32[]{:S(2)}) collective-permute-start(f32[40,128]{1,0:T(8,128)S(1)} %attitude.3.refs_0_), channel_id=1, source_target_pairs={{0,24},{8,16},{16,8},{24,0},{1,25},{9,17},{17,9},{25,1},{2,26},{10... | collective-permute-start | bytes 61448 | tf_op jit(solution)/shard_map/ppermute | solution.py:360
  27.1 4.2 %collective-permute-start.8 = (f32[40,128]{1,0:T(8,128)S(1)}, f32[40,128]{1,0:T(8,128)S(1)}, u32[]{:S(2)}, u32[]{:S(2)}) collective-permute-start(f32[40,128]{1,0:T(8,128)S(1)} %attitude.3.refs_0_), channel_id=1, source_target_pairs={{0,8},{8,0},{16,24},{24,16},{1,9},{9,1},{17,25},{25,17},{2,10},{10... | collective-permute-start | bytes 61448 | tf_op jit(solution)/shard_map/ppermute | solution.py:360

commit v9 on v8

--- a/solution.py
+++ b/solution.py
@@ -458,11 +458,11 @@
 
     first_pair = swapped(passed(across[:1], picked), "tm", tm, 1)
     tables[across[0] - 1] = first_pair[0]
-    picked = pick([1, across[0]], picked)
+    picked = pick(across[:1], picked)
     others = swapped(passed(far, picked), "tm", tm, 1)
     for q, offset in enumerate(far):
         tables[offset - 1] = others[q]
-    picked = pick([across[0] - 1, *far], picked)
+    picked = pick([1, across[0] - 1, *far], picked)
     late = [o - 1 for o in across[1:]]
     offsets = sorted(tables)
     grads_from = up8((params + 1) * share)

time: 32.1 us -> 31.7 us (0.988)
  starting transfers between devices: 9.73 us -> 9.22 us
  waiting for transfers between devices: 4.15 us -> 4.63 us
  blocking collectives: 8.84 us -> 8.48 us
    ppermute x9, starting transfers between devices: 9.73 us -> 9.22 us  [swapped(): return lax.ppermute(x, axis, [(i, i ^ offset) for i in range(size)])]
    ppermute x9, waiting for transfers between devices: 4.15 us -> 4.63 us  [swapped(): return lax.ppermute(x, axis, [(i, i ^ offset) for i in range(size)])]
    all_to_all x1, blocking collectives: 8.84 us -> 8.48 us  [per_device(): lax.all_to_all(sent.reshape(tm, depth, LANES), 'tm', 0, 0)]
where the time goes in v9:
time: 31.7 us; the launch traced here: 31.5 us
  starting transfers between devices  9.22 us (29%)
  Pallas kernels  8.49 us (27%)
  blocking collectives  8.48 us (27%)
  waiting for transfers between devices  4.63 us (15%)
  between operations  0.7 us (2%)
    ppermute x9, starting transfers between devices, swapped(): return lax.ppermute(x, axis, [(i, i ^ offset) for i in range(size)])  9.22 us
    all_to_all x1, blocking collectives, per_device(): lax.all_to_all(sent.reshape(tm, depth, LANES), 'tm', 0, 0)  8.48 us
    ppermute x9, waiting for transfers between devices, swapped(): return lax.ppermute(x, axis, [(i, i ^ offset) for i in range(size)])  4.63 us
    pallas_call x1, Pallas kernels, per_device(): pl.pallas_call(functools.partial(source_kernel, owners=tm, share=share),...  1.87 us
    pallas_call x1, Pallas kernels, per_device(): pl.pallas_call(functools.partial(own_kernel, share=share), out_shape=(pic...  1.65 us
    pallas_call x1, Pallas kernels, per_device(): pl.pallas_call(functools.partial(order_kernel, owners=tm, span=span, cap=...  1.34 us
    pallas_call x1, Pallas kernels, per_device(): pl.pallas_call(functools.partial(project_kernel, seg_rows=seg_rows, offse...  1.22 us
    pallas_call x1, Pallas kernels, per_device(): pl.pallas_call(pack_kernel, out_shape=(jax.ShapeDtypeStruct((params * (sp...  1 us
  transfers between devices with their start and end apart: 9, of which 4 were waited for; matrix products, arithmetic and copies ran while one was open for 0% of the time, Pallas kernels for 17%

profile of v9, /device:TPU:0, one launch (start us, length us, event | category | flops | bytes accessed | tf_op | source)
XLA Modules:
  0.0 31.5 jit_solution(12934831042736419263)
XLA Ops:
  0.6 1.0 %pack.1 = (f32[192,128]{1,0:T(8,128)S(1)}, s32[16,128]{1,0:T(8,128)S(1)}, f32[5,16,128]{2,1,0:T(8,128)S(1)}, f32[16,128]{1,0:T(8,128)S(1)}, s32[1,16]{1,0:T(1,128)S(1)}, /*index=5*/s32[1,16]{1,0:T(1,128)S(1)}) custom-call(f32[5,4096]{1,0:T(8,128)} %source.2, f32[16,256]{1,0:T(8,128)} %attitude.2, s32[16,128]{1,0:T(8,128)} %refs_0_.1, f32[5,16,128]{2,1,0:T(8,128)} %refs_1_.1, ...), custom_call_target="tpu_custom_call" | custom-call | tf_op jit(solution)/shard_map/pack/pallas_call | solution.py:371
  1.6 3.4 %collective-permute-start.1 = (f32[192,128]{1,0:T(8,128)S(1)}, f32[192,128]{1,0:T(8,128)S(1)}, u32[]{:S(2)}, u32[]{:S(2)}) collective-permute-start(f32[192,128]{1,0:T(8,128)S(1)} %get-tuple-element.33.table.refs_18_), channel_id=1, source_target_pairs={{0,7},{1,6},{2,5},{3,4},{4,3},{5,2},{6,1},{7,0},{8,15},{9,14},{10,... | collective-permute-start | bytes 294920 | tf_op jit(solution)/shard_map/ppermute | solution.py:360
  5.0 0.8 %collective-permute-start.3 = (f32[192,128]{1,0:T(8,128)S(1)}, f32[192,128]{1,0:T(8,128)S(1)}, u32[]{:S(2)}, u32[]{:S(2)}) collective-permute-start(f32[192,128]{1,0:T(8,128)S(1)} %get-tuple-element.33.table.refs_18_), channel_id=1, source_target_pairs={{0,5},{1,4},{2,7},{3,6},{4,1},{5,0},{6,3},{7,2},{8,13},{9,12},{10,... | collective-permute-start | bytes 294920 | tf_op jit(solution)/shard_map/ppermute | solution.py:360
  5.8 0.1 collective-permute-start.4
  6.0 0.0 collective-permute-start
  6.0 1.3 %order.1 = (s32[32,128]{1,0:T(8,128)S(1)}, s32[32,128]{1,0:T(8,128)S(1)}, f32[5,32,128]{2,1,0:T(8,128)S(1)}, f32[32,128]{1,0:T(8,128)S(1)}, s32[64,128]{1,0:T(8,...) custom-call(s32[1]{0:T(128)} %bitcast.me.refs_0_, ...), custom_call_target="tpu_custom_call" | custom-call | flops 1500000000 | bytes 1 | tf_op jit(solution)/shard_map/order/pallas_call | solution.py:409
  7.3 1.6 %own.1 = (f32[64,128]{1,0:T(8,128)S(1)}, f32[16,128,256]{2,1,0:T(8,128)S(1)}, bf16[16,256,256]{2,1,0:T(8,128)(2,1)S(1)}) custom-call(s32[1]{0:T(128)} %bitcast.me.refs_0_, f32[192,128]{1,0:T(8,128)S(1)} %get-tuple-element.33.table.refs_18_, s32[64,128]{1,0:T(8,128)S(1)} %get-tuple-element.38.block.refs_2_.refs_5_.refs_9_, ...), custom_call_target="tpu_custom_call" | custom-call | flops 1600000000 | bytes 1 | tf_op jit(solution)/shard_map/own/pallas_call | solution.py:437
  9.0 0.0 collective-permute-done.1.refs_0_.refs_1_.refs_25_
  9.0 0.6 %collective-permute-start.2 = (f32[1,192,128]{2,1,0:T(8,128)S(1)}, f32[1,192,128]{2,1,0:T(8,128)S(1)}, u32[]{:S(2)}, u32[]{:S(2)}) collective-permute-start(f32[1,192,128]{2,1,0:T(8,128)S(1)} %pass.2), channel_id=1, source_target_pairs={{0,1},{1,0},{2,3},{3,2},{4,5},{5,4},{6,7},{7,6},{8,9},{9,8},{10,11... | collective-permute-start | bytes 294920 | tf_op jit(solution)/shard_map/ppermute | solution.py:360
  9.6 0.2 pick.2.refs_8_.refs_2_
  9.7 0.6 %collective-permute-done.3.refs_3_.refs_0_.refs_23_ = f32[192,128]{1,0:T(8,128)S(1)} collective-permute-done((f32[192,128]{1,0:T(8,128)S(1)}, f32[192,128]{1,0:T(8,128)S(1)}, u32[]{:S(2)}, u32[]{:S(2)}) %collective-permute-start.3) | collective-permute-done | bytes 98336 | tf_op jit(solution)/shard_map/ppermute | solution.py:360
  10.3 1.0 %collective-permute-done.4.refs_4_.refs_1_.refs_21_ = f32[192,128]{1,0:T(8,128)S(1)} collective-permute-done((f32[192,128]{1,0:T(8,128)S(1)}, f32[192,128]{1,0:T(8,128)S(1)}, u32[]{:S(2)}, u32[]{:S(2)}) %collective-permute-start.4) | collective-permute-done | bytes 98336 | tf_op jit(solution)/shard_map/ppermute | solution.py:360
  11.4 0.2 collective-permute-start.5
  11.5 0.0 collective-permute-done.refs_1_.refs_19_
  11.5 0.0 collective-permute-done.2
  11.5 0.4 %pick.3.refs_3_ = f32[64,128]{1,0:T(8,128)S(1)} custom-call(s32[1]{0:T(128)} %bitcast.me.refs_0_, f32[192,128]{1,0:T(8,128)S(1)} %collective-permute-done.refs_1_.refs_19_, f32[192,128]{1,0:T(8,128)S(1)} %bitcast.14, f32[192,128]{1,0:T(8,128)S(1)} %collective-permute-done.3.refs_3_.refs_0_.refs_23_, ...), custom_call_target="tpu_custom_call" | custom-call | flops 1600000000 | bytes 1 | tf_op jit(solution)/shard_map/pick/pallas_call | solution.py:449
  12.0 0.9 %collective-permute-done.5 = f32[2,192,128]{2,1,0:T(8,128)S(1)} collective-permute-done((f32[2,192,128]{2,1,0:T(8,128)S(1)}, f32[2,192,128]{2,1,0:T(8,128)S(1)}, u32[]{:S(2)}, u32[]{:S(2)}) %collective-permute-start.5) | collective-permute-done | bytes 196640 | tf_op jit(solution)/shard_map/ppermute | solution.py:360
  12.9 1.2 %project.1 = (f32[16,128]{1,0:T(8,128)S(1)}, f32[320,128]{1,0:T(8,128)S(1)}) custom-call(s32[1]{0:T(128)} %bitcast.me.refs_0_, f32[16,128,256]{2,1,0:T(8,128)S(1)} %get-tuple-element.41.refs_1_, bf16[16,256,256]{2,1,0:T(8,128)(2,1)S(1)} %get-tuple-element.42.refs_2_, f32[64,128]{1,0:T(8,128)S(1)} %pick.3.refs_3_, f32[16,128]{1,0:T(8,128)S(1)} %get-tuple-element.44.refs_4_, ...), custom_call_target="tpu_custom_call" | custom-call | tf_op jit(solution)/shard_map/project/pallas_call | solution.py:470
  14.1 8.5 %all_to_all.5 = f32[8,40,128]{2,1,0:T(8,128)S(1)} all-to-all(f32[8,40,128]{2,1,0:T(8,128)S(1)} %bitcast.13), channel_id=1, replica_groups=mesh['sky'=4,'tm'=8] {'tm'}, dimensions={0} | all-to-all | bytes 327680 | tf_op jit(solution)/shard_map/all_to_all | solution.py:503
  22.6 0.2 attitude.3.refs_0_
  22.8 2.6 %collective-permute-start.6 = (f32[40,128]{1,0:T(8,128)S(1)}, f32[40,128]{1,0:T(8,128)S(1)}, u32[]{:S(2)}, u32[]{:S(2)}) collective-permute-start(f32[40,128]{1,0:T(8,128)S(1)} %attitude.3.refs_0_), channel_id=1, source_target_pairs={{0,16},{8,24},{16,0},{24,8},{1,17},{9,25},{17,1},{25,9},{2,18},{10... | collective-permute-start | bytes 61448 | tf_op jit(solution)/shard_map/ppermute | solution.py:360
  25.3 1.4 %collective-permute-start.7 = (f32[40,128]{1,0:T(8,128)S(1)}, f32[40,128]{1,0:T(8,128)S(1)}, u32[]{:S(2)}, u32[]{:S(2)}) collective-permute-start(f32[40,128]{1,0:T(8,128)S(1)} %attitude.3.refs_0_), channel_id=1, source_target_pairs={{0,24},{8,16},{16,8},{24,0},{1,25},{9,17},{17,9},{25,1},{2,26},{10... | collective-permute-start | bytes 61448 | tf_op jit(solution)/shard_map/ppermute | solution.py:360
  26.7 0.2 collective-permute-start.8
  26.9 1.9 %source.3 = (f32[5,4096]{1,0:T(8,128)}, f32[16,128]{1,0:T(8,128)}, f32[8,128]{1,0:T(8,128)S(1)}) custom-call(s32[1]{0:T(128)} %bitcast.me.refs_0_, f32[320,128]{1,0:T(8,128)S(1)} %bitcast.12, f32[16,128]{1,0:T(8,128)S(1)} %get-tuple-element.56.held), custom_call_target="tpu_custom_call" | custom-call | flops 2000000000 | bytes 1 | tf_op jit(solution)/shard_map/source/pallas_call | solution.py:514
  28.8 0.0 collective-permute-done.6.refs_1_
  28.8 2.1 %collective-permute-done.7.refs_2_ = f32[40,128]{1,0:T(8,128)S(1)} collective-permute-done((f32[40,128]{1,0:T(8,128)S(1)}, f32[40,128]{1,0:T(8,128)S(1)}, u32[]{:S(2)}, u32[]{:S(2)}) %collective-permute-start.7) | collective-permute-done | bytes 20512 | tf_op jit(solution)/shard_map/ppermute | solution.py:360
  30.9 0.0 collective-permute-done.8.refs_3_
  30.9 0.6 %finish.1 = (f32[16,256]{1,0:T(8,128)}, f32[1,1]{1,0:T(1,128)}) custom-call(f32[40,128]{1,0:T(8,128)S(1)} %attitude.3.refs_0_, f32[40,128]{1,0:T(8,128)S(1)} %collective-permute-done.6.refs_1_, f32[40,128]{1,0:T(8,128)S(1)} %collective-permute-done.7.refs_2_, f32[40,128]{1,0:T(8,128)S(1)} %collective-permute-done.8.refs_3_, ...), custom_call_target="tpu_custom_call" | custom-call | tf_op jit(solution)/shard_map/finish/pallas_call | solution.py:533
  (3 shorter events, 0.0 us)
Async XLA Ops:
  1.6 7.3 %collective-permute-start.1 = (f32[192,128]{1,0:T(8,128)S(1)}, f32[192,128]{1,0:T(8,128)S(1)}, u32[]{:S(2)}, u32[]{:S(2)}) collective-permute-start(f32[192,128]{1,0:T(8,128)S(1)} %get-tuple-element.33.table.refs_18_), channel_id=1, source_target_pairs={{0,7},{1,6},{2,5},{3,4},{4,3},{5,2},{6,1},{7,0},{8,15},{9,14},{10,... | collective-permute-start | bytes 294920 | tf_op jit(solution)/shard_map/ppermute | solution.py:360
  5.0 5.3 %collective-permute-start.3 = (f32[192,128]{1,0:T(8,128)S(1)}, f32[192,128]{1,0:T(8,128)S(1)}, u32[]{:S(2)}, u32[]{:S(2)}) collective-permute-start(f32[192,128]{1,0:T(8,128)S(1)} %get-tuple-element.33.table.refs_18_), channel_id=1, source_target_pairs={{0,5},{1,4},{2,7},{3,6},{4,1},{5,0},{6,3},{7,2},{8,13},{9,12},{10,... | collective-permute-start | bytes 294920 | tf_op jit(solution)/shard_map/ppermute | solution.py:360
  5.8 5.5 %collective-permute-start.4 = (f32[192,128]{1,0:T(8,128)S(1)}, f32[192,128]{1,0:T(8,128)S(1)}, u32[]{:S(2)}, u32[]{:S(2)}) collective-permute-start(f32[192,128]{1,0:T(8,128)S(1)} %get-tuple-element.33.table.refs_18_), channel_id=1, source_target_pairs={{0,3},{1,2},{2,1},{3,0},{4,7},{5,6},{6,5},{7,4},{8,11},{9,10},{10,... | collective-permute-start | bytes 294920 | tf_op jit(solution)/shard_map/ppermute | solution.py:360
  6.0 5.6 %collective-permute-start = (f32[192,128]{1,0:T(8,128)S(1)}, f32[192,128]{1,0:T(8,128)S(1)}, u32[]{:S(2)}, u32[]{:S(2)}) collective-permute-start(f32[192,128]{1,0:T(8,128)S(1)} %get-tuple-element.33.table.refs_18_), channel_id=1, source_target_pairs={{0,1},{1,0},{2,3},{3,2},{4,5},{5,4},{6,7},{7,6},{8,9},{9,8},{10,11... | collective-permute-start | bytes 294920 | tf_op jit(solution)/shard_map/ppermute | solution.py:360
  9.0 2.5 %collective-permute-start.2 = (f32[1,192,128]{2,1,0:T(8,128)S(1)}, f32[1,192,128]{2,1,0:T(8,128)S(1)}, u32[]{:S(2)}, u32[]{:S(2)}) collective-permute-start(f32[1,192,128]{2,1,0:T(8,128)S(1)} %pass.2), channel_id=1, source_target_pairs={{0,1},{1,0},{2,3},{3,2},{4,5},{5,4},{6,7},{7,6},{8,9},{9,8},{10,11... | collective-permute-start | bytes 294920 | tf_op jit(solution)/shard_map/ppermute | solution.py:360
  11.4 1.5 %collective-permute-start.5 = (f32[2,192,128]{2,1,0:T(8,128)S(1)}, f32[2,192,128]{2,1,0:T(8,128)S(1)}, u32[]{:S(2)}, u32[]{:S(2)}) collective-permute-start(f32[2,192,128]{2,1,0:T(8,128)S(1)} %pass.3), channel_id=1, source_target_pairs={{0,1},{1,0},{2,3},{3,2},{4,5},{5,4},{6,7},{7,6},{8,9},{9,8},{10,11... | collective-permute-start | bytes 589832 | tf_op jit(solution)/shard_map/ppermute | solution.py:360
  22.8 6.0 %collective-permute-start.6 = (f32[40,128]{1,0:T(8,128)S(1)}, f32[40,128]{1,0:T(8,128)S(1)}, u32[]{:S(2)}, u32[]{:S(2)}) collective-permute-start(f32[40,128]{1,0:T(8,128)S(1)} %attitude.3.refs_0_), channel_id=1, source_target_pairs={{0,16},{8,24},{16,0},{24,8},{1,17},{9,25},{17,1},{25,9},{2,18},{10... | collective-permute-start | bytes 61448 | tf_op jit(solution)/shard_map/ppermute | solution.py:360
  25.3 5.6 %collective-permute-start.7 = (f32[40,128]{1,0:T(8,128)S(1)}, f32[40,128]{1,0:T(8,128)S(1)}, u32[]{:S(2)}, u32[]{:S(2)}) collective-permute-start(f32[40,128]{1,0:T(8,128)S(1)} %attitude.3.refs_0_), channel_id=1, source_target_pairs={{0,24},{8,16},{16,8},{24,0},{1,25},{9,17},{17,9},{25,1},{2,26},{10... | collective-permute-start | bytes 61448 | tf_op jit(solution)/shard_map/ppermute | solution.py:360
  26.7 4.2 %collective-permute-start.8 = (f32[40,128]{1,0:T(8,128)S(1)}, f32[40,128]{1,0:T(8,128)S(1)}, u32[]{:S(2)}, u32[]{:S(2)}) collective-permute-start(f32[40,128]{1,0:T(8,128)S(1)} %attitude.3.refs_0_), channel_id=1, source_target_pairs={{0,8},{8,0},{16,24},{24,16},{1,9},{9,1},{17,25},{25,17},{2,10},{10... | collective-permute-start | bytes 61448 | tf_op jit(solution)/shard_map/ppermute | solution.py:360

commit v10 on v9

--- a/solution.py
+++ b/solution.py
@@ -439,7 +439,7 @@
         out_shape=(picked_shape, jax.ShapeDtypeStruct(tiles.shape, F32), jax.ShapeDtypeStruct((tile_total, 2 * row_count, cols), BF16)),
         in_specs=[SMEM] + [VMEM] * 4 + [HBM],
         out_specs=(VMEM,) * 3,
-        scratch_shapes=[pltpu.SemaphoreType.DMA((4,))],
+        scratch_shapes=[pltpu.SemaphoreType.DMA((8,))],
         compiler_params=PARAMS,
         cost_estimate=cost(1.6),
         name="own",

time: 31.7 us -> 31.7 us (level)
  no operation moved by 1% of the time
where the time goes in v10:
time: 31.7 us; the launch traced here: 31.5 us
  starting transfers between devices  9.22 us (29%)
  blocking collectives  8.48 us (27%)
  Pallas kernels  8.47 us (27%)
  waiting for transfers between devices  4.65 us (15%)
  between operations  0.7 us (2%)
    ppermute x9, starting transfers between devices, swapped(): return lax.ppermute(x, axis, [(i, i ^ offset) for i in range(size)])  9.22 us
    all_to_all x1, blocking collectives, per_device(): lax.all_to_all(sent.reshape(tm, depth, LANES), 'tm', 0, 0)  8.48 us
    ppermute x9, waiting for transfers between devices, swapped(): return lax.ppermute(x, axis, [(i, i ^ offset) for i in range(size)])  4.65 us
    pallas_call x1, Pallas kernels, per_device(): pl.pallas_call(functools.partial(source_kernel, owners=tm, share=share),...  1.87 us
    pallas_call x1, Pallas kernels, per_device(): pl.pallas_call(functools.partial(own_kernel, share=share), out_shape=(pic...  1.63 us
    pallas_call x1, Pallas kernels, per_device(): pl.pallas_call(functools.partial(order_kernel, owners=tm, span=span, cap=...  1.34 us
    pallas_call x1, Pallas kernels, per_device(): pl.pallas_call(functools.partial(project_kernel, seg_rows=seg_rows, offse...  1.22 us
    pallas_call x1, Pallas kernels, per_device(): pl.pallas_call(pack_kernel, out_shape=(jax.ShapeDtypeStruct((params * (sp...  1 us
  transfers between devices with their start and end apart: 9, of which 4 were waited for; matrix products, arithmetic and copies ran while one was open for 0% of the time, Pallas kernels for 17%

profile of v10, /device:TPU:0, one launch (start us, length us, event | category | flops | bytes accessed | tf_op | source)
XLA Modules:
  0.0 31.5 jit_solution(17262081966811664689)
XLA Ops:
  0.6 1.0 %pack.1 = (f32[192,128]{1,0:T(8,128)S(1)}, s32[16,128]{1,0:T(8,128)S(1)}, f32[5,16,128]{2,1,0:T(8,128)S(1)}, f32[16,128]{1,0:T(8,128)S(1)}, s32[1,16]{1,0:T(1,128)S(1)}, /*index=5*/s32[1,16]{1,0:T(1,128)S(1)}) custom-call(f32[5,4096]{1,0:T(8,128)} %source.2, f32[16,256]{1,0:T(8,128)} %attitude.2, s32[16,128]{1,0:T(8,128)} %refs_0_.1, f32[5,16,128]{2,1,0:T(8,128)} %refs_1_.1, ...), custom_call_target="tpu_custom_call" | custom-call | tf_op jit(solution)/shard_map/pack/pallas_call | solution.py:371
  1.6 3.4 %collective-permute-start.1 = (f32[192,128]{1,0:T(8,128)S(1)}, f32[192,128]{1,0:T(8,128)S(1)}, u32[]{:S(2)}, u32[]{:S(2)}) collective-permute-start(f32[192,128]{1,0:T(8,128)S(1)} %get-tuple-element.33.table.refs_18_), channel_id=1, source_target_pairs={{0,7},{1,6},{2,5},{3,4},{4,3},{5,2},{6,1},{7,0},{8,15},{9,14},{10,... | collective-permute-start | bytes 294920 | tf_op jit(solution)/shard_map/ppermute | solution.py:360
  5.0 0.8 %collective-permute-start.3 = (f32[192,128]{1,0:T(8,128)S(1)}, f32[192,128]{1,0:T(8,128)S(1)}, u32[]{:S(2)}, u32[]{:S(2)}) collective-permute-start(f32[192,128]{1,0:T(8,128)S(1)} %get-tuple-element.33.table.refs_18_), channel_id=1, source_target_pairs={{0,5},{1,4},{2,7},{3,6},{4,1},{5,0},{6,3},{7,2},{8,13},{9,12},{10,... | collective-permute-start | bytes 294920 | tf_op jit(solution)/shard_map/ppermute | solution.py:360
  5.8 0.1 collective-permute-start.4
  6.0 0.0 collective-permute-start
  6.0 1.3 %order.1 = (s32[32,128]{1,0:T(8,128)S(1)}, s32[32,128]{1,0:T(8,128)S(1)}, f32[5,32,128]{2,1,0:T(8,128)S(1)}, f32[32,128]{1,0:T(8,128)S(1)}, s32[64,128]{1,0:T(8,...) custom-call(s32[1]{0:T(128)} %bitcast.me.refs_0_, ...), custom_call_target="tpu_custom_call" | custom-call | flops 1500000000 | bytes 1 | tf_op jit(solution)/shard_map/order/pallas_call | solution.py:409
  7.3 1.6 %own.1 = (f32[64,128]{1,0:T(8,128)S(1)}, f32[16,128,256]{2,1,0:T(8,128)S(1)}, bf16[16,256,256]{2,1,0:T(8,128)(2,1)S(1)}) custom-call(s32[1]{0:T(128)} %bitcast.me.refs_0_, f32[192,128]{1,0:T(8,128)S(1)} %get-tuple-element.33.table.refs_18_, s32[64,128]{1,0:T(8,128)S(1)} %get-tuple-element.38.block.refs_2_.refs_5_.refs_9_, ...), custom_call_target="tpu_custom_call" | custom-call | flops 1600000000 | bytes 1 | tf_op jit(solution)/shard_map/own/pallas_call | solution.py:437
  9.0 0.0 collective-permute-done.1.refs_0_.refs_1_.refs_25_
  9.0 0.6 %collective-permute-start.2 = (f32[1,192,128]{2,1,0:T(8,128)S(1)}, f32[1,192,128]{2,1,0:T(8,128)S(1)}, u32[]{:S(2)}, u32[]{:S(2)}) collective-permute-start(f32[1,192,128]{2,1,0:T(8,128)S(1)} %pass.2), channel_id=1, source_target_pairs={{0,1},{1,0},{2,3},{3,2},{4,5},{5,4},{6,7},{7,6},{8,9},{9,8},{10,11... | collective-permute-start | bytes 294920 | tf_op jit(solution)/shard_map/ppermute | solution.py:360
  9.6 0.2 pick.2.refs_8_.refs_2_
  9.7 0.6 %collective-permute-done.3.refs_3_.refs_0_.refs_23_ = f32[192,128]{1,0:T(8,128)S(1)} collective-permute-done((f32[192,128]{1,0:T(8,128)S(1)}, f32[192,128]{1,0:T(8,128)S(1)}, u32[]{:S(2)}, u32[]{:S(2)}) %collective-permute-start.3) | collective-permute-done | bytes 98336 | tf_op jit(solution)/shard_map/ppermute | solution.py:360
  10.3 1.0 %collective-permute-done.4.refs_4_.refs_1_.refs_21_ = f32[192,128]{1,0:T(8,128)S(1)} collective-permute-done((f32[192,128]{1,0:T(8,128)S(1)}, f32[192,128]{1,0:T(8,128)S(1)}, u32[]{:S(2)}, u32[]{:S(2)}) %collective-permute-start.4) | collective-permute-done | bytes 98336 | tf_op jit(solution)/shard_map/ppermute | solution.py:360
  11.4 0.2 collective-permute-start.5
  11.5 0.0 collective-permute-done.refs_1_.refs_19_
  11.5 0.0 collective-permute-done.2
  11.5 0.4 %pick.3.refs_3_ = f32[64,128]{1,0:T(8,128)S(1)} custom-call(s32[1]{0:T(128)} %bitcast.me.refs_0_, f32[192,128]{1,0:T(8,128)S(1)} %collective-permute-done.refs_1_.refs_19_, f32[192,128]{1,0:T(8,128)S(1)} %bitcast.14, f32[192,128]{1,0:T(8,128)S(1)} %collective-permute-done.3.refs_3_.refs_0_.refs_23_, ...), custom_call_target="tpu_custom_call" | custom-call | flops 1600000000 | bytes 1 | tf_op jit(solution)/shard_map/pick/pallas_call | solution.py:449
  12.0 0.9 %collective-permute-done.5 = f32[2,192,128]{2,1,0:T(8,128)S(1)} collective-permute-done((f32[2,192,128]{2,1,0:T(8,128)S(1)}, f32[2,192,128]{2,1,0:T(8,128)S(1)}, u32[]{:S(2)}, u32[]{:S(2)}) %collective-permute-start.5) | collective-permute-done | bytes 196640 | tf_op jit(solution)/shard_map/ppermute | solution.py:360
  12.9 1.2 %project.1 = (f32[16,128]{1,0:T(8,128)S(1)}, f32[320,128]{1,0:T(8,128)S(1)}) custom-call(s32[1]{0:T(128)} %bitcast.me.refs_0_, f32[16,128,256]{2,1,0:T(8,128)S(1)} %get-tuple-element.41.refs_1_, bf16[16,256,256]{2,1,0:T(8,128)(2,1)S(1)} %get-tuple-element.42.refs_2_, f32[64,128]{1,0:T(8,128)S(1)} %pick.3.refs_3_, f32[16,128]{1,0:T(8,128)S(1)} %get-tuple-element.44.refs_4_, ...), custom_call_target="tpu_custom_call" | custom-call | tf_op jit(solution)/shard_map/project/pallas_call | solution.py:470
  14.1 8.5 %all_to_all.5 = f32[8,40,128]{2,1,0:T(8,128)S(1)} all-to-all(f32[8,40,128]{2,1,0:T(8,128)S(1)} %bitcast.13), channel_id=1, replica_groups=mesh['sky'=4,'tm'=8] {'tm'}, dimensions={0} | all-to-all | bytes 327680 | tf_op jit(solution)/shard_map/all_to_all | solution.py:503
  22.6 0.2 attitude.3.refs_0_
  22.8 2.6 %collective-permute-start.6 = (f32[40,128]{1,0:T(8,128)S(1)}, f32[40,128]{1,0:T(8,128)S(1)}, u32[]{:S(2)}, u32[]{:S(2)}) collective-permute-start(f32[40,128]{1,0:T(8,128)S(1)} %attitude.3.refs_0_), channel_id=1, source_target_pairs={{0,16},{8,24},{16,0},{24,8},{1,17},{9,25},{17,1},{25,9},{2,18},{10... | collective-permute-start | bytes 61448 | tf_op jit(solution)/shard_map/ppermute | solution.py:360
  25.3 1.4 %collective-permute-start.7 = (f32[40,128]{1,0:T(8,128)S(1)}, f32[40,128]{1,0:T(8,128)S(1)}, u32[]{:S(2)}, u32[]{:S(2)}) collective-permute-start(f32[40,128]{1,0:T(8,128)S(1)} %attitude.3.refs_0_), channel_id=1, source_target_pairs={{0,24},{8,16},{16,8},{24,0},{1,25},{9,17},{17,9},{25,1},{2,26},{10... | collective-permute-start | bytes 61448 | tf_op jit(solution)/shard_map/ppermute | solution.py:360
  26.7 0.2 collective-permute-start.8
  26.9 1.9 %source.3 = (f32[5,4096]{1,0:T(8,128)}, f32[16,128]{1,0:T(8,128)}, f32[8,128]{1,0:T(8,128)S(1)}) custom-call(s32[1]{0:T(128)} %bitcast.me.refs_0_, f32[320,128]{1,0:T(8,128)S(1)} %bitcast.12, f32[16,128]{1,0:T(8,128)S(1)} %get-tuple-element.56.held), custom_call_target="tpu_custom_call" | custom-call | flops 2000000000 | bytes 1 | tf_op jit(solution)/shard_map/source/pallas_call | solution.py:514
  28.8 0.0 collective-permute-done.6.refs_1_
  28.8 2.1 %collective-permute-done.7.refs_2_ = f32[40,128]{1,0:T(8,128)S(1)} collective-permute-done((f32[40,128]{1,0:T(8,128)S(1)}, f32[40,128]{1,0:T(8,128)S(1)}, u32[]{:S(2)}, u32[]{:S(2)}) %collective-permute-start.7) | collective-permute-done | bytes 20512 | tf_op jit(solution)/shard_map/ppermute | solution.py:360
  30.9 0.0 collective-permute-done.8.refs_3_
  30.9 0.6 %finish.1 = (f32[16,256]{1,0:T(8,128)}, f32[1,1]{1,0:T(1,128)}) custom-call(f32[40,128]{1,0:T(8,128)S(1)} %attitude.3.refs_0_, f32[40,128]{1,0:T(8,128)S(1)} %collective-permute-done.6.refs_1_, f32[40,128]{1,0:T(8,128)S(1)} %collective-permute-done.7.refs_2_, f32[40,128]{1,0:T(8,128)S(1)} %collective-permute-done.8.refs_3_, ...), custom_call_target="tpu_custom_call" | custom-call | tf_op jit(solution)/shard_map/finish/pallas_call | solution.py:533
  (3 shorter events, 0.0 us)
Async XLA Ops:
  1.6 7.3 %collective-permute-start.1 = (f32[192,128]{1,0:T(8,128)S(1)}, f32[192,128]{1,0:T(8,128)S(1)}, u32[]{:S(2)}, u32[]{:S(2)}) collective-permute-start(f32[192,128]{1,0:T(8,128)S(1)} %get-tuple-element.33.table.refs_18_), channel_id=1, source_target_pairs={{0,7},{1,6},{2,5},{3,4},{4,3},{5,2},{6,1},{7,0},{8,15},{9,14},{10,... | collective-permute-start | bytes 294920 | tf_op jit(solution)/shard_map/ppermute | solution.py:360
  5.0 5.3 %collective-permute-start.3 = (f32[192,128]{1,0:T(8,128)S(1)}, f32[192,128]{1,0:T(8,128)S(1)}, u32[]{:S(2)}, u32[]{:S(2)}) collective-permute-start(f32[192,128]{1,0:T(8,128)S(1)} %get-tuple-element.33.table.refs_18_), channel_id=1, source_target_pairs={{0,5},{1,4},{2,7},{3,6},{4,1},{5,0},{6,3},{7,2},{8,13},{9,12},{10,... | collective-permute-start | bytes 294920 | tf_op jit(solution)/shard_map/ppermute | solution.py:360
  5.8 5.5 %collective-permute-start.4 = (f32[192,128]{1,0:T(8,128)S(1)}, f32[192,128]{1,0:T(8,128)S(1)}, u32[]{:S(2)}, u32[]{:S(2)}) collective-permute-start(f32[192,128]{1,0:T(8,128)S(1)} %get-tuple-element.33.table.refs_18_), channel_id=1, source_target_pairs={{0,3},{1,2},{2,1},{3,0},{4,7},{5,6},{6,5},{7,4},{8,11},{9,10},{10,... | collective-permute-start | bytes 294920 | tf_op jit(solution)/shard_map/ppermute | solution.py:360
  6.0 5.6 %collective-permute-start = (f32[192,128]{1,0:T(8,128)S(1)}, f32[192,128]{1,0:T(8,128)S(1)}, u32[]{:S(2)}, u32[]{:S(2)}) collective-permute-start(f32[192,128]{1,0:T(8,128)S(1)} %get-tuple-element.33.table.refs_18_), channel_id=1, source_target_pairs={{0,1},{1,0},{2,3},{3,2},{4,5},{5,4},{6,7},{7,6},{8,9},{9,8},{10,11... | collective-permute-start | bytes 294920 | tf_op jit(solution)/shard_map/ppermute | solution.py:360
  9.0 2.6 %collective-permute-start.2 = (f32[1,192,128]{2,1,0:T(8,128)S(1)}, f32[1,192,128]{2,1,0:T(8,128)S(1)}, u32[]{:S(2)}, u32[]{:S(2)}) collective-permute-start(f32[1,192,128]{2,1,0:T(8,128)S(1)} %pass.2), channel_id=1, source_target_pairs={{0,1},{1,0},{2,3},{3,2},{4,5},{5,4},{6,7},{7,6},{8,9},{9,8},{10,11... | collective-permute-start | bytes 294920 | tf_op jit(solution)/shard_map/ppermute | solution.py:360
  11.4 1.5 %collective-permute-start.5 = (f32[2,192,128]{2,1,0:T(8,128)S(1)}, f32[2,192,128]{2,1,0:T(8,128)S(1)}, u32[]{:S(2)}, u32[]{:S(2)}) collective-permute-start(f32[2,192,128]{2,1,0:T(8,128)S(1)} %pass.3), channel_id=1, source_target_pairs={{0,1},{1,0},{2,3},{3,2},{4,5},{5,4},{6,7},{7,6},{8,9},{9,8},{10,11... | collective-permute-start | bytes 589832 | tf_op jit(solution)/shard_map/ppermute | solution.py:360
  22.8 6.0 %collective-permute-start.6 = (f32[40,128]{1,0:T(8,128)S(1)}, f32[40,128]{1,0:T(8,128)S(1)}, u32[]{:S(2)}, u32[]{:S(2)}) collective-permute-start(f32[40,128]{1,0:T(8,128)S(1)} %attitude.3.refs_0_), channel_id=1, source_target_pairs={{0,16},{8,24},{16,0},{24,8},{1,17},{9,25},{17,1},{25,9},{2,18},{10... | collective-permute-start | bytes 61448 | tf_op jit(solution)/shard_map/ppermute | solution.py:360
  25.3 5.6 %collective-permute-start.7 = (f32[40,128]{1,0:T(8,128)S(1)}, f32[40,128]{1,0:T(8,128)S(1)}, u32[]{:S(2)}, u32[]{:S(2)}) collective-permute-start(f32[40,128]{1,0:T(8,128)S(1)} %attitude.3.refs_0_), channel_id=1, source_target_pairs={{0,24},{8,16},{16,8},{24,0},{1,25},{9,17},{17,9},{25,1},{2,26},{10... | collective-permute-start | bytes 61448 | tf_op jit(solution)/shard_map/ppermute | solution.py:360
  26.7 4.2 %collective-permute-start.8 = (f32[40,128]{1,0:T(8,128)S(1)}, f32[40,128]{1,0:T(8,128)S(1)}, u32[]{:S(2)}, u32[]{:S(2)}) collective-permute-start(f32[40,128]{1,0:T(8,128)S(1)} %attitude.3.refs_0_), channel_id=1, source_target_pairs={{0,8},{8,0},{16,24},{24,16},{1,9},{9,1},{17,25},{25,17},{2,10},{10... | collective-permute-start | bytes 61448 | tf_op jit(solution)/shard_map/ppermute | solution.py:360
